TPU v7x, 128 devices: a whole 4x4x4 slice. The times are simulated.
128 devices in a mesh: dp: 16 (over y_hi, z, core), mp: 8 (over y_lo, x).
Axes of the slice: x: 4, y: 4 (y_hi: 2, y_lo: 2; y = y_hi * 2 + y_lo), z: 4, core: 2. Of those that a mesh axis runs over, the one named last changes fastest.
Arguments:
- tokens: bfloat16 [17408, 2048], P(('dp', 'mp')), may hold values from -6 to 6
- lengths: int32 [16, 3], P('dp'), may hold values from 1 to 512, 832 in all within a row
- place: int32 [32], replicated, may hold values from 0 to 31, each once
- attn_gain: float32 [2048], replicated, may hold values from 0.5 to 1.5
- w_query: bfloat16 [2048, 2048], P(None, 'mp'), may hold values from -0.125 to 0.125
- w_key: bfloat16 [2048, 512], P(None, 'mp'), may hold values from -0.125 to 0.125
- w_value: bfloat16 [2048, 512], P(None, 'mp'), may hold values from -0.125 to 0.125
- w_out: bfloat16 [2048, 2048], P('mp'), may hold values from -1.5 to 1.5
- mlp_gain: float32 [2048], replicated, may hold values from 0.5 to 1.5
- w_gate: bfloat16 [2048, 8192], P(None, 'mp'), may hold values from -0.125 to 0.125
- w_up: bfloat16 [2048, 8192], P(None, 'mp'), may hold values from -0.125 to 0.125
- w_down: bfloat16 [8192, 2048], P('mp'), may hold values from -0.0625 to 0.0625
- out_grad: bfloat16 [17408, 2048], P(('dp', 'mp')), may hold values from -6 to 6
Outputs:
- output: bfloat16 [17408, 2048], P(('dp', 'mp'))
- tokens_grad: bfloat16 [17408, 2048], P(('dp', 'mp'))
- attn_gain_grad: float32 [2048], replicated
- w_query_grad: float32 [2048, 2048], P('dp', 'mp')
- w_key_grad: float32 [2048, 512], P('dp', 'mp')
- w_value_grad: float32 [2048, 512], P('dp', 'mp')
- w_out_grad: float32 [2048, 2048], P('mp', 'dp')
- mlp_gain_grad: float32 [2048], replicated
- w_gate_grad: float32 [2048, 8192], P('dp', 'mp')
- w_up_grad: float32 [2048, 8192], P('dp', 'mp')
- w_down_grad: float32 [8192, 2048], P('mp', 'dp')
Inputs may be any that keep to these rules, and one draw needn't show every extreme that they name: Row g holds, in order, the lengths of the short sequences packed in dp group g after its long-sequence rows; each row sums to 832 and its largest entry is 512. A permutation; dp group g holds half-blocks place[2 * g] and place[2 * g + 1] of the long sequence, in that order.
All inputs are finite; a program needn't handle non-finite values.
Results may differ from a plain program's by a relative error of at most 0.025.
Values may be sent and summed in bfloat16 or wider, within the bound.
No kernel may reach another device: no remote copies, remote signals or barrier semaphores. Data moves between devices by JAX's collectives and lax.ppermute only.
A program may use at most 256 MiB of HBM per device.

v0:
```python
import jax
import jax.numpy as jnp
from jax import lax
from jax.sharding import PartitionSpec as P

HEAD_DIM = 64
HALF = 128


EPS = 1e-05
THETA = 500000.0
MASKED = -1e30


def inverse_freq(head_width):
    indices = jnp.arange(head_width // 2, dtype=jnp.float32)
    base_freq = jnp.exp(-jnp.log(THETA) * 2.0 * indices / head_width)
    wavelength = 2.0 * jnp.pi / base_freq
    smooth = (8192.0 / wavelength - 1.0) / 3.0
    blended = (1.0 - smooth) * base_freq / 32.0 + smooth * base_freq
    return jnp.where(
        wavelength < 2048.0, base_freq, jnp.where(wavelength > 8192.0, base_freq / 32.0, blended)
    )


def tables(positions, head_width):
    angles = positions.astype(jnp.float32)[:, None] * inverse_freq(head_width)[None, :]
    return (jnp.cos(angles)[:, None, :], jnp.sin(angles)[:, None, :])


def rotate(values, cos_table, sin_table):
    half_dim = values.shape[-1] // 2
    first_half = values[..., :half_dim]
    second_half = values[..., half_dim:]
    return jnp.concatenate(
        [
            first_half * cos_table - second_half * sin_table,
            second_half * cos_table + first_half * sin_table,
        ],
        axis=-1,
    )


def pack_layout(seq_lengths, pack_rows):
    pack_index = jnp.arange(pack_rows, dtype=jnp.int32)
    seq_ends = jnp.cumsum(seq_lengths)
    seq_starts = seq_ends - seq_lengths
    member = (pack_index[:, None] >= seq_starts[None, :]) & (
        pack_index[:, None] < seq_ends[None, :]
    )
    seq_ids = jnp.arange(seq_lengths.shape[0], dtype=jnp.int32)
    segment = jnp.sum(jnp.where(member, seq_ids[None, :], 0), axis=1)
    offset = jnp.sum(jnp.where(member, seq_starts[None, :], 0), axis=1)
    return (pack_index - offset, segment)


def contract(left, right, left_dim, right_dim):
    return lax.dot_general(
        left, right, (((left_dim,), (right_dim,)), ((), ())), preferred_element_type=jnp.float32
    )


def attend_forward(queries, key_rows, value_rows, visible):
    score_scale = queries.shape[-1] ** (-0.5)
    scores = (
        jnp.einsum("rkgd,ckd->kgrc", queries, key_rows, preferred_element_type=jnp.float32)
        * score_scale
    )
    scores = jnp.where(visible[None, None], scores, MASKED)
    row_max = jnp.max(scores, axis=-1, keepdims=True)
    exp_scores = jnp.exp(scores - row_max)
    attn_probs = exp_scores / jnp.sum(exp_scores, axis=-1, keepdims=True)
    probs_low = attn_probs.astype(jnp.bfloat16)
    attn_rows = jnp.einsum(
        "kgrc,ckd->rkgd", probs_low, value_rows, preferred_element_type=jnp.float32
    )
    return (attn_rows, attn_probs, probs_low)


def attend_backward(queries, key_rows, value_rows, attn_probs, probs_low, grad_rows):
    score_scale = queries.shape[-1] ** (-0.5)
    grad_probs = jnp.einsum(
        "rkgd,ckd->kgrc", grad_rows, value_rows, preferred_element_type=jnp.float32
    )
    grad_values = jnp.einsum(
        "kgrc,rkgd->ckd", probs_low, grad_rows, preferred_element_type=jnp.float32
    )
    grad_scores = attn_probs * (
        grad_probs - jnp.sum(attn_probs * grad_probs, axis=-1, keepdims=True)
    )
    scores_low = grad_scores.astype(jnp.bfloat16)
    grad_queries = (
        jnp.einsum("kgrc,ckd->rkgd", scores_low, key_rows, preferred_element_type=jnp.float32)
        * score_scale
    )
    grad_keys = (
        jnp.einsum("kgrc,rkgd->ckd", scores_low, queries, preferred_element_type=jnp.float32)
        * score_scale
    )
    return (grad_queries, grad_keys, grad_values)


def norm_back(grad_in, unit_rows, inv_rms, gain):
    scaled = grad_in * gain
    return inv_rms * (scaled - unit_rows * jnp.mean(scaled * unit_rows, axis=-1, keepdims=True))


def local(
    tokens,
    lengths,
    place,
    attn_gain,
    w_query,
    w_key,
    w_value,
    w_out,
    mlp_gain,
    w_gate,
    w_up,
    w_down,
    out_grad,
):
    head_width = HEAD_DIM
    kv_local = w_key.shape[1] // head_width
    query_heads = w_query.shape[1] // head_width
    kv_group = query_heads // kv_local
    kv_width = kv_local * head_width
    attn_width = query_heads * head_width
    local_rows = tokens.shape[0]
    group_rows = local_rows * lax.axis_size("mp")
    long_rows = 2 * HALF
    pack_rows = group_rows - long_rows
    dp_index = lax.axis_index("dp")
    long_local = jnp.arange(long_rows, dtype=jnp.int32)
    place_pair = lax.dynamic_slice_in_dim(place, 2 * dp_index, 2)
    long_pos = jnp.where(long_local < HALF, place_pair[0], place_pair[1]) * HALF + long_local % HALF
    short_pos, segment = pack_layout(lengths[0], pack_rows)
    positions = jnp.concatenate([long_pos, short_pos])
    cos_table, sin_table = tables(positions, head_width)
    far_pos = (place[:, None] * HALF + jnp.arange(HALF, dtype=jnp.int32)[None, :]).reshape(-1)
    long_visible = long_pos[:, None] >= far_pos[None, :]
    pack_index = jnp.arange(pack_rows, dtype=jnp.int32)
    short_visible = (segment[:, None] == segment[None, :]) & (
        pack_index[:, None] >= pack_index[None, :]
    )
    residual = tokens.astype(jnp.float32)
    inv_one = lax.rsqrt(jnp.mean(residual * residual, axis=-1, keepdims=True) + EPS)
    unit_one = residual * inv_one
    local_one = (unit_one * attn_gain).astype(jnp.bfloat16)
    hidden_in = lax.all_gather(local_one, "mp", axis=0, tiled=True)
    query_raw = jnp.dot(hidden_in, w_query, preferred_element_type=jnp.float32).reshape(
        group_rows, query_heads, head_width
    )
    key_raw = jnp.dot(hidden_in, w_key, preferred_element_type=jnp.float32).reshape(
        group_rows, kv_local, head_width
    )
    value_all = jnp.dot(hidden_in, w_value, preferred_element_type=jnp.float32).astype(jnp.bfloat16)
    query_all = (
        rotate(query_raw, cos_table, sin_table)
        .astype(jnp.bfloat16)
        .reshape(group_rows, kv_local, kv_group, head_width)
    )
    key_all = (
        rotate(key_raw, cos_table, sin_table).astype(jnp.bfloat16).reshape(group_rows, kv_width)
    )
    far_rows = lax.all_gather(
        jnp.concatenate([key_all[:long_rows], value_all[:long_rows]], axis=1),
        "dp",
        axis=0,
        tiled=True,
    )
    far_keys = far_rows[:, :kv_width].reshape(-1, kv_local, head_width)
    far_values = far_rows[:, kv_width:].reshape(-1, kv_local, head_width)
    key_local = key_all.reshape(group_rows, kv_local, head_width)
    value_local = value_all.reshape(group_rows, kv_local, head_width)
    long_attn, long_probs, long_low = attend_forward(
        query_all[:long_rows], far_keys, far_values, long_visible
    )
    short_attn, short_probs, short_low = attend_forward(
        query_all[long_rows:], key_local[long_rows:], value_local[long_rows:], short_visible
    )
    attn_cast = (
        jnp.concatenate([long_attn, short_attn])
        .reshape(group_rows, attn_width)
        .astype(jnp.bfloat16)
    )
    mixed = residual + lax.psum_scatter(
        jnp.dot(attn_cast, w_out, preferred_element_type=jnp.float32).astype(jnp.bfloat16),
        "mp",
        scatter_dimension=0,
        tiled=True,
    ).astype(jnp.float32)
    inv_two = lax.rsqrt(jnp.mean(mixed * mixed, axis=-1, keepdims=True) + EPS)
    unit_two = mixed * inv_two
    local_two = (unit_two * mlp_gain).astype(jnp.bfloat16)
    hidden_two = lax.all_gather(local_two, "mp", axis=0, tiled=True)
    gate_proj = jnp.dot(hidden_two, w_gate, preferred_element_type=jnp.float32)
    up_proj = jnp.dot(hidden_two, w_up, preferred_element_type=jnp.float32)
    gate_sig = jax.nn.sigmoid(gate_proj)
    gate_act = gate_proj * gate_sig
    act_low = (gate_act * up_proj).astype(jnp.bfloat16)
    output = mixed + lax.psum_scatter(
        jnp.dot(act_low, w_down, preferred_element_type=jnp.float32).astype(jnp.bfloat16),
        "mp",
        scatter_dimension=0,
        tiled=True,
    ).astype(jnp.float32)
    grad_rows = lax.all_gather(out_grad, "mp", axis=0, tiled=True)
    grad_act = contract(grad_rows, w_down, 1, 1)
    down_grad = contract(act_low, grad_rows, 0, 0)
    grad_gate = (grad_act * up_proj * gate_sig * (1.0 + gate_proj * (1.0 - gate_sig))).astype(
        jnp.bfloat16
    )
    grad_up = (grad_act * gate_act).astype(jnp.bfloat16)
    gate_grad = contract(hidden_two, grad_gate, 0, 0)
    up_grad = contract(hidden_two, grad_up, 0, 0)
    grad_two = lax.psum_scatter(
        (contract(grad_gate, w_gate, 1, 1) + contract(grad_up, w_up, 1, 1)).astype(jnp.bfloat16),
        "mp",
        scatter_dimension=0,
        tiled=True,
    ).astype(jnp.float32)
    grad_mixed = out_grad.astype(jnp.float32) + norm_back(grad_two, unit_two, inv_two, mlp_gain)
    attn_grad_rows = lax.all_gather(grad_mixed.astype(jnp.bfloat16), "mp", axis=0, tiled=True)
    mlp_gain_part = jnp.sum(grad_two * unit_two, axis=0)
    out_weight_grad = contract(attn_cast, attn_grad_rows, 0, 0)
    grad_attn = (
        contract(attn_grad_rows, w_out, 1, 1)
        .astype(jnp.bfloat16)
        .reshape(group_rows, kv_local, kv_group, head_width)
    )
    long_dq, long_dk, long_dv = attend_backward(
        query_all[:long_rows], far_keys, far_values, long_probs, long_low, grad_attn[:long_rows]
    )
    short_dq, short_dk, short_dv = attend_backward(
        query_all[long_rows:],
        key_local[long_rows:],
        value_local[long_rows:],
        short_probs,
        short_low,
        grad_attn[long_rows:],
    )
    far_terms = jnp.concatenate(
        [long_dk.reshape(-1, kv_width), long_dv.reshape(-1, kv_width)], axis=1
    )
    far_grads = lax.psum_scatter(
        far_terms.astype(jnp.bfloat16), "dp", scatter_dimension=0, tiled=True
    ).astype(jnp.float32)
    key_grad_all = jnp.concatenate(
        [far_grads[:, :kv_width], short_dk.reshape(pack_rows, kv_width)]
    ).reshape(group_rows, kv_local, head_width)
    value_low = jnp.concatenate(
        [far_grads[:, kv_width:], short_dv.reshape(pack_rows, kv_width)]
    ).astype(jnp.bfloat16)
    query_grad_all = jnp.concatenate([long_dq, short_dq]).reshape(
        group_rows, query_heads, head_width
    )
    query_low = (
        rotate(query_grad_all, cos_table, -sin_table)
        .reshape(group_rows, attn_width)
        .astype(jnp.bfloat16)
    )
    key_low = (
        rotate(key_grad_all, cos_table, -sin_table)
        .reshape(group_rows, kv_width)
        .astype(jnp.bfloat16)
    )
    query_grad = contract(hidden_in, query_low, 0, 0)
    key_grad = contract(hidden_in, key_low, 0, 0)
    value_grad = contract(hidden_in, value_low, 0, 0)
    grad_one = lax.psum_scatter(
        (
            contract(query_low, w_query, 1, 1)
            + contract(key_low, w_key, 1, 1)
            + contract(value_low, w_value, 1, 1)
        ).astype(jnp.bfloat16),
        "mp",
        scatter_dimension=0,
        tiled=True,
    ).astype(jnp.float32)
    attn_gain_part = jnp.sum(grad_one * unit_one, axis=0)
    grad_tokens = grad_mixed + norm_back(grad_one, unit_one, inv_one, attn_gain)
    gain_one, gain_two = lax.psum((attn_gain_part, mlp_gain_part), ("dp", "mp"))
    query_sum, key_sum, value_sum, out_sum, gate_sum, up_sum, down_sum = (
        lax.psum_scatter(
            query_grad.astype(jnp.bfloat16), "dp", scatter_dimension=0, tiled=True
        ).astype(jnp.float32),
        lax.psum_scatter(
            key_grad.astype(jnp.bfloat16), "dp", scatter_dimension=0, tiled=True
        ).astype(jnp.float32),
        lax.psum_scatter(
            value_grad.astype(jnp.bfloat16), "dp", scatter_dimension=0, tiled=True
        ).astype(jnp.float32),
        lax.psum_scatter(
            out_weight_grad.astype(jnp.bfloat16), "dp", scatter_dimension=1, tiled=True
        ).astype(jnp.float32),
        lax.psum_scatter(
            gate_grad.astype(jnp.bfloat16), "dp", scatter_dimension=0, tiled=True
        ).astype(jnp.float32),
        lax.psum_scatter(
            up_grad.astype(jnp.bfloat16), "dp", scatter_dimension=0, tiled=True
        ).astype(jnp.float32),
        lax.psum_scatter(
            down_grad.astype(jnp.bfloat16), "dp", scatter_dimension=1, tiled=True
        ).astype(jnp.float32),
    )
    return (
        output.astype(jnp.bfloat16),
        grad_tokens.astype(jnp.bfloat16),
        gain_one,
        query_sum,
        key_sum,
        value_sum,
        out_sum,
        gain_two,
        gate_sum,
        up_sum,
        down_sum,
    )


def solution(mesh):
    placed = (
        P(("dp", "mp"), None),
        P("dp", None),
        P(),
        P(),
        P(None, "mp"),
        P(None, "mp"),
        P(None, "mp"),
        P("mp", None),
        P(),
        P(None, "mp"),
        P(None, "mp"),
        P("mp", None),
        P(("dp", "mp"), None),
    )
    return jax.shard_map(
        local,
        mesh=mesh,
        in_specs=placed,
        out_specs=(
            P(("dp", "mp"), None),
            P(("dp", "mp"), None),
            P(),
            P("dp", "mp"),
            P("dp", "mp"),
            P("dp", "mp"),
            P("mp", "dp"),
            P(),
            P("dp", "mp"),
            P("dp", "mp"),
            P("mp", "dp"),
        ),
        check_vma=False,
    )
```

profile of v0, /device:TPU:1, one launch (start us, length us, event | category | flops | bytes accessed | tf_op | source)
XLA Modules:
  0.0 1239.8 jit_solution(13932328559073468236)
XLA Ops:
  19.9 49.7 %all-gather.6.cloned.1.call-done = bf16[1088,2048]{1,0:T(8,128)(2,1)} async-done(((bf16[136,2048]{1,0:T(8,128)(2,1)}), bf16[1088,2048]{1,0:T(8,128)(2,1)}) %all-gather.6.cloned.1.call-update) | async-done | bytes 4456464 | tf_op jit(solution)/shard_map/all_gather | solution.py:150
  93.6 26.0 %all-gather.8.cloned.1.call-done = bf16[4096,128]{0,1:T(8,128)(2,1)} async-done(((bf16[256,128]{0,1:T(8,128)(2,1)}), bf16[4096,128]{0,1:T(8,128)(2,1)}) %all-gather.8.cloned.1.call-update) | async-done | bytes 1048592 | tf_op jit(solution)/shard_map/all_gather | solution.py:166
  138.6 55.2 %reduce-scatter.21.cloned.1.call-done = bf16[136,2048]{1,0:T(8,128)(2,1)} async-done(((bf16[1088,2048]{1,0:T(8,128)(2,1)}), bf16[136,2048]{1,0:T(8,128)(2,1)}) %reduce-scatter.21.cloned.1.call-update) | async-done | bytes 557072 | tf_op jit(solution)/shard_map/reduce_scatter | solution.py:187
  197.9 53.3 %all-gather.10.cloned.1.call-done = bf16[1088,2048]{1,0:T(8,128)(2,1)} async-done(((bf16[136,2048]{1,0:T(8,128)(2,1)}), bf16[1088,2048]{1,0:T(8,128)(2,1)}) %all-gather.10.cloned.1.call-update) | async-done | bytes 4456464 | tf_op jit(solution)/shard_map/all_gather | solution.py:196
  251.2 10.6 fusion.129
  268.4 38.2 %all-gather.12.cloned.1.call-done = bf16[1088,2048]{1,0:T(8,128)(2,1)} async-done(((bf16[136,2048]{1,0:T(8,128)(2,1)}), bf16[1088,2048]{1,0:T(8,128)(2,1)}) %all-gather.12.cloned.1.call-update) | async-done | bytes 4456464 | tf_op jit(solution)/shard_map/all_gather | solution.py:208
  306.5 14.1 %multiply_convert_fusion = (bf16[1088,1024]{1,0:T(8,128)(2,1)S(1)}, bf16[1088,1024]{1,0:T(8,128)(2,1)S(1)}, bf16[1088,1024]{1,0:T(8,128)(2,1)}) fusion(f32[1088,1024]{1,0:T(8,128)} %fusion.128, f32[1088,1024]{1,0:T(8,128)} %fusion.129, bf16[1088,2048]{1,0:T(8,128)(2,1)} %all-gather.12.cloned.1.call-done, bf16[1024,2048]{1,0:T(8,128)(2,1)} %param.24), kind=kOutput, calls=%fused_computation.45 | convolution fusion | flops 4580114432 | bytes 24248320 | tf_op jit(solution)/shard_map/dot_general | solution.py:58
  337.1 54.1 %reduce-scatter.25.cloned.1.call-done = bf16[136,2048]{1,0:T(8,128)(2,1)} async-done(((bf16[1088,2048]{1,0:T(8,128)(2,1)}), bf16[136,2048]{1,0:T(8,128)(2,1)}) %reduce-scatter.25.cloned.1.call-update) | async-done | bytes 557072 | tf_op jit(solution)/shard_map/reduce_scatter | solution.py:217
  396.0 53.9 %all-gather.14.cloned.1.call-done = bf16[1088,2048]{1,0:T(8,128)(2,1)} async-done(((bf16[136,2048]{1,0:T(8,128)(2,1)}), bf16[1088,2048]{1,0:T(8,128)(2,1)}) %all-gather.14.cloned.1.call-update) | async-done | bytes 4456464 | tf_op jit(solution)/shard_map/all_gather | solution.py:224
  462.9 12.9 %fusion = (f32[4,256]{1,0:T(4,128)S(1)}, f32[4096,256,4]{1,0,2:T(8,128)}) fusion(f32[4,256]{1,0:T(4,128)S(1)} %fusion.4, f32[4,256]{1,0:T(4,128)S(1)} %get-tuple-element.41, f32[4096,256,4]{1,0,2:T(8,128)} %copy-done.4, pred[256,4096]{0,1:T(8,128)(4,1)S(1)} %broadcast_compare_fusion, bf16[256,4,64]{0,2,1:T(8,128)(2,1)S(1)} %bitcast.293, ...), kind=kOutput, calls=%fused_computation.3 | convolution fusion | flops 562035712 | bytes 35270656 | tf_op jit(solution)/shard_map/rkgd,ckd->kgrc/dot_general | solution.py:82
  475.9 8.9 fusion.12
  489.3 9.6 convolution_convert_fusion.2
  505.5 9.8 convolution_convert_fusion.3
  515.3 9.5 convolution_convert_fusion.4
  531.5 11.0 fusion.6
  611.9 26.0 %reduce-scatter.43.cloned.1.call-done = bf16[128,1024]{1,0:T(8,128)(2,1)} async-done(((bf16[2048,1024]{1,0:T(8,128)(2,1)}), bf16[128,1024]{1,0:T(8,128)(2,1)}) %reduce-scatter.43.cloned.1.call-update) | async-done | bytes 262160
  640.0 81.2 %reduce-scatter.35.cloned.1.call-done = bf16[128,1024]{1,0:T(8,128)(2,1)} async-done(((bf16[2048,1024]{1,0:T(8,128)(2,1)}), bf16[128,1024]{1,0:T(8,128)(2,1)}) %reduce-scatter.35.cloned.1.call-update) | async-done | bytes 262160 | tf_op jit(solution)/shard_map/reduce_scatter | solution.py:300
  723.0 82.3 %reduce-scatter.33.cloned.1.call-done = bf16[128,1024]{1,0:T(8,128)(2,1)} async-done(((bf16[2048,1024]{1,0:T(8,128)(2,1)}), bf16[128,1024]{1,0:T(8,128)(2,1)}) %reduce-scatter.33.cloned.1.call-update) | async-done | bytes 262160 | tf_op jit(solution)/shard_map/reduce_scatter | solution.py:297
  807.1 67.2 %reduce-scatter.41.cloned.1.call-done = bf16[128,256]{1,0:T(8,128)(2,1)} async-done(((bf16[2048,256]{1,0:T(8,128)(2,1)}), bf16[128,256]{1,0:T(8,128)(2,1)}) %reduce-scatter.41.cloned.1.call-update) | async-done | bytes 65552
  875.9 68.6 %reduce-scatter.31.cloned.1.call-done = bf16[128,256]{1,0:T(8,128)(2,1)} async-done(((bf16[2048,256]{1,0:T(8,128)(2,1)}), bf16[128,256]{1,0:T(8,128)(2,1)}) %reduce-scatter.31.cloned.1.call-update) | async-done | bytes 65552 | tf_op jit(solution)/shard_map/reduce_scatter | solution.py:285
  946.0 67.2 %reduce-scatter.37.cloned.1.call-done = bf16[128,64]{1,0:T(8,128)(2,1)} async-done(((bf16[2048,64]{1,0:T(8,128)(2,1)}), bf16[128,64]{1,0:T(8,128)(2,1)}) %reduce-scatter.37.cloned.1.call-update) | async-done | bytes 16400
  1014.7 67.7 %reduce-scatter.39.cloned.1.call-done = bf16[128,64]{1,0:T(8,128)(2,1)} async-done(((bf16[2048,64]{1,0:T(8,128)(2,1)}), bf16[128,64]{1,0:T(8,128)(2,1)}) %reduce-scatter.39.cloned.1.call-update) | async-done | bytes 16400
  1083.9 57.2 %reduce-scatter.29.cloned.1.call-done = bf16[136,2048]{1,0:T(8,128)(2,1)} async-done(((bf16[1088,2048]{1,0:T(8,128)(2,1)}), bf16[136,2048]{1,0:T(8,128)(2,1)}) %reduce-scatter.29.cloned.1.call-update) | async-done | bytes 557072 | tf_op jit(solution)/shard_map/reduce_scatter | solution.py:271
  1142.6 87.0 %all-reduce = (f32[2048]{0:T(1024)}, f32[2048]{0:T(1024)}) all-reduce(f32[2048]{0:T(1024)S(1)} %get-tuple-element.13, f32[2048]{0:T(1024)} %get-tuple-element.11), channel_id=1, replica_groups=mesh['dp'=16,'mp'=8] {'dp','mp'}, use_global_device_ids=true, to_apply=%region_19.20 | all-reduce | flops 4096 | bytes 32768 | tf_op jit(solution)/shard_map/psum | solution.py:283
  (267 shorter events, 203.4 us)
Async XLA Ops:
  7.2 62.4 %all-gather.6.cloned.1.call-start = ((), (), s32[]{:S(2)}) async-start(), calls=%async_computation.12 | async-start | bytes 5013504 | tf_op jit(solution)/shard_map/all_gather | solution.py:150
  11.2 108.4 %all-gather.8.cloned.1.call-start = ((), (), s32[]{:S(2)}) async-start(), calls=%async_computation.13 | async-start | bytes 1114112 | tf_op jit(solution)/shard_map/all_gather | solution.py:166
  77.3 116.5 %reduce-scatter.21.cloned.1.call-start = ((), (), s32[]{:S(2)}) async-start(), calls=%async_computation.14 | async-start | bytes 5013504 | tf_op jit(solution)/shard_map/reduce_scatter | solution.py:187
  138.6 112.6 %all-gather.10.cloned.1.call-start = ((), (), s32[]{:S(2)}) async-start(), calls=%async_computation.15 | async-start | bytes 5013504 | tf_op jit(solution)/shard_map/all_gather | solution.py:196
  197.2 109.3 %all-gather.12.cloned.1.call-start = ((), (), s32[]{:S(2)}) async-start(), calls=%async_computation.17 | async-start | bytes 5013504 | tf_op jit(solution)/shard_map/all_gather | solution.py:208
  197.8 193.4 %reduce-scatter.25.cloned.1.call-start = ((), (), s32[]{:S(2)}) async-start(), calls=%async_computation.18 | async-start | bytes 5013504 | tf_op jit(solution)/shard_map/reduce_scatter | solution.py:217
  336.7 113.2 %all-gather.14.cloned.1.call-start = ((), (), s32[]{:S(2)}) async-start(), calls=%async_computation.19 | async-start | bytes 5013504 | tf_op jit(solution)/shard_map/all_gather | solution.py:224
  395.9 179.9 %reduce-scatter.27.cloned.1.call-start = ((), (), s32[]{:S(2)}) async-start(), calls=%async_computation.20 | async-start | bytes 1114112 | tf_op jit(solution)/shard_map/reduce_scatter | solution.py:246
  489.1 148.9 %reduce-scatter.43.cloned.1.call-start = ((), (), s32[]{:S(2)}) async-start(), calls=%async_computation.28 | async-start | bytes 4456448
  505.4 215.8 %reduce-scatter.35.cloned.1.call-start = ((), (), s32[]{:S(2)}) async-start(), calls=%async_computation.24 | async-start | bytes 4456448 | tf_op jit(solution)/shard_map/reduce_scatter | solution.py:300
  515.3 290.0 %reduce-scatter.33.cloned.1.call-start = ((), (), s32[]{:S(2)}) async-start(), calls=%async_computation.23 | async-start | bytes 4456448 | tf_op jit(solution)/shard_map/reduce_scatter | solution.py:297
  524.8 349.4 %reduce-scatter.41.cloned.1.call-start = ((), (), s32[]{:S(2)}) async-start(), calls=%async_computation.27 | async-start | bytes 1114112
  563.8 380.7 %reduce-scatter.31.cloned.1.call-start = ((), (), s32[]{:S(2)}) async-start(), calls=%async_computation.22 | async-start | bytes 1114112 | tf_op jit(solution)/shard_map/reduce_scatter | solution.py:285
  575.8 437.4 %reduce-scatter.37.cloned.1.call-start = ((), (), s32[]{:S(2)}) async-start(), calls=%async_computation.25 | async-start | bytes 557056
  586.1 496.3 %reduce-scatter.39.cloned.1.call-start = ((), (), s32[]{:S(2)}) async-start(), calls=%async_computation.26 | async-start | bytes 557056
  594.6 546.4 %reduce-scatter.29.cloned.1.call-start = ((), (), s32[]{:S(2)}) async-start(), calls=%async_computation.21 | async-start | bytes 5013504 | tf_op jit(solution)/shard_map/reduce_scatter | solution.py:271
  601.7 627.9 %reduce-scatter.23.cloned.1.call-start = ((), (), s32[]{:S(2)}) async-start(), calls=%async_computation.16 | async-start | bytes 5013504 | tf_op jit(solution)/shard_map/reduce_scatter | solution.py:202
  611.9 529.2 %copy-start.7 = (bf16[136,2048]{1,0:T(8,128)(2,1)S(1)}, bf16[136,2048]{1,0:T(8,128)(2,1)}, u32[]{:S(2)}) copy-start(bf16[136,2048]{1,0:T(8,128)(2,1)} %param.13) | copy-start | bytes 1671172
  611.9 529.2 %copy-start.45 = (f32[2048]{0:T(1024)S(1)}, f32[2048]{0:T(1024)}, u32[]{:S(2)}) copy-start(f32[2048]{0:T(1024)} %param.16) | copy-start | bytes 24580
  611.9 617.7 %copy-start.9 = (bf16[136,2048]{1,0:T(8,128)(2,1)S(1)}, bf16[136,2048]{1,0:T(8,128)(2,1)}, u32[]{:S(2)}) copy-start(bf16[136,2048]{1,0:T(8,128)(2,1)} %reduce-scatter.21.cloned.1.call-done) | copy-start | bytes 1671172
  611.9 617.7 %copy-start.12 = (bf16[136,2048]{1,0:T(8,128)(2,1)S(1)}, bf16[136,2048]{1,0:T(8,128)(2,1)}, u32[]{:S(2)}) copy-start(bf16[136,2048]{1,0:T(8,128)(2,1)} %reduce-scatter.25.cloned.1.call-done) | copy-start | bytes 1671172
  611.9 617.7 %copy-start.13 = (bf16[136,2048]{1,0:T(8,128)(2,1)S(1)}, bf16[136,2048]{1,0:T(8,128)(2,1)}, u32[]{:S(2)}) copy-start(bf16[136,2048]{1,0:T(8,128)(2,1)} %param.25) | copy-start | bytes 1671172
  611.9 617.7 %copy-start.42 = (f32[2048]{0:T(1024)S(1)}, f32[2048]{0:T(1024)}, u32[]{:S(2)}) copy-start(f32[2048]{0:T(1024)} %param.21) | copy-start | bytes 24580
  638.0 594.8 %copy-start.1 = (bf16[256,2048]{1,0:T(8,128)(2,1)S(1)}, bf16[256,2048]{1,0:T(8,128)(2,1)}, u32[]{:S(2)}) copy-start(bf16[256,2048]{1,0:T(8,128)(2,1)} %param.20) | copy-start | bytes 3145732
  (64 other events, 1248.3 us)
Sparse Core Ops, SparseCore 0:
  11.3 58.2 all-gather.5
  77.4 42.1 all-gather.7
  138.7 55.0 reduce-scatter.20
  197.4 53.7 all-gather.9
  252.7 53.7 all-gather.11
  336.8 54.3 reduce-scatter.24
  396.1 53.7 all-gather.13
  489.2 63.9 reduce-scatter.26
  557.8 80.1 reduce-scatter.42
  641.8 79.3 reduce-scatter.34
  725.8 79.4 reduce-scatter.32
  808.9 65.2 reduce-scatter.40
  878.5 65.9 reduce-scatter.30
  948.6 64.5 reduce-scatter.36
  1017.8 64.5 reduce-scatter.38
  1084.7 56.3 reduce-scatter.28
  1143.3 55.2 reduce-scatter.22
where the time goes:
time: 1240 us
  waiting for transfers between devices  848 us (68%)
  matrix products  204 us (16%)
  blocking collectives  87 us (7%)
  other arithmetic  57.8 us (5%)
  local copies, waits for them, and re-layouts  25.3 us (2%)
  between operations  15.4 us (1%)
    unnamed x21, waiting for transfers between devices  229 us
    dot_general x14, matrix products, contract(): lax.dot_general(left, right, (((left_dim,), (right_dim,)), ((), ())), pre...  98.5 us
    psum x1, blocking collectives, local(): gain_one, gain_two = lax.psum((attn_gain_part, mlp_gain_part), ('dp', 'mp'))  87 us
    reduce_scatter x1, waiting for transfers between devices, local(): lax.psum_scatter(gate_grad.astype(jnp.bfloat16), 'dp', scatter_dimension=...  82.3 us
    reduce_scatter x1, waiting for transfers between devices, local(): lax.psum_scatter(up_grad.astype(jnp.bfloat16), 'dp', scatter_dimension=0,...  81.2 us
    reduce_scatter x1, waiting for transfers between devices, local(): lax.psum_scatter(query_grad.astype(jnp.bfloat16), 'dp', scatter_dimension...  68.6 us
    reduce_scatter x1, waiting for transfers between devices, local(): lax.psum_scatter((contract(query_low, w_query, 1, 1) + contract(key_low,...  57.2 us
    reduce_scatter x1, waiting for transfers between devices, local(): lax.psum_scatter(jnp.dot(attn_cast, w_out, preferred_element_type=jnp.flo...  55.2 us
  transfers between devices with their start and end apart: 17, of which 15 were waited for; matrix products, arithmetic and copies ran while one was open for 14% of the time, Pallas kernels for 0%

commit v1 on v0

v1 whole, which is shorter than its diff:
```python
import jax
import jax.numpy as jnp
from jax import lax
from jax.sharding import PartitionSpec as P

HEAD_DIM = 64
HALF = 128


EPS = 1e-05
THETA = 500000.0
MASKED = -1e30

BOTH = ("dp", "mp")


def place_of(yh, z, c, yl, x):
    return ((yh * 4 + z) * 2 + c) * 8 + yl * 4 + x


def pairs_of(target, sender=lambda yh, z, c, yl, x: True):
    return [
        (place_of(yh, z, c, yl, x), place_of(*target(yh, z, c, yl, x)))
        for yh in range(2)
        for z in range(4)
        for c in range(2)
        for yl in range(2)
        for x in range(4)
        if sender(yh, z, c, yl, x)
    ]


X_UP = pairs_of(lambda yh, z, c, yl, x: (yh, z, c, yl, (x + 1) % 4))
X_DOWN = pairs_of(lambda yh, z, c, yl, x: (yh, z, c, yl, (x + 3) % 4))
X_FAR = pairs_of(lambda yh, z, c, yl, x: (yh, z, c, yl, (x + 2) % 4))
Z_UP = pairs_of(lambda yh, z, c, yl, x: (yh, (z + 1) % 4, c, yl, x))
Z_DOWN = pairs_of(lambda yh, z, c, yl, x: (yh, (z + 3) % 4, c, yl, x))
Z_FAR = pairs_of(lambda yh, z, c, yl, x: (yh, (z + 2) % 4, c, yl, x))
CORE = pairs_of(lambda yh, z, c, yl, x: (yh, z, 1 - c, yl, x))
Y_LOW = pairs_of(lambda yh, z, c, yl, x: (yh, z, c, 1 - yl, x))
Y_HIGH = pairs_of(lambda yh, z, c, yl, x: (1 - yh, z, c, 1 - yl, x))
Y_FAR = pairs_of(lambda yh, z, c, yl, x: (1 - yh, z, c, yl, x))
TURN = pairs_of(lambda yh, z, c, yl, x: (yh, z, yl, c, x))
NATIVE = lambda yh, z, c, yl, x: c == yl
FOREIGN = lambda yh, z, c, yl, x: c != yl
FOREIGN_LOW = pairs_of(lambda yh, z, c, yl, x: (yh, z, c, 1 - yl, x), FOREIGN)
FOREIGN_HIGH = pairs_of(lambda yh, z, c, yl, x: (1 - yh, z, c, 1 - yl, x), FOREIGN)
NATIVE_FAR = pairs_of(lambda yh, z, c, yl, x: (1 - yh, z, c, yl, x), NATIVE)
NATIVE_CORE = pairs_of(lambda yh, z, c, yl, x: (yh, z, 1 - c, yl, x), NATIVE)
WEIGHT_LOW = pairs_of(
    lambda yh, z, c, yl, x: (yh, z, c, 1 - yl, x) if c == yl else (yh, z, 1 - c, yl, x)
)
WEIGHT_HIGH = pairs_of(
    lambda yh, z, c, yl, x: (1 - yh, z, c, 1 - yl, x) if c == yl else (yh, z, 1 - c, yl, x)
)
Z_GROUPS = [
    [place_of(yh, z, c, yl, x) for z in range(4)]
    for yh in range(2)
    for c in range(2)
    for yl in range(2)
    for x in range(4)
]


def send(values, pairs):
    return lax.ppermute(values, BOTH, pairs)


def gather(rows):
    own = jnp.concatenate([rows, send(rows, X_DOWN), send(rows, X_FAR), send(rows, X_UP)])
    return (own, send(own, CORE))


def scatter(own, other):
    total = (own.astype(jnp.float32) + send(other, CORE).astype(jnp.float32)).astype(jnp.bfloat16)
    rows = total.shape[0] // 4
    part = [total[k * rows : (k + 1) * rows] for k in range(4)]
    one, two, three = send(part[1], X_UP), send(part[2], X_FAR), send(part[3], X_DOWN)
    return (part[0].astype(jnp.float32) + one.astype(jnp.float32)) + (
        two.astype(jnp.float32) + three.astype(jnp.float32)
    )


def in_order(values, core, x):
    half = values.shape[0] // 2
    rows = half // 4
    first = lax.dynamic_slice_in_dim(
        jnp.concatenate([values[:half], values[:half]]), (4 - x) % 4 * rows, half
    )
    second = lax.dynamic_slice_in_dim(
        jnp.concatenate([values[half:], values[half:]]), (4 - x) % 4 * rows, half
    )
    return jnp.concatenate(
        [jnp.where(core == 0, first, second), jnp.where(core == 0, second, first)]
    )


def from_order(values, core, x):
    half = values.shape[0] // 2
    rows = half // 4
    own = jnp.where(core == 0, values[:half], values[half:])
    other = jnp.where(core == 0, values[half:], values[:half])
    return (
        lax.dynamic_slice_in_dim(jnp.concatenate([own, own]), x * rows, half),
        lax.dynamic_slice_in_dim(jnp.concatenate([other, other]), x * rows, half),
    )


def sum_groups(grad, yh, core, native):
    width = grad.shape[1]
    ordered = grad.reshape(2, 4, 2, -1, width).transpose(1, 0, 2, 3, 4).reshape(-1, width)
    kept = lax.psum_scatter(
        ordered, BOTH, scatter_dimension=0, tiled=True, axis_index_groups=Z_GROUPS
    ).reshape(2, -1, width)
    near = jnp.where(yh == 0, kept[0], kept[1])
    far = jnp.where(yh == 0, kept[1], kept[0])
    low = send(near, FOREIGN_LOW)
    high = send(far, FOREIGN_HIGH)
    across = send(far, NATIVE_FAR)
    total = (near.astype(jnp.float32) + low.astype(jnp.float32)) + (
        high.astype(jnp.float32) + across.astype(jnp.float32)
    )
    rows = total.shape[0] // 2
    mine = jnp.where(core == 0, total[:rows], total[rows:])
    theirs = jnp.where(core == 0, total[rows:], total[:rows])
    passed = send(theirs.astype(jnp.bfloat16), NATIVE_CORE).astype(jnp.float32)
    return jnp.where(native, mine, passed)


def inverse_freq(head_width):
    indices = jnp.arange(head_width // 2, dtype=jnp.float32)
    base_freq = jnp.exp(-jnp.log(THETA) * 2.0 * indices / head_width)
    wavelength = 2.0 * jnp.pi / base_freq
    smooth = (8192.0 / wavelength - 1.0) / 3.0
    blended = (1.0 - smooth) * base_freq / 32.0 + smooth * base_freq
    return jnp.where(
        wavelength < 2048.0, base_freq, jnp.where(wavelength > 8192.0, base_freq / 32.0, blended)
    )


def tables(positions, head_width):
    angles = positions.astype(jnp.float32)[:, None] * inverse_freq(head_width)[None, :]
    return (jnp.cos(angles)[:, None, :], jnp.sin(angles)[:, None, :])


def rotate(values, cos_table, sin_table):
    half_dim = values.shape[-1] // 2
    first_half = values[..., :half_dim]
    second_half = values[..., half_dim:]
    return jnp.concatenate(
        [
            first_half * cos_table - second_half * sin_table,
            second_half * cos_table + first_half * sin_table,
        ],
        axis=-1,
    )


def pack_layout(seq_lengths, pack_rows):
    pack_index = jnp.arange(pack_rows, dtype=jnp.int32)
    seq_ends = jnp.cumsum(seq_lengths)
    seq_starts = seq_ends - seq_lengths
    member = (pack_index[:, None] >= seq_starts[None, :]) & (
        pack_index[:, None] < seq_ends[None, :]
    )
    seq_ids = jnp.arange(seq_lengths.shape[0], dtype=jnp.int32)
    segment = jnp.sum(jnp.where(member, seq_ids[None, :], 0), axis=1)
    offset = jnp.sum(jnp.where(member, seq_starts[None, :], 0), axis=1)
    return (pack_index - offset, segment)


def contract(left, right, left_dim, right_dim):
    return lax.dot_general(
        left, right, (((left_dim,), (right_dim,)), ((), ())), preferred_element_type=jnp.float32
    )


def attend_forward(queries, key_rows, value_rows, visible):
    score_scale = queries.shape[-1] ** (-0.5)
    scores = (
        jnp.einsum("rkgd,ckd->kgrc", queries, key_rows, preferred_element_type=jnp.float32)
        * score_scale
    )
    scores = jnp.where(visible[None, None], scores, MASKED)
    row_max = jnp.max(scores, axis=-1, keepdims=True)
    exp_scores = jnp.exp(scores - row_max)
    attn_probs = exp_scores / jnp.sum(exp_scores, axis=-1, keepdims=True)
    probs_low = attn_probs.astype(jnp.bfloat16)
    attn_rows = jnp.einsum(
        "kgrc,ckd->rkgd", probs_low, value_rows, preferred_element_type=jnp.float32
    )
    return (attn_rows, attn_probs, probs_low)


def attend_backward(queries, key_rows, value_rows, attn_probs, probs_low, grad_rows):
    score_scale = queries.shape[-1] ** (-0.5)
    grad_probs = jnp.einsum(
        "rkgd,ckd->kgrc", grad_rows, value_rows, preferred_element_type=jnp.float32
    )
    grad_values = jnp.einsum(
        "kgrc,rkgd->ckd", probs_low, grad_rows, preferred_element_type=jnp.float32
    )
    grad_scores = attn_probs * (
        grad_probs - jnp.sum(attn_probs * grad_probs, axis=-1, keepdims=True)
    )
    scores_low = grad_scores.astype(jnp.bfloat16)
    grad_queries = (
        jnp.einsum("kgrc,ckd->rkgd", scores_low, key_rows, preferred_element_type=jnp.float32)
        * score_scale
    )
    grad_keys = (
        jnp.einsum("kgrc,rkgd->ckd", scores_low, queries, preferred_element_type=jnp.float32)
        * score_scale
    )
    return (grad_queries, grad_keys, grad_values)


def norm_back(grad_in, unit_rows, inv_rms, gain):
    scaled = grad_in * gain
    return inv_rms * (scaled - unit_rows * jnp.mean(scaled * unit_rows, axis=-1, keepdims=True))


def all_sum(values):
    for group in ((CORE,), (X_UP, X_DOWN, X_FAR), (Z_UP, Z_DOWN, Z_FAR), (Y_LOW, Y_HIGH, Y_FAR)):
        values = sum([send(values, pairs) for pairs in group], values)
    return values


def local(
    tokens,
    lengths,
    place,
    attn_gain,
    w_query,
    w_key,
    w_value,
    w_out,
    mlp_gain,
    w_gate,
    w_up,
    w_down,
    out_grad,
):
    head_width = HEAD_DIM
    kv_local = w_key.shape[1] // head_width
    query_heads = w_query.shape[1] // head_width
    kv_group = query_heads // kv_local
    kv_width = kv_local * head_width
    attn_width = query_heads * head_width
    local_rows = tokens.shape[0]
    group_rows = local_rows * 8
    long_rows = 2 * HALF
    pack_rows = group_rows - long_rows
    dp_index, mp_index = lax.axis_index("dp"), lax.axis_index("mp")
    yh, z, core = dp_index // 8, dp_index // 2 % 4, dp_index % 2
    yl, x = mp_index // 4, mp_index % 4
    native = core == yl

    tokens = send(tokens, TURN)
    lengths = send(lengths, TURN)
    w_key, w_value = send(w_key, WEIGHT_HIGH), send(w_value, WEIGHT_HIGH)
    w_query = send(w_query, WEIGHT_LOW)
    w_out = send(w_out, WEIGHT_HIGH)
    w_gate = send(w_gate, WEIGHT_LOW)
    w_up = send(w_up, WEIGHT_HIGH)
    w_down = send(w_down, WEIGHT_LOW)
    out_grad = send(out_grad, TURN)

    long_local = jnp.arange(long_rows, dtype=jnp.int32)

    def place_at(index):
        return jnp.sum(jnp.where(jnp.arange(place.shape[0]) == index, place, 0))

    def long_positions(group):
        pair = (place_at(2 * group), place_at(2 * group + 1))
        return jnp.where(long_local < HALF, pair[0], pair[1]) * HALF + long_local % HALF

    long_pos = long_positions((yh * 4 + z) * 2 + yl)
    far_pos = jnp.concatenate(
        [
            long_positions((gy * 4 + (z + step) % 4) * 2 + gl)
            for gy, gl in ((yh, yl), (yh, 1 - yl), (1 - yh, 1 - yl), (1 - yh, yl))
            for step in range(4)
        ]
    )
    short_pos, segment = pack_layout(lengths[0], pack_rows)
    positions = jnp.concatenate([long_pos, short_pos])
    cos_table, sin_table = tables(positions, head_width)
    long_visible = long_pos[:, None] >= far_pos[None, :]
    pack_index = jnp.arange(pack_rows, dtype=jnp.int32)
    short_visible = (segment[:, None] == segment[None, :]) & (
        pack_index[:, None] >= pack_index[None, :]
    )
    residual = tokens.astype(jnp.float32)
    inv_one = lax.rsqrt(jnp.mean(residual * residual, axis=-1, keepdims=True) + EPS)
    unit_one = residual * inv_one
    local_one = (unit_one * attn_gain).astype(jnp.bfloat16)
    hidden_own, hidden_other = gather(local_one)
    w_qkv = jnp.concatenate([w_query, w_key, w_value], axis=1)
    qkv = in_order(
        jnp.concatenate(
            [
                jnp.dot(hidden_own, w_qkv, preferred_element_type=jnp.float32),
                jnp.dot(hidden_other, w_qkv, preferred_element_type=jnp.float32),
            ]
        ),
        core,
        x,
    )
    query_raw = qkv[:, :attn_width].reshape(group_rows, query_heads, head_width)
    key_raw = qkv[:, attn_width : attn_width + kv_width].reshape(group_rows, kv_local, head_width)
    value_all = qkv[:, attn_width + kv_width :].astype(jnp.bfloat16)
    key_all = (
        rotate(key_raw, cos_table, sin_table).astype(jnp.bfloat16).reshape(group_rows, kv_width)
    )
    near_rows = jnp.concatenate([key_all[:long_rows], value_all[:long_rows]], axis=1)
    ring_rows = jnp.concatenate(
        [near_rows, send(near_rows, Z_DOWN), send(near_rows, Z_FAR), send(near_rows, Z_UP)]
    )
    far_rows = jnp.concatenate(
        [ring_rows, send(ring_rows, Y_LOW), send(ring_rows, Y_HIGH), send(ring_rows, Y_FAR)]
    )
    query_all = (
        rotate(query_raw, cos_table, sin_table)
        .astype(jnp.bfloat16)
        .reshape(group_rows, kv_local, kv_group, head_width)
    )
    far_keys = far_rows[:, :kv_width].reshape(-1, kv_local, head_width)
    far_values = far_rows[:, kv_width:].reshape(-1, kv_local, head_width)
    key_local = key_all.reshape(group_rows, kv_local, head_width)
    value_local = value_all.reshape(group_rows, kv_local, head_width)
    short_attn, short_probs, short_low = attend_forward(
        query_all[long_rows:], key_local[long_rows:], value_local[long_rows:], short_visible
    )
    long_attn, long_probs, long_low = attend_forward(
        query_all[:long_rows], far_keys, far_values, long_visible
    )
    attn_own, attn_other = from_order(
        jnp.concatenate([long_attn, short_attn])
        .reshape(group_rows, attn_width)
        .astype(jnp.bfloat16),
        core,
        x,
    )

    def project(left, right):
        return jnp.dot(left, right, preferred_element_type=jnp.float32).astype(jnp.bfloat16)

    mixed = residual + scatter(project(attn_own, w_out), project(attn_other, w_out))
    inv_two = lax.rsqrt(jnp.mean(mixed * mixed, axis=-1, keepdims=True) + EPS)
    unit_two = mixed * inv_two
    local_two = (unit_two * mlp_gain).astype(jnp.bfloat16)
    grad_rows = jnp.concatenate(gather(out_grad))
    grad_act = contract(grad_rows, w_down, 1, 1)
    hidden_two = jnp.concatenate(gather(local_two))
    gate_proj = jnp.dot(hidden_two, w_gate, preferred_element_type=jnp.float32)
    up_proj = jnp.dot(hidden_two, w_up, preferred_element_type=jnp.float32)
    gate_sig = jax.nn.sigmoid(gate_proj)
    gate_act = gate_proj * gate_sig
    act_low = (gate_act * up_proj).astype(jnp.bfloat16)
    grad_gate = (grad_act * up_proj * gate_sig * (1.0 + gate_proj * (1.0 - gate_sig))).astype(
        jnp.bfloat16
    )
    grad_up = (grad_act * gate_act).astype(jnp.bfloat16)
    half_rows = group_rows // 2
    grad_hidden = (contract(grad_gate, w_gate, 1, 1) + contract(grad_up, w_up, 1, 1)).astype(
        jnp.bfloat16
    )
    grad_two = scatter(grad_hidden[:half_rows], grad_hidden[half_rows:])
    down_part = contract(grad_rows, act_low, 0, 0).astype(jnp.bfloat16)
    gate_part = contract(hidden_two, grad_gate, 0, 0).astype(jnp.bfloat16)
    up_part = contract(hidden_two, grad_up, 0, 0).astype(jnp.bfloat16)
    down_sum = sum_groups(down_part, yh, core, native).T
    gate_sum = sum_groups(gate_part, yh, core, native)
    up_sum = sum_groups(up_part, yh, core, native)
    down_rows = project(act_low, w_down)
    output = mixed + scatter(down_rows[:half_rows], down_rows[half_rows:])
    output = send(output.astype(jnp.bfloat16), TURN)
    grad_mixed = out_grad.astype(jnp.float32) + norm_back(grad_two, unit_two, inv_two, mlp_gain)
    mixed_grad_rows = jnp.concatenate(gather(grad_mixed.astype(jnp.bfloat16)))
    mlp_gain_part = jnp.sum(grad_two * unit_two, axis=0)
    attn_rel = jnp.concatenate([attn_own, attn_other])
    out_part = contract(mixed_grad_rows, attn_rel, 0, 0).astype(jnp.bfloat16)
    out_sum = sum_groups(out_part, yh, core, native).T
    grad_attn = in_order(
        contract(mixed_grad_rows, w_out, 1, 1).astype(jnp.bfloat16), core, x
    ).reshape(group_rows, kv_local, kv_group, head_width)
    long_dq, long_dk, long_dv = attend_backward(
        query_all[:long_rows], far_keys, far_values, long_probs, long_low, grad_attn[:long_rows]
    )
    far_terms = jnp.concatenate(
        [long_dk.reshape(-1, kv_width), long_dv.reshape(-1, kv_width)], axis=1
    ).astype(jnp.bfloat16)
    ring = far_terms.reshape(4, 4 * long_rows, 2 * kv_width)
    ring_terms = (
        (ring[0].astype(jnp.float32) + send(ring[1], Y_LOW).astype(jnp.float32))
        + (send(ring[2], Y_HIGH).astype(jnp.float32) + send(ring[3], Y_FAR).astype(jnp.float32))
    ).astype(jnp.bfloat16)
    near = ring_terms.reshape(4, long_rows, 2 * kv_width)
    far_grads = (near[0].astype(jnp.float32) + send(near[1], Z_UP).astype(jnp.float32)) + (
        send(near[2], Z_FAR).astype(jnp.float32) + send(near[3], Z_DOWN).astype(jnp.float32)
    )
    short_dq, short_dk, short_dv = attend_backward(
        query_all[long_rows:],
        key_local[long_rows:],
        value_local[long_rows:],
        short_probs,
        short_low,
        grad_attn[long_rows:],
    )
    key_grad_all = jnp.concatenate(
        [far_grads[:, :kv_width], short_dk.reshape(pack_rows, kv_width)]
    ).reshape(group_rows, kv_local, head_width)
    value_low = jnp.concatenate(
        [far_grads[:, kv_width:], short_dv.reshape(pack_rows, kv_width)]
    ).astype(jnp.bfloat16)
    query_grad_all = jnp.concatenate([long_dq, short_dq]).reshape(
        group_rows, query_heads, head_width
    )
    query_low = (
        rotate(query_grad_all, cos_table, -sin_table)
        .reshape(group_rows, attn_width)
        .astype(jnp.bfloat16)
    )
    key_low = (
        rotate(key_grad_all, cos_table, -sin_table)
        .reshape(group_rows, kv_width)
        .astype(jnp.bfloat16)
    )
    low_own, low_other = from_order(
        jnp.concatenate([query_low, key_low, value_low], axis=1), core, x
    )
    grad_one = scatter(
        contract(low_own, w_qkv, 1, 1).astype(jnp.bfloat16),
        contract(low_other, w_qkv, 1, 1).astype(jnp.bfloat16),
    )
    qkv_part = (
        contract(hidden_own, low_own, 0, 0) + contract(hidden_other, low_other, 0, 0)
    ).astype(jnp.bfloat16)
    qkv_sum = sum_groups(qkv_part, yh, core, native)
    attn_gain_part = jnp.sum(grad_one * unit_one, axis=0)
    grad_tokens = grad_mixed + norm_back(grad_one, unit_one, inv_one, attn_gain)
    grad_tokens = send(grad_tokens.astype(jnp.bfloat16), TURN)
    gains = all_sum(jnp.stack([attn_gain_part, mlp_gain_part]))
    return (
        output,
        grad_tokens,
        gains[0],
        qkv_sum[:, :attn_width],
        qkv_sum[:, attn_width : attn_width + kv_width],
        qkv_sum[:, attn_width + kv_width :],
        out_sum,
        gains[1],
        gate_sum,
        up_sum,
        down_sum,
    )


def solution(mesh):
    placed = (
        P(("dp", "mp"), None),
        P("dp", None),
        P(),
        P(),
        P(None, "mp"),
        P(None, "mp"),
        P(None, "mp"),
        P("mp", None),
        P(),
        P(None, "mp"),
        P(None, "mp"),
        P("mp", None),
        P(("dp", "mp"), None),
    )
    return jax.shard_map(
        local,
        mesh=mesh,
        in_specs=placed,
        out_specs=(
            P(("dp", "mp"), None),
            P(("dp", "mp"), None),
            P(),
            P("dp", "mp"),
            P("dp", "mp"),
            P("dp", "mp"),
            P("mp", "dp"),
            P(),
            P("dp", "mp"),
            P("dp", "mp"),
            P("mp", "dp"),
        ),
        check_vma=False,
    )
```

time: 1240 us -> 764 us (0.62)
  waiting for transfers between devices: 848 us -> 237 us
  starting transfers between devices: 2.21 us -> 135 us
  blocking collectives: 87 us -> 0 us
  local copies, waits for them, and re-layouts: 25.3 us -> 96.5 us
  other arithmetic: 57.8 us -> 94.7 us
  matrix products: 204 us -> 175 us
    reduce_scatter x8 -> x5, waiting for transfers between devices: 398 us -> 0.03 us  [sum_groups(): lax.psum_scatter(ordered, BOTH, scatter_dimension=0, tiled=True, axis_ind...]
    ppermute x0 -> x86, waiting for transfers between devices: none -> 237 us  [send(): return lax.ppermute(values, BOTH, pairs)]
    unnamed x21 -> x5, waiting for transfers between devices: 229 us -> 0.08 us
    all_gather x5 -> x0, waiting for transfers between devices: 221 us -> none  [the longest x1 53.9 us: local(): lax.all_gather(grad_mixed.astype(jnp.bfloat16), 'mp', axis=0, tiled=True)]
    ppermute x0 -> x86, starting transfers between devices: none -> 135 us  [send(): return lax.ppermute(values, BOTH, pairs)]
    psum x1 -> x0, blocking collectives: 87 us -> none  [local(): gain_one, gain_two = lax.psum((attn_gain_part, mlp_gain_part), ('dp', 'mp'))]
    transpose x0 -> x5, local copies, waits for them, and re-layouts: none -> 40.1 us  [sum_groups(): grad.reshape(2, 4, 2, -1, width).transpose(1, 0, 2, 3, 4).reshape(-1, width)]
    reshape x0 -> x5, local copies, waits for them, and re-layouts: none -> 29.1 us  [sum_groups(): grad.reshape(2, 4, 2, -1, width).transpose(1, 0, 2, 3, 4).reshape(-1, width)]
  transfers between devices with their start and end apart: 17 -> 91, of which waited for: 15 -> 35; matrix products, arithmetic and copies ran while one was open for 14% -> 43% of each run, Pallas kernels for 0% -> 0%
where the time goes in v1:
time: 764 us; the launch traced here: 755 us
  waiting for transfers between devices  237 us (31%)
  matrix products  175 us (23%)
  starting transfers between devices  135 us (18%)
  local copies, waits for them, and re-layouts  96.5 us (13%)
  other arithmetic  94.7 us (12%)
  between operations  16.8 us (2%)
    ppermute x86, waiting for transfers between devices, send(): return lax.ppermute(values, BOTH, pairs)  237 us
    ppermute x86, starting transfers between devices, send(): return lax.ppermute(values, BOTH, pairs)  135 us
    dot_general x12, matrix products, contract(): lax.dot_general(left, right, (((left_dim,), (right_dim,)), ((), ())), pre...  80.6 us
    transpose x5, local copies, waits for them, and re-layouts, sum_groups(): grad.reshape(2, 4, 2, -1, width).transpose(1, 0, 2, 3, 4).reshape(-1, width)  40.1 us
    reshape x5, local copies, waits for them, and re-layouts, sum_groups(): grad.reshape(2, 4, 2, -1, width).transpose(1, 0, 2, 3, 4).reshape(-1, width)  29.1 us
    dot_general x2, matrix products, attend_backward(): jnp.einsum('rkgd,ckd->kgrc', grad_rows, value_rows, preferred_element_typ...  25.1 us
    unnamed x20, other arithmetic  22.4 us
    unnamed x188, local copies, waits for them, and re-layouts  18.8 us
  transfers between devices with their start and end apart: 91, of which 35 were waited for; matrix products, arithmetic and copies ran while one was open for 43% of the time, Pallas kernels for 0%

profile of v1, /device:TPU:1, one launch (start us, length us, event | category | flops | bytes accessed | tf_op | source)
XLA Modules:
  0.0 755.5 jit_solution(13639557935104171882)
XLA Ops:
  51.3 9.4 %collective-permute-done.2 = bf16[136,2048]{1,0:T(8,128)(2,1)S(1)} collective-permute-done((bf16[136,2048]{1,0:T(8,128)(2,1)S(1)}, bf16[136,2048]{1,0:T(8,128)(2,1)S(1)}, u32[]{:S(2)}, u32[]{:S(2)}) %collective-permute-start.2) | collective-permute-done | bytes 557088 | tf_op jit(solution)/shard_map/ppermute | solution.py:66
  141.0 14.5 %collective-permute-done.32 = bf16[136,2048]{1,0:T(8,128)(2,1)S(1)} collective-permute-done((bf16[136,2048]{1,0:T(8,128)(2,1)S(1)}, bf16[136,2048]{1,0:T(8,128)(2,1)S(1)}, u32[]{:S(2)}, u32[]{:S(2)}) %collective-permute-start.32) | collective-permute-done | bytes 557088 | tf_op jit(solution)/shard_map/ppermute | solution.py:66
  161.2 21.4 %collective-permute-done.35 = bf16[136,2048]{1,0:T(8,128)(2,1)S(1)} collective-permute-done((bf16[136,2048]{1,0:T(8,128)(2,1)S(1)}, bf16[136,2048]{1,0:T(8,128)(2,1)S(1)}, u32[]{:S(2)}, u32[]{:S(2)}) %collective-permute-start.35) | collective-permute-done | bytes 557088 | tf_op jit(solution)/shard_map/ppermute | solution.py:66
  183.0 13.7 %collective-permute-done.17 = bf16[136,2048]{1,0:T(8,128)(2,1)S(1)} collective-permute-done((bf16[136,2048]{1,0:T(8,128)(2,1)S(1)}, bf16[136,2048]{1,0:T(8,128)(2,1)S(1)}, u32[]{:S(2)}, u32[]{:S(2)}) %collective-permute-start.17) | collective-permute-done | bytes 557088 | tf_op jit(solution)/shard_map/ppermute | solution.py:66
  235.7 10.8 %collective-permute-done.25 = bf16[2048,1024]{1,0:T(8,128)(2,1)} collective-permute-done((bf16[2048,1024]{1,0:T(8,128)(2,1)}, bf16[2048,1024]{1,0:T(8,128)(2,1)}, u32[]{:S(2)}, u32[]{:S(2)}) %collective-permute-start.25) | collective-permute-done | bytes 4194336 | tf_op jit(solution)/shard_map/ppermute | solution.py:66
  253.5 14.4 %collective-permute-done.24 = bf16[2048,1024]{1,0:T(8,128)(2,1)} collective-permute-done((bf16[2048,1024]{1,0:T(8,128)(2,1)}, bf16[2048,1024]{1,0:T(8,128)(2,1)}, u32[]{:S(2)}, u32[]{:S(2)}) %collective-permute-start.24) | collective-permute-done | bytes 4194336 | tf_op jit(solution)/shard_map/ppermute | solution.py:66
  267.9 10.1 %multiply_convert_fusion.1 = (bf16[1088,1024]{1,0:T(8,128)(2,1)}, bf16[1088,1024]{1,0:T(8,128)(2,1)S(1)}, bf16[1088,1024]{1,0:T(8,128)(2,1)S(1)}) fusion(f32[1088,1024]{1,0:T(8,128)S(1)} %fusion.180, f32[1088,1024]{1,0:T(8,128)S(1)} %fusion.179, bf16[1088,2048]{1,0:T(8,128)(2,1)S(1)} %constant_dynamic-update-slice_fusion.8, ...), kind=kOutput, calls=%fused_computation.44 | convolution fusion | flops 4580114432 | bytes 24248320 | tf_op jit(solution)/shard_map/dot_general | solution.py:356
  288.5 9.3 %fusion.181 = f32[1088,2048]{1,0:T(8,128)} fusion(bf16[1088,1024]{1,0:T(8,128)(2,1)S(1)} %get-tuple-element.103, bf16[2048,1024]{1,0:T(8,128)(2,1)} %collective-permute-done.25), kind=kOutput, calls=%fused_computation.381 | convolution fusion | flops 4563402752 | bytes 15335424 | tf_op jit(solution)/shard_map/dot_general | solution.py:173
  297.8 10.3 %fusion.17 = bf16[1088,2048]{1,0:T(8,128)(2,1)S(1)} fusion(f32[1088,2048]{1,0:T(8,128)} %fusion.181, bf16[1088,1024]{1,0:T(8,128)(2,1)} %get-tuple-element.102, bf16[2048,1024]{1,0:T(8,128)(2,1)} %collective-permute-done.24), kind=kOutput, calls=%fused_computation.27 | convolution fusion | flops 4567859200 | bytes 19791872 | tf_op jit(solution)/shard_map/dot_general | solution.py:173
  316.5 19.1 %collective-permute-done.28 = bf16[136,2048]{1,0:T(8,128)(2,1)S(1)} collective-permute-done((bf16[136,2048]{1,0:T(8,128)(2,1)S(1)}, bf16[136,2048]{1,0:T(8,128)(2,1)S(1)}, u32[]{:S(2)}, u32[]{:S(2)}) %collective-permute-start.28) | collective-permute-done | bytes 557088 | tf_op jit(solution)/shard_map/ppermute | solution.py:66
  335.6 13.7 %collective-permute-done.38 = bf16[136,2048]{1,0:T(8,128)(2,1)S(1)} collective-permute-done((bf16[136,2048]{1,0:T(8,128)(2,1)S(1)}, bf16[136,2048]{1,0:T(8,128)(2,1)S(1)}, u32[]{:S(2)}, u32[]{:S(2)}) %collective-permute-start.38) | collective-permute-done | bytes 557088 | tf_op jit(solution)/shard_map/ppermute | solution.py:66
  349.3 10.1 %collective-permute-done.39 = bf16[136,2048]{1,0:T(8,128)(2,1)S(1)} collective-permute-done((bf16[136,2048]{1,0:T(8,128)(2,1)S(1)}, bf16[136,2048]{1,0:T(8,128)(2,1)S(1)}, u32[]{:S(2)}, u32[]{:S(2)}) %collective-permute-start.39) | collective-permute-done | bytes 557088 | tf_op jit(solution)/shard_map/ppermute | solution.py:66
  368.1 9.8 %collective-permute-done.43 = bf16[136,2048]{1,0:T(8,128)(2,1)S(1)} collective-permute-done((bf16[136,2048]{1,0:T(8,128)(2,1)S(1)}, bf16[136,2048]{1,0:T(8,128)(2,1)S(1)}, u32[]{:S(2)}, u32[]{:S(2)}) %collective-permute-start.43) | collective-permute-done | bytes 557088 | tf_op jit(solution)/shard_map/ppermute | solution.py:66
  378.0 13.1 %collective-permute-done.42 = bf16[136,2048]{1,0:T(8,128)(2,1)S(1)} collective-permute-done((bf16[136,2048]{1,0:T(8,128)(2,1)S(1)}, bf16[136,2048]{1,0:T(8,128)(2,1)S(1)}, u32[]{:S(2)}, u32[]{:S(2)}) %collective-permute-start.42) | collective-permute-done | bytes 557088 | tf_op jit(solution)/shard_map/ppermute | solution.py:66
  403.0 9.6 %convolution_convert_fusion.1 = bf16[2048,1024]{1,0:T(8,128)(2,1)} fusion(bf16[1088,2048]{1,0:T(8,128)(2,1)} %copy-done.56, bf16[1088,1024]{1,0:T(8,128)(2,1)} %copy-done.76), kind=kOutput, calls=%fused_computation.51 | convolution fusion | flops 4565499904 | bytes 10878976 | tf_op jit(solution)/shard_map/dot_general | solution.py:173
  412.7 11.3 %copy.149 = bf16[4,2,2,128,1024]{3,2,1,0,4:T(2,128)(2,1)} copy(bf16[4,2,2,128,1024]{4,3,2,0,1:T(8,128)(2,1)} %bitcast.296) | data formatting | bytes 8388608 | tf_op jit(solution)/shard_map/transpose | solution.py:111
  433.4 9.5 %convolution_convert_fusion.3 = bf16[2048,1024]{1,0:T(8,128)(2,1)} fusion(bf16[1088,2048]{1,0:T(8,128)(2,1)} %copy-done.55, bf16[1088,1024]{1,0:T(8,128)(2,1)S(1)} %copy-done.75), kind=kOutput, calls=%fused_computation.53 | convolution fusion | flops 4565499904 | bytes 10878976 | tf_op jit(solution)/shard_map/dot_general | solution.py:173
  442.9 11.4 %copy.147 = bf16[4,2,2,128,1024]{3,2,1,0,4:T(2,128)(2,1)} copy(bf16[4,2,2,128,1024]{4,3,2,0,1:T(8,128)(2,1)} %bitcast.298) | data formatting | bytes 8388608 | tf_op jit(solution)/shard_map/transpose | solution.py:111
  463.8 9.6 %convolution_convert_fusion.2 = bf16[2048,1024]{1,0:T(8,128)(2,1)} fusion(bf16[1088,2048]{1,0:T(8,128)(2,1)} %copy-done.55, bf16[1088,1024]{1,0:T(8,128)(2,1)S(1)} %copy-done.74), kind=kOutput, calls=%fused_computation.52 | convolution fusion | flops 4565499904 | bytes 10878976 | tf_op jit(solution)/shard_map/dot_general | solution.py:173
  473.4 11.3 %copy.148 = bf16[4,2,2,128,1024]{3,2,1,0,4:T(2,128)(2,1)} copy(bf16[4,2,2,128,1024]{4,3,2,0,1:T(8,128)(2,1)} %bitcast.297) | data formatting | bytes 8388608 | tf_op jit(solution)/shard_map/transpose | solution.py:111
  507.1 13.3 %fusion = (f32[4,256]{1,0:T(4,128)S(1)}, f32[4096,256,4]{1,0,2:T(8,128)}) fusion(f32[4,256]{1,0:T(4,128)S(1)} %copy-done.67, f32[4,256]{1,0:T(4,128)S(1)} %copy-done.65, f32[4096,256,4]{1,0,2:T(8,128)} %copy-done, pred[256,4096]{0,1:T(8,128)(4,1)S(1)} %copy-done.5, bf16[256,4,64]{0,2,1:T(8,128)(2,1)S(1)} %bitcast.313, bf16[4096,128]{0,1:T(8,128)(2,1)} %copy-done.43), kind=kOutput, calls=%fused_computation.3 | convolution fusion | flops 562035712 | bytes 35270656 | tf_op jit(solution)/shard_map/rkgd,ckd->kgrc/dot_general | solution.py:197
  520.4 9.0 %fusion.12 = bf16[4,256,4096]{1,2,0:T(8,128)(2,1)S(1)} fusion(f32[4096,256,4]{1,0,2:T(8,128)} %get-tuple-element.166, f32[4,256]{1,0:T(4,128)S(1)} %get-tuple-element.165, f32[4,256]{1,0:T(4,128)S(1)} %copy-done.67, f32[4,256]{1,0:T(4,128)S(1)} %copy-done.65, f32[4096,256,4]{1,0,2:T(8,128)S(1)} %bitcast.292, pred[256,4096]{0,1:T(8,128)(4,1)S(1)} %copy-done.5), kind=kLoop, calls=%fused_computation.21 | loop fusion | flops 29360128 | bytes 43003904 | tf_op jit(solution)/shard_map/reshape.32
  534.0 11.8 %fusion.6 = (f32[4,832]{1,0:T(4,128)S(1)}, f32[832,832,4]{1,0,2:T(8,128)}) fusion(f32[4,832]{1,0:T(4,128)S(1)} %copy-done.61, f32[4,832]{1,0:T(4,128)S(1)} %copy-done.59, f32[832,832,4]{1,0,2:T(8,128)} %copy-done.1, pred[832,832]{0,1:T(8,128)(4,1)S(1)} %copy-done.7, bf16[832,4,64]{0,2,1:T(8,128)(2,1)S(1)} %bitcast.304, bf16[1088,384]{0,1:T(8,128)(2,1)} %copy-done.24), kind=kOutput, calls=%fused_computation.13 | convolution fusion | flops 371028736 | bytes 24275968 | tf_op jit(solution)/shard_map/rkgd,ckd->kgrc/dot_general | solution.py:197
  681.9 9.5 %collective-permute-done.82 = bf16[256,1024]{0,1:T(8,128)(2,1)S(1)} collective-permute-done((bf16[256,1024]{0,1:T(8,128)(2,1)S(1)}, bf16[256,1024]{0,1:T(8,128)(2,1)S(1)}, u32[]{:S(2)}, u32[]{:S(2)}) %collective-permute-start.82) | collective-permute-done | bytes 524320 | tf_op jit(solution)/shard_map/ppermute | solution.py:66
  (520 shorter events, 452.8 us)
Async XLA Ops:
  7.2 599.0 %reduce-scatter.8.cloned.1.call-start = ((), (), s32[]{:S(2)}) async-start(), calls=%async_computation.6 | async-start | bytes 1310720 | tf_op jit(solution)/shard_map/reduce_scatter | solution.py:112
  7.2 61.5 %collective-permute-start.8 = (s32[1,3]{1,0:T(1,128)}, s32[1,3]{1,0:T(1,128)S(1)}, u32[]{:S(2)}, u32[]{:S(2)}) collective-permute-start(s32[1,3]{1,0:T(1,128)} %param.14), channel_id=1, source_target_pairs={{0,0},{1,1},{2,2},{3,3},{4,8},{5,9},{6,10},{7,11},{8,4},{9,5},{10,... | collective-permute-start | bytes 44 | tf_op jit(solution)/shard_map/ppermute | solution.py:66
  11.8 59.4 %collective-permute-start.5 = (bf16[2048,64]{0,1:T(8,128)(2,1)}, bf16[2048,64]{0,1:T(8,128)(2,1)}, u32[]{:S(2)}, u32[]{:S(2)}) collective-permute-start(bf16[2048,64]{0,1:T(8,128)(2,1)} %param.18), channel_id=1, source_target_pairs={{0,68},{1,69},{2,70},{3,71},{4,12},{5,13},{6,14},{7,15},{8,0},{9,1... | collective-permute-start | bytes 786440 | tf_op jit(solution)/shard_map/ppermute | solution.py:66
  68.8 68.0 %collective-permute-start.15 = (bf16[256,2048]{1,0:T(8,128)(2,1)}, bf16[256,2048]{1,0:T(8,128)(2,1)S(1)}, u32[]{:S(2)}, u32[]{:S(2)}) collective-permute-start(bf16[256,2048]{1,0:T(8,128)(2,1)} %param.20), channel_id=1, source_target_pairs={{0,68},{1,69},{2,70},{3,71},{4,12},{5,13},{6,14},{7,15},{8,0},{9,1... | collective-permute-start | bytes 3145736 | tf_op jit(solution)/shard_map/ppermute | solution.py:66
  140.9 85.8 %collective-permute-start.26 = (bf16[1024,2048]{1,0:T(8,128)(2,1)}, bf16[1024,2048]{1,0:T(8,128)(2,1)}, u32[]{:S(2)}, u32[]{:S(2)}) collective-permute-start(bf16[1024,2048]{1,0:T(8,128)(2,1)} %param.24), channel_id=1, source_target_pairs={{0,4},{1,5},{2,6},{3,7},{4,12},{5,13},{6,14},{7,15},{8,0},{9,1},{1... | collective-permute-start | bytes 12582920 | tf_op jit(solution)/shard_map/ppermute | solution.py:66
  160.6 36.1 %collective-permute-start.17 = (bf16[136,2048]{1,0:T(8,128)(2,1)S(1)}, bf16[136,2048]{1,0:T(8,128)(2,1)S(1)}, u32[]{:S(2)}, u32[]{:S(2)}) collective-permute-start(bf16[136,2048]{1,0:T(8,128)(2,1)S(1)} %get-tuple-element.114), channel_id=1, source_target_pairs={{0,1},{1,2},{2,3},{3,0},{4,5},{5,6},{6,7},{7,4},{8,9},{9,10},{10,1... | collective-permute-start | bytes 1671176 | tf_op jit(solution)/shard_map/ppermute | solution.py:66
  182.9 43.5 %collective-permute-start.36 = (bf16[544,2048]{1,0:T(8,128)(2,1)S(1)}, bf16[544,2048]{1,0:T(8,128)(2,1)S(1)}, u32[]{:S(2)}, u32[]{:S(2)}) collective-permute-start(bf16[544,2048]{1,0:T(8,128)(2,1)S(1)} %pad_maximum_fusion.3), channel_id=1, source_target_pairs={{0,8},{1,9},{2,10},{3,11},{4,12},{5,13},{6,14},{7,15},{8,0},{9,1},... | collective-permute-start | bytes 6684680 | tf_op jit(solution)/shard_map/ppermute | solution.py:66
  197.6 49.0 %collective-permute-start.25 = (bf16[2048,1024]{1,0:T(8,128)(2,1)}, bf16[2048,1024]{1,0:T(8,128)(2,1)}, u32[]{:S(2)}, u32[]{:S(2)}) collective-permute-start(bf16[2048,1024]{1,0:T(8,128)(2,1)} %param.23), channel_id=1, source_target_pairs={{0,68},{1,69},{2,70},{3,71},{4,12},{5,13},{6,14},{7,15},{8,0},{9,1... | collective-permute-start | bytes 12582920 | tf_op jit(solution)/shard_map/ppermute | solution.py:66
  220.2 47.7 %collective-permute-start.24 = (bf16[2048,1024]{1,0:T(8,128)(2,1)}, bf16[2048,1024]{1,0:T(8,128)(2,1)}, u32[]{:S(2)}, u32[]{:S(2)}) collective-permute-start(bf16[2048,1024]{1,0:T(8,128)(2,1)} %param.22), channel_id=1, source_target_pairs={{0,4},{1,5},{2,6},{3,7},{4,12},{5,13},{6,14},{7,15},{8,0},{9,1},{1... | collective-permute-start | bytes 12582920 | tf_op jit(solution)/shard_map/ppermute | solution.py:66
  313.8 35.5 %collective-permute-start.38 = (bf16[136,2048]{1,0:T(8,128)(2,1)S(1)}, bf16[136,2048]{1,0:T(8,128)(2,1)S(1)}, u32[]{:S(2)}, u32[]{:S(2)}) collective-permute-start(bf16[136,2048]{1,0:T(8,128)(2,1)S(1)} %get-tuple-element.108), channel_id=1, source_target_pairs={{0,1},{1,2},{2,3},{3,0},{4,5},{5,6},{6,7},{7,4},{8,9},{9,10},{10,1... | collective-permute-start | bytes 1671176 | tf_op jit(solution)/shard_map/ppermute | solution.py:66
  314.0 35.3 %collective-permute-start.40 = (bf16[136,2048]{1,0:T(8,128)(2,1)S(1)}, bf16[136,2048]{1,0:T(8,128)(2,1)S(1)}, u32[]{:S(2)}, u32[]{:S(2)}) collective-permute-start(bf16[136,2048]{1,0:T(8,128)(2,1)S(1)} %get-tuple-element.109), channel_id=1, source_target_pairs={{0,3},{1,0},{2,1},{3,2},{4,7},{5,4},{6,5},{7,6},{8,11},{9,8},{10,9... | collective-permute-start | bytes 1671176 | tf_op jit(solution)/shard_map/ppermute | solution.py:66
  403.0 234.9 %reduce-scatter.14.cloned.1.call-start = ((), (), s32[]{:S(2)}) async-start(), calls=%async_computation.9 | async-start | bytes 5242880 | tf_op jit(solution)/shard_map/reduce_scatter | solution.py:112
  431.8 218.4 %reduce-scatter.10.cloned.1.call-start = ((), (), s32[]{:S(2)}) async-start(), calls=%async_computation.7 | async-start | bytes 5242880 | tf_op jit(solution)/shard_map/reduce_scatter | solution.py:112
  462.2 193.3 %reduce-scatter.12.cloned.1.call-start = ((), (), s32[]{:S(2)}) async-start(), calls=%async_computation.8 | async-start | bytes 5242880 | tf_op jit(solution)/shard_map/reduce_scatter | solution.py:112
  492.7 229.4 %reduce-scatter.6.cloned.1.call-start = ((), (), s32[]{:S(2)}) async-start(), calls=%async_computation.5 | async-start | bytes 1966080 | tf_op jit(solution)/shard_map/reduce_scatter | solution.py:112
  586.2 29.2 %collective-permute-start.51 = (bf16[544,2048]{1,0:T(8,128)(2,1)}, bf16[544,2048]{1,0:T(8,128)(2,1)}, u32[]{:S(2)}, u32[]{:S(2)}) collective-permute-start(bf16[544,2048]{1,0:T(8,128)(2,1)} %convolution_convert_fusion.4), channel_id=1, source_target_pairs={{0,8},{1,9},{2,10},{3,11},{4,12},{5,13},{6,14},{7,15},{8,0},{9,1},... | collective-permute-start | bytes 6684680 | tf_op jit(solution)/shard_map/ppermute | solution.py:66
  619.1 28.9 %collective-permute-start.52 = (bf16[136,2048]{1,0:T(8,128)(2,1)}, bf16[136,2048]{1,0:T(8,128)(2,1)S(1)}, u32[]{:S(2)}, u32[]{:S(2)}) collective-permute-start(bf16[136,2048]{1,0:T(8,128)(2,1)} %get-tuple-element.105), channel_id=1, source_target_pairs={{0,1},{1,2},{2,3},{3,0},{4,5},{5,6},{6,7},{7,4},{8,9},{9,10},{10,1... | collective-permute-start | bytes 1671176 | tf_op jit(solution)/shard_map/ppermute | solution.py:66
  619.1 28.8 %collective-permute-start.54 = (bf16[136,2048]{1,0:T(8,128)(2,1)}, bf16[136,2048]{1,0:T(8,128)(2,1)}, u32[]{:S(2)}, u32[]{:S(2)}) collective-permute-start(bf16[136,2048]{1,0:T(8,128)(2,1)} %get-tuple-element.106), channel_id=1, source_target_pairs={{0,3},{1,0},{2,1},{3,2},{4,7},{5,4},{6,5},{7,6},{8,11},{9,8},{10,9... | collective-permute-start | bytes 1671176 | tf_op jit(solution)/shard_map/ppermute | solution.py:66
  640.1 52.0 %collective-permute-start.84 = (bf16[256,1024]{0,1:T(8,128)(2,1)}, bf16[256,1024]{0,1:T(8,128)(2,1)}, u32[]{:S(2)}, u32[]{:S(2)}) collective-permute-start(bf16[256,1024]{0,1:T(8,128)(2,1)} %get-tuple-element.125), channel_id=1, source_target_pairs={{0,64},{1,65},{2,66},{3,67},{12,76},{13,77},{14,78},{15,79},{16,80... | collective-permute-start | bytes 1572872 | tf_op jit(solution)/shard_map/ppermute | solution.py:66
  641.6 58.0 %collective-permute-start.83 = (bf16[256,1024]{0,1:T(8,128)(2,1)}, bf16[256,1024]{0,1:T(8,128)(2,1)}, u32[]{:S(2)}, u32[]{:S(2)}) collective-permute-start(bf16[256,1024]{0,1:T(8,128)(2,1)} %get-tuple-element.125), channel_id=1, source_target_pairs={{4,64},{5,65},{6,66},{7,67},{8,76},{9,77},{10,78},{11,79},{20,80},... | collective-permute-start | bytes 1572872 | tf_op jit(solution)/shard_map/ppermute | solution.py:66
  672.2 40.1 %collective-permute-start.80 = (bf16[256,1024]{0,1:T(8,128)(2,1)S(1)}, bf16[256,1024]{0,1:T(8,128)(2,1)S(1)}, u32[]{:S(2)}, u32[]{:S(2)}) collective-permute-start(bf16[256,1024]{0,1:T(8,128)(2,1)S(1)} %get-tuple-element.127), channel_id=1, source_target_pairs={{0,64},{1,65},{2,66},{3,67},{12,76},{13,77},{14,78},{15,79},{16,80... | collective-permute-start | bytes 1572872 | tf_op jit(solution)/shard_map/ppermute | solution.py:66
  672.9 41.9 %collective-permute-start.79 = (bf16[256,1024]{0,1:T(8,128)(2,1)S(1)}, bf16[256,1024]{0,1:T(8,128)(2,1)S(1)}, u32[]{:S(2)}, u32[]{:S(2)}) collective-permute-start(bf16[256,1024]{0,1:T(8,128)(2,1)S(1)} %get-tuple-element.127), channel_id=1, source_target_pairs={{4,64},{5,65},{6,66},{7,67},{8,76},{9,77},{10,78},{11,79},{20,80},... | collective-permute-start | bytes 1572872 | tf_op jit(solution)/shard_map/ppermute | solution.py:66
  691.4 28.3 %collective-permute-start.76 = (bf16[256,1024]{0,1:T(8,128)(2,1)S(1)}, bf16[256,1024]{0,1:T(8,128)(2,1)S(1)}, u32[]{:S(2)}, u32[]{:S(2)}) collective-permute-start(bf16[256,1024]{0,1:T(8,128)(2,1)S(1)} %copy-done.35), channel_id=1, source_target_pairs={{0,64},{1,65},{2,66},{3,67},{12,76},{13,77},{14,78},{15,79},{16,80... | collective-permute-start | bytes 1572872 | tf_op jit(solution)/shard_map/ppermute | solution.py:66
  712.3 29.1 %collective-permute-start.55 = (bf16[136,2048]{1,0:T(8,128)(2,1)}, bf16[136,2048]{1,0:T(8,128)(2,1)}, u32[]{:S(2)}, u32[]{:S(2)}) collective-permute-start(bf16[136,2048]{1,0:T(8,128)(2,1)} %fusion.75), channel_id=1, source_target_pairs={{0,0},{1,1},{2,2},{3,3},{4,8},{5,9},{6,10},{7,11},{8,4},{9,5},{10,... | collective-permute-start | bytes 1671176 | tf_op jit(solution)/shard_map/ppermute | solution.py:66
  (151 other events, 2057.8 us)
Sparse Core Ops, SparseCore 0:
  403.1 21.6 reduce-scatter.7
  432.0 46.7 reduce-scatter.13
  481.1 46.5 reduce-scatter.9
  530.2 46.5 reduce-scatter.11
  636.3 22.2 reduce-scatter.5

commit v2 on v1

v2 whole, which is shorter than its diff:
```python
import jax
import jax.numpy as jnp
from jax import lax
from jax.experimental import pallas as pl
from jax.experimental.pallas import tpu as pltpu
from jax.sharding import PartitionSpec as P

HEAD_DIM = 64
HALF = 128
MASKED = -1e30


EPS = 1e-05
THETA = 500000.0

BOTH = ("dp", "mp")


def place_of(yh, z, c, yl, x):
    return ((yh * 4 + z) * 2 + c) * 8 + yl * 4 + x


def pairs_of(target, sender=lambda yh, z, c, yl, x: True):
    return [
        (place_of(yh, z, c, yl, x), place_of(*target(yh, z, c, yl, x)))
        for yh in range(2)
        for z in range(4)
        for c in range(2)
        for yl in range(2)
        for x in range(4)
        if sender(yh, z, c, yl, x)
    ]


X_UP = pairs_of(lambda yh, z, c, yl, x: (yh, z, c, yl, (x + 1) % 4))
X_DOWN = pairs_of(lambda yh, z, c, yl, x: (yh, z, c, yl, (x + 3) % 4))
X_FAR = pairs_of(lambda yh, z, c, yl, x: (yh, z, c, yl, (x + 2) % 4))
Z_UP = pairs_of(lambda yh, z, c, yl, x: (yh, (z + 1) % 4, c, yl, x))
Z_DOWN = pairs_of(lambda yh, z, c, yl, x: (yh, (z + 3) % 4, c, yl, x))
Z_FAR = pairs_of(lambda yh, z, c, yl, x: (yh, (z + 2) % 4, c, yl, x))
CORE = pairs_of(lambda yh, z, c, yl, x: (yh, z, 1 - c, yl, x))
Y_LOW = pairs_of(lambda yh, z, c, yl, x: (yh, z, c, 1 - yl, x))
Y_HIGH = pairs_of(lambda yh, z, c, yl, x: (1 - yh, z, c, 1 - yl, x))
Y_FAR = pairs_of(lambda yh, z, c, yl, x: (1 - yh, z, c, yl, x))
TURN = pairs_of(lambda yh, z, c, yl, x: (yh, z, yl, c, x))
NATIVE = lambda yh, z, c, yl, x: c == yl
FOREIGN = lambda yh, z, c, yl, x: c != yl
FOREIGN_LOW = pairs_of(lambda yh, z, c, yl, x: (yh, z, c, 1 - yl, x), FOREIGN)
FOREIGN_HIGH = pairs_of(lambda yh, z, c, yl, x: (1 - yh, z, c, 1 - yl, x), FOREIGN)
NATIVE_FAR = pairs_of(lambda yh, z, c, yl, x: (1 - yh, z, c, yl, x), NATIVE)
NATIVE_CORE = pairs_of(lambda yh, z, c, yl, x: (yh, z, 1 - c, yl, x), NATIVE)
WEIGHT_LOW = pairs_of(
    lambda yh, z, c, yl, x: (yh, z, c, 1 - yl, x) if c == yl else (yh, z, 1 - c, yl, x)
)
WEIGHT_HIGH = pairs_of(
    lambda yh, z, c, yl, x: (1 - yh, z, c, 1 - yl, x) if c == yl else (yh, z, 1 - c, yl, x)
)
Z_GROUPS = [
    [place_of(yh, z, c, yl, x) for z in range(4)]
    for yh in range(2)
    for c in range(2)
    for yl in range(2)
    for x in range(4)
]


def send(values, pairs):
    return lax.ppermute(values, BOTH, pairs)


def gather(rows):
    own = jnp.concatenate([rows, send(rows, X_DOWN), send(rows, X_FAR), send(rows, X_UP)])
    return (own, send(own, CORE))


def scatter(own, other):
    total = (own.astype(jnp.float32) + send(other, CORE).astype(jnp.float32)).astype(jnp.bfloat16)
    rows = total.shape[0] // 4
    part = [total[k * rows : (k + 1) * rows] for k in range(4)]
    one, two, three = send(part[1], X_UP), send(part[2], X_FAR), send(part[3], X_DOWN)
    return (part[0].astype(jnp.float32) + one.astype(jnp.float32)) + (
        two.astype(jnp.float32) + three.astype(jnp.float32)
    )


def in_order(values, core, x):
    half = values.shape[0] // 2
    start = (4 - x) % 4 * (half // 4)
    pair = jnp.stack([values[:half], values[half:]])
    pair = lax.dynamic_slice_in_dim(jnp.concatenate([pair, pair], axis=1), start, half, axis=1)
    return jnp.where(core == 0, pair, pair[::-1]).reshape(values.shape)


def from_order(values, core, x):
    half = values.shape[0] // 2
    pair = values.reshape(2, half, -1)
    pair = jnp.where(core == 0, pair, pair[::-1])
    pair = lax.dynamic_slice_in_dim(
        jnp.concatenate([pair, pair], axis=1), x * (half // 4), half, axis=1
    )
    return pair.reshape(values.shape)


def sum_groups(grad, yh, core, native):
    width = grad.shape[-1]
    kept = lax.psum_scatter(
        grad.reshape(-1, width),
        BOTH,
        scatter_dimension=0,
        tiled=True,
        axis_index_groups=Z_GROUPS,
    ).reshape(2, -1, width)
    near = jnp.where(yh == 0, kept[0], kept[1])
    far = jnp.where(yh == 0, kept[1], kept[0])
    low = send(near, FOREIGN_LOW)
    high = send(far, FOREIGN_HIGH)
    across = send(far, NATIVE_FAR)
    total = (near.astype(jnp.float32) + low.astype(jnp.float32)) + (
        high.astype(jnp.float32) + across.astype(jnp.float32)
    )
    rows = total.shape[0] // 2
    mine = jnp.where(core == 0, total[:rows], total[rows:])
    theirs = jnp.where(core == 0, total[rows:], total[:rows])
    passed = send(theirs.astype(jnp.bfloat16), NATIVE_CORE).astype(jnp.float32)
    return jnp.where(native, mine, passed)


def inverse_freq(head_width):
    indices = jnp.arange(head_width // 2, dtype=jnp.float32)
    base_freq = jnp.exp(-jnp.log(THETA) * 2.0 * indices / head_width)
    wavelength = 2.0 * jnp.pi / base_freq
    smooth = (8192.0 / wavelength - 1.0) / 3.0
    blended = (1.0 - smooth) * base_freq / 32.0 + smooth * base_freq
    return jnp.where(
        wavelength < 2048.0, base_freq, jnp.where(wavelength > 8192.0, base_freq / 32.0, blended)
    )


VMEM = pl.BlockSpec(memory_space=pltpu.VMEM)


def params(mib):
    return pltpu.CompilerParams(vmem_limit_bytes=mib * 1024 * 1024)


def dot(left, right, left_dim=1, right_dim=0):
    return lax.dot_general(
        left, right, (((left_dim,), (right_dim,)), ((), ())), preferred_element_type=jnp.float32
    )


def stacked(block):
    return jnp.concatenate(
        [block[:, h * HEAD_DIM : (h + 1) * HEAD_DIM] for h in range(4)], axis=0
    )


def unstacked(block):
    rows = block.shape[0] // 4
    return jnp.concatenate([block[h * rows : (h + 1) * rows] for h in range(4)], axis=1)


def as_row(column):
    return jnp.transpose(jnp.broadcast_to(column, (column.shape[0], 128)))[:8]


def turned(values, cos_rows, sin_rows):
    half = HEAD_DIM // 2
    swapped = jnp.concatenate([values[:, half:], values[:, :half]], axis=1)
    return values * cos_rows + swapped * sin_rows


def short_forward_kernel(qkv_ref, start_ref, attn_ref, lse_ref):
    blocks = attn_ref.shape[0] // HALF
    for i in range(blocks):
        rows = pl.ds((i + 2) * HALF, HALF)
        keys = (i + 1) * HALF
        q = stacked(qkv_ref[rows, :256]) * jnp.bfloat16(HEAD_DIM**-0.5)
        k = qkv_ref[pl.ds(2 * HALF, keys), 256:320]
        v = qkv_ref[pl.ds(2 * HALF, keys), 320:384]
        scores = dot(q, k, 1, 1)
        column = lax.broadcasted_iota(jnp.int32, (HALF, keys), 1)
        row = lax.broadcasted_iota(jnp.int32, (HALF, keys), 0) + i * HALF
        seen = (column <= row) & (column >= start_ref[pl.ds(i * HALF, HALF), :1])
        scores = jnp.where(jnp.concatenate([seen] * 4, axis=0), scores, MASKED)
        top = jnp.max(scores, axis=1, keepdims=True)
        weights = jnp.exp(scores - top)
        total = jnp.sum(weights, axis=1, keepdims=True)
        out = dot(weights.astype(jnp.bfloat16), v) / total
        attn_ref[pl.ds(i * HALF, HALF), :] = unstacked(out).astype(jnp.bfloat16)
        lse_ref[i] = as_row(top + jnp.log(total))


def short_forward(qkv, start):
    rows = qkv.shape[0] - 2 * HALF
    blocks = rows // HALF
    return pl.pallas_call(
        short_forward_kernel,
        out_shape=(
            jax.ShapeDtypeStruct((rows, 256), jnp.bfloat16),
            jax.ShapeDtypeStruct((blocks, 8, 4 * HALF), jnp.float32),
        ),
        in_specs=[VMEM] * 2,
        out_specs=(VMEM,) * 2,
        compiler_params=params(40),
        name="short_forward",
    )(qkv, start)


CHUNK = 1024


def long_forward_kernel(q_ref, far_ref, far_pos_ref, pos_ref, attn_ref, lse_ref):
    for half in range(2):
        rows = pl.ds(half * HALF, HALF)
        q = stacked(q_ref[rows, :256]) * jnp.bfloat16(HEAD_DIM**-0.5)
        position = jnp.concatenate([pos_ref[rows, :1]] * 4, axis=0)

        def step(i, carry):
            top, total, out = carry
            keys = pl.ds(pl.multiple_of(i * CHUNK, CHUNK), CHUNK)
            block = far_ref[keys, :]
            scores = dot(q, block[:, :HEAD_DIM], 1, 1)
            seen = far_pos_ref[i, :1] <= position
            scores = jnp.where(seen, scores, MASKED)
            now = jnp.maximum(top, jnp.max(scores, axis=1, keepdims=True))
            weights = jnp.where(seen, jnp.exp(scores - now), 0.0)
            scale = jnp.exp(top - now)
            total = total * scale + jnp.sum(weights, axis=1, keepdims=True)
            out = out * scale + dot(weights.astype(jnp.bfloat16), block[:, HEAD_DIM:])
            return now, total, out

        first = (
            jnp.full((4 * HALF, 1), MASKED, jnp.float32),
            jnp.zeros((4 * HALF, 1), jnp.float32),
            jnp.zeros((4 * HALF, HEAD_DIM), jnp.float32),
        )
        top, total, out = lax.fori_loop(0, far_ref.shape[0] // CHUNK, step, first)
        attn_ref[rows, :] = unstacked(out / total).astype(jnp.bfloat16)
        lse_ref[half] = as_row(top + jnp.log(total))


def long_forward(q, far, far_pos, pos):
    return pl.pallas_call(
        long_forward_kernel,
        out_shape=(
            jax.ShapeDtypeStruct((2 * HALF, 256), jnp.bfloat16),
            jax.ShapeDtypeStruct((2, 8, 4 * HALF), jnp.float32),
        ),
        in_specs=[VMEM] * 4,
        out_specs=(VMEM,) * 2,
        compiler_params=params(40),
        name="long_forward",
    )(q, far, far_pos, pos)


def grad_terms(q, grad, k, v, seen, lse, delta):
    weights = jnp.where(seen, jnp.exp(dot(k, q, 1, 1) - lse), 0.0)
    grad_scores = (weights * (dot(v, grad, 1, 1) - delta)).astype(jnp.bfloat16)
    return (
        dot(grad_scores, k, 0, 0),
        dot(grad_scores, q),
        dot(weights.astype(jnp.bfloat16), grad),
    )


def row_product(left, right):
    return as_row(
        jnp.sum(left.astype(jnp.float32) * right.astype(jnp.float32), axis=1, keepdims=True)
    )[:1]


def short_backward_kernel(
    qkv_ref, start_ref, attn_ref, grad_ref, lse_ref, cos_ref, sin_ref, out_ref, dk_ref, dv_ref
):
    blocks = attn_ref.shape[0] // HALF
    scale = HEAD_DIM**-0.5
    dk_ref[...] = jnp.zeros_like(dk_ref)
    dv_ref[...] = jnp.zeros_like(dv_ref)
    for i in range(blocks):
        rows = pl.ds((i + 2) * HALF, HALF)
        keys = (i + 1) * HALF
        q = stacked(qkv_ref[rows, :256]) * jnp.bfloat16(scale)
        k = qkv_ref[pl.ds(2 * HALF, keys), 256:320]
        v = qkv_ref[pl.ds(2 * HALF, keys), 320:384]
        grad = stacked(grad_ref[rows, :])
        delta = row_product(grad, stacked(attn_ref[pl.ds(i * HALF, HALF), :]))
        key = lax.broadcasted_iota(jnp.int32, (keys, HALF), 0)
        query = lax.broadcasted_iota(jnp.int32, (keys, HALF), 1) + i * HALF
        seen = (key <= query) & (key >= start_ref[:1, pl.ds(i * HALF, HALF)])
        dq, dk, dv = grad_terms(
            q, grad, k, v, jnp.concatenate([seen] * 4, axis=1), lse_ref[i, :1], delta
        )
        cos_rows = cos_ref[rows, :]
        sin_rows = sin_ref[rows, :]
        dq = turned(
            dq * scale,
            jnp.concatenate([cos_rows] * 4, axis=0),
            jnp.concatenate([-sin_rows] * 4, axis=0),
        )
        out_ref[pl.ds(i * HALF, HALF), :256] = unstacked(dq).astype(jnp.bfloat16)
        dk_ref[pl.ds(0, keys), :] += dk
        dv_ref[pl.ds(0, keys), :] += dv
    rows = pl.ds(2 * HALF, blocks * HALF)
    dk = turned(dk_ref[...], cos_ref[rows, :], -sin_ref[rows, :])
    out_ref[:, 256:] = jnp.concatenate([dk, dv_ref[...]], axis=1).astype(jnp.bfloat16)


def short_backward(qkv, start, attn, grad, lse, cos_rows, sin_rows):
    rows = attn.shape[0]
    return pl.pallas_call(
        short_backward_kernel,
        out_shape=jax.ShapeDtypeStruct((rows, 384), jnp.bfloat16),
        in_specs=[VMEM] * 7,
        out_specs=VMEM,
        scratch_shapes=[pltpu.VMEM((rows, HEAD_DIM), jnp.float32)] * 2,
        compiler_params=params(48),
        name="short_backward",
    )(qkv, start, attn, grad, lse, cos_rows, sin_rows)


BACK_CHUNK = 1024


def long_backward_kernel(
    q_ref, far_ref, far_pos_ref, pos_ref, attn_ref, grad_ref, lse_ref, cos_ref, sin_ref,
    dq_ref, far_grad_ref, acc_ref,
):
    scale = HEAD_DIM**-0.5
    acc_ref[...] = jnp.zeros_like(acc_ref)
    queries = []
    for half in range(2):
        rows = pl.ds(half * HALF, HALF)
        grad = stacked(grad_ref[rows, :])
        queries.append(
            (
                stacked(q_ref[rows, :256]) * jnp.bfloat16(scale),
                grad,
                lse_ref[half, :1],
                row_product(grad, stacked(attn_ref[rows, :])),
                jnp.concatenate([pos_ref[:1, rows]] * 4, axis=1),
            )
        )

    def step(i, carry):
        keys = pl.ds(pl.multiple_of(i * BACK_CHUNK, BACK_CHUNK), BACK_CHUNK)
        block = far_ref[keys, :]
        k, v = block[:, :HEAD_DIM], block[:, HEAD_DIM:]
        sums = []
        for half, (q, grad, lse, delta, position) in enumerate(queries):
            seen = far_pos_ref[keys, :1] <= position
            dq, dk, dv = grad_terms(q, grad, k, v, seen, lse, delta)
            acc_ref[half] += dq
            sums.append((dk, dv))
        far_grad_ref[keys, :] = jnp.concatenate(
            [sums[0][0] + sums[1][0], sums[0][1] + sums[1][1]], axis=1
        ).astype(jnp.bfloat16)
        return carry

    lax.fori_loop(0, far_ref.shape[0] // BACK_CHUNK, step, 0)
    for half in range(2):
        rows = pl.ds(half * HALF, HALF)
        dq = turned(
            acc_ref[half] * scale,
            jnp.concatenate([cos_ref[rows, :]] * 4, axis=0),
            jnp.concatenate([-sin_ref[rows, :]] * 4, axis=0),
        )
        dq_ref[rows, :] = unstacked(dq).astype(jnp.bfloat16)


def long_backward(q, far, far_pos, pos, attn, grad, lse, cos_rows, sin_rows):
    return pl.pallas_call(
        long_backward_kernel,
        out_shape=(
            jax.ShapeDtypeStruct((2 * HALF, 256), jnp.bfloat16),
            jax.ShapeDtypeStruct(far.shape, jnp.bfloat16),
        ),
        in_specs=[VMEM] * 9,
        out_specs=(VMEM,) * 2,
        scratch_shapes=[pltpu.VMEM((2, 4 * HALF, HEAD_DIM), jnp.float32)],
        compiler_params=params(48),
        name="long_backward",
    )(q, far, far_pos, pos, attn, grad, lse, cos_rows, sin_rows)


def weight_grad_kernel(left_ref, right_ref, out_ref):
    out_ref[0, 0] = dot(left_ref[...], right_ref[...], 0, 0).astype(jnp.bfloat16)


def weight_grad(left, right):
    tokens, width = right.shape
    return pl.pallas_call(
        weight_grad_kernel,
        grid=(8,),
        out_shape=jax.ShapeDtypeStruct((4, 2, 256, width), jnp.bfloat16),
        in_specs=[
            pl.BlockSpec((tokens, 256), lambda i: (0, i)),
            pl.BlockSpec((tokens, width), lambda i: (0, 0), pipeline_mode=pl.Buffered(1)),
        ],
        out_specs=pl.BlockSpec((1, 1, 256, width), lambda i: (i % 4, i // 4, 0, 0)),
        compiler_params=params(40),
        name="weight_grad",
    )(left, right)


def mlp_kernel(hidden_ref, grad_act_ref, gate_ref, up_ref, act_ref, both_ref, back_ref):
    hidden = hidden_ref[...]
    gate = dot(hidden, gate_ref[...])
    up = dot(hidden, up_ref[...])
    grad_act = grad_act_ref[...].astype(jnp.float32)
    sig = jax.nn.sigmoid(gate)
    silu = gate * sig
    act_ref[...] = (silu * up).astype(jnp.bfloat16)
    grad_gate = (grad_act * up * sig * (1.0 + gate * (1.0 - sig))).astype(jnp.bfloat16)
    grad_up = (grad_act * silu).astype(jnp.bfloat16)
    width = gate.shape[1]
    both_ref[:, :width] = grad_gate
    both_ref[:, width:] = grad_up
    back_ref[...] = (dot(grad_gate, gate_ref[...], 1, 1) + dot(grad_up, up_ref[...], 1, 1)).astype(
        jnp.bfloat16
    )


def mlp(hidden, grad_act, w_gate, w_up, block=272):
    rows, d = hidden.shape
    width = w_gate.shape[1]
    return pl.pallas_call(
        mlp_kernel,
        grid=(rows // block,),
        out_shape=(
            jax.ShapeDtypeStruct((rows, width), jnp.bfloat16),
            jax.ShapeDtypeStruct((rows, 2 * width), jnp.bfloat16),
            jax.ShapeDtypeStruct((rows, d), jnp.bfloat16),
        ),
        in_specs=[
            pl.BlockSpec((block, d), lambda i: (i, 0)),
            pl.BlockSpec((block, width), lambda i: (i, 0)),
            pl.BlockSpec((d, width), lambda i: (0, 0), pipeline_mode=pl.Buffered(1)),
            pl.BlockSpec((d, width), lambda i: (0, 0), pipeline_mode=pl.Buffered(1)),
        ],
        out_specs=(
            pl.BlockSpec((block, width), lambda i: (i, 0)),
            pl.BlockSpec((block, 2 * width), lambda i: (i, 0)),
            pl.BlockSpec((block, d), lambda i: (i, 0)),
        ),
        compiler_params=params(56),
        name="mlp",
    )(hidden, grad_act, w_gate, w_up)


def qkv_kernel(hidden_ref, query_ref, kv_ref, cos_ref, sin_ref, out_ref):
    hidden = hidden_ref[...]
    query = dot(hidden, query_ref[...])
    kv = dot(hidden, kv_ref[...])
    cos_rows, sin_rows = cos_ref[...], sin_ref[...]
    heads = [
        turned(query[:, h * HEAD_DIM : (h + 1) * HEAD_DIM], cos_rows, sin_rows) for h in range(4)
    ]
    heads += [turned(kv[:, :HEAD_DIM], cos_rows, sin_rows), kv[:, HEAD_DIM:]]
    out_ref[...] = jnp.concatenate(heads, axis=1).astype(jnp.bfloat16)


def project_qkv(hidden, w_query, w_key_value, cos_rows, sin_rows, block=272):
    rows, d = hidden.shape
    return pl.pallas_call(
        qkv_kernel,
        grid=(rows // block,),
        out_shape=jax.ShapeDtypeStruct((rows, 384), jnp.bfloat16),
        in_specs=[
            pl.BlockSpec((block, d), lambda i: (i, 0)),
            pl.BlockSpec((d, 256), lambda i: (0, 0), pipeline_mode=pl.Buffered(1)),
            pl.BlockSpec((d, 128), lambda i: (0, 0), pipeline_mode=pl.Buffered(1)),
            pl.BlockSpec((block, HEAD_DIM), lambda i: (i, 0)),
            pl.BlockSpec((block, HEAD_DIM), lambda i: (i, 0)),
        ],
        out_specs=pl.BlockSpec((block, 384), lambda i: (i, 0)),
        compiler_params=params(32),
        name="project_qkv",
    )(hidden, w_query, w_key_value, cos_rows, sin_rows)


def norm_back(grad_in, unit_rows, inv_rms, gain):
    scaled = grad_in * gain
    return inv_rms * (scaled - unit_rows * jnp.mean(scaled * unit_rows, axis=-1, keepdims=True))


def all_sum(values):
    for group in ((CORE,), (X_UP, X_DOWN, X_FAR), (Z_UP, Z_DOWN, Z_FAR), (Y_LOW, Y_HIGH, Y_FAR)):
        values = sum([send(values, pairs) for pairs in group], values)
    return values


def local(
    tokens,
    lengths,
    place,
    attn_gain,
    w_query,
    w_key,
    w_value,
    w_out,
    mlp_gain,
    w_gate,
    w_up,
    w_down,
    out_grad,
):
    rows = tokens.shape[0]
    group_rows = rows * 8
    half_rows = rows * 4
    long_rows = 2 * HALF
    padded_rows = -(-group_rows // HALF) * HALF
    dp_index, mp_index = lax.axis_index("dp"), lax.axis_index("mp")
    yh, z, core = dp_index // 8, dp_index // 2 % 4, dp_index % 2
    yl, x = mp_index // 4, mp_index % 4
    native = core == yl

    tokens = send(tokens, TURN)
    lengths = send(lengths, TURN)[0]
    w_key_value = send(jnp.concatenate([w_key, w_value], axis=1), WEIGHT_HIGH)
    w_query = send(w_query, WEIGHT_LOW)
    w_out = send(w_out, WEIGHT_HIGH)
    w_gate = send(w_gate, WEIGHT_LOW)
    w_up = send(w_up, WEIGHT_HIGH)
    w_down = send(w_down, WEIGHT_LOW)
    out_grad = send(out_grad, TURN)

    group = (yh * 4 + z) * 2 + yl
    half_ids = jnp.arange(place.shape[0], dtype=jnp.int32)

    def place_at(index):
        return jnp.sum(jnp.where(half_ids == index[..., None], place, 0), axis=-1)

    def position_of(row):
        packed = row - long_rows
        first, second = lengths[0], lengths[0] + lengths[1]
        start = jnp.where(packed >= second, second, jnp.where(packed >= first, first, 0))
        start = jnp.where(row >= group_rows, packed, start)
        own = jnp.where(row < HALF, place_at(2 * group), place_at(2 * group + 1))
        return jnp.where(row < long_rows, own * HALF + row % HALF, packed - start), start

    def tables(position):
        angles = position.astype(jnp.float32)[:, None] * inverse_freq(HEAD_DIM)[None, :]
        cos_rows, sin_rows = jnp.cos(angles), jnp.sin(angles)
        return (
            jnp.concatenate([cos_rows, cos_rows], axis=1),
            jnp.concatenate([-sin_rows, sin_rows], axis=1),
        )

    ordered_rows = jnp.arange(padded_rows, dtype=jnp.int32)
    ordered_pos, ordered_start = position_of(ordered_rows)
    cos_ordered, sin_ordered = tables(ordered_pos)
    index = jnp.arange(group_rows, dtype=jnp.int32)
    shard = jnp.where(index < half_rows, core, 1 - core) * 4 + (x + index % half_rows // rows) % 4
    cos_gathered, sin_gathered = tables(position_of(shard * rows + index % rows)[0])
    starts = ordered_start[long_rows:]
    start_column = jnp.broadcast_to(starts[:, None], (starts.shape[0], 128))
    start_row = jnp.broadcast_to(starts[None, :], (8, starts.shape[0]))
    long_pos = ordered_pos[:long_rows]
    pos_column = jnp.broadcast_to(long_pos[:, None], (long_rows, 128))
    pos_row = jnp.broadcast_to(long_pos[None, :], (8, long_rows))
    step = jnp.arange(16, dtype=jnp.int32)
    far_yh = jnp.where(step // 4 >= 2, 1 - yh, yh)
    far_yl = jnp.where((step // 4 == 1) | (step // 4 == 2), 1 - yl, yl)
    far_group = (far_yh * 4 + (z + step) % 4) * 2 + far_yl
    far_half = place_at(2 * far_group[:, None] + jnp.arange(2, dtype=jnp.int32)[None, :])
    far_pos = (
        far_half.reshape(-1, 1) * HALF + jnp.arange(HALF, dtype=jnp.int32)[None, :]
    ).reshape(-1)
    far_row = jnp.broadcast_to(far_pos.reshape(-1, 1, CHUNK), (far_pos.shape[0] // CHUNK, 8, CHUNK))
    far_column = jnp.broadcast_to(far_pos[:, None], (far_pos.shape[0], 128))

    residual = tokens.astype(jnp.float32)
    inv_one = lax.rsqrt(jnp.mean(residual * residual, axis=-1, keepdims=True) + EPS)
    unit_one = residual * inv_one
    hidden_one = jnp.concatenate(gather((unit_one * attn_gain).astype(jnp.bfloat16)))
    qkv = project_qkv(hidden_one, w_query, w_key_value, cos_gathered, sin_gathered)
    qkv = jnp.pad(in_order(qkv, core, x), ((0, padded_rows - group_rows), (0, 0)))
    near_rows = qkv[:long_rows, 256:]
    ring_rows = jnp.concatenate(
        [near_rows, send(near_rows, Z_DOWN), send(near_rows, Z_FAR), send(near_rows, Z_UP)]
    )
    far_rows = jnp.concatenate(
        [ring_rows, send(ring_rows, Y_LOW), send(ring_rows, Y_HIGH), send(ring_rows, Y_FAR)]
    )
    long_q = qkv[:long_rows]
    short_attn, short_lse = short_forward(qkv, start_column)
    long_attn, long_lse = long_forward(long_q, far_rows, far_row, pos_column)
    attn_rows = from_order(
        jnp.concatenate([long_attn, short_attn[: group_rows - long_rows]]), core, x
    )

    def project(left, right):
        return jnp.dot(left, right, preferred_element_type=jnp.float32).astype(jnp.bfloat16)

    mixed = residual + scatter(
        project(attn_rows[:half_rows], w_out), project(attn_rows[half_rows:], w_out)
    )
    inv_two = lax.rsqrt(jnp.mean(mixed * mixed, axis=-1, keepdims=True) + EPS)
    unit_two = mixed * inv_two
    grad_rows = jnp.concatenate(gather(out_grad))
    grad_act = dot(grad_rows, w_down, 1, 1).astype(jnp.bfloat16)
    hidden_two = jnp.concatenate(gather((unit_two * mlp_gain).astype(jnp.bfloat16)))

    act, grad_both, grad_hidden = mlp(hidden_two, grad_act, w_gate, w_up)
    grad_two = scatter(grad_hidden[:half_rows], grad_hidden[half_rows:])
    down_sum = sum_groups(weight_grad(grad_rows, act), yh, core, native).T
    both_sum = sum_groups(weight_grad(hidden_two, grad_both), yh, core, native)
    ff = act.shape[1]
    down_rows = project(act, w_down)
    output = mixed + scatter(down_rows[:half_rows], down_rows[half_rows:])
    output = send(output.astype(jnp.bfloat16), TURN)

    grad_mixed = out_grad.astype(jnp.float32) + norm_back(grad_two, unit_two, inv_two, mlp_gain)
    mixed_grad_rows = jnp.concatenate(gather(grad_mixed.astype(jnp.bfloat16)))
    mlp_gain_part = jnp.sum(grad_two * unit_two, axis=0)
    grad_attn = in_order(dot(mixed_grad_rows, w_out, 1, 1).astype(jnp.bfloat16), core, x)
    grad_attn = jnp.pad(grad_attn, ((0, padded_rows - group_rows), (0, 0)))
    long_dq, far_terms = long_backward(
        long_q,
        far_rows,
        far_column,
        pos_row,
        long_attn,
        grad_attn[:long_rows],
        long_lse,
        cos_ordered[:long_rows],
        sin_ordered[:long_rows],
    )
    ring = far_terms.reshape(4, 4 * long_rows, -1)
    ring_terms = (
        (ring[0].astype(jnp.float32) + send(ring[1], Y_LOW).astype(jnp.float32))
        + (send(ring[2], Y_HIGH).astype(jnp.float32) + send(ring[3], Y_FAR).astype(jnp.float32))
    ).astype(jnp.bfloat16)
    near = ring_terms.reshape(4, long_rows, -1)
    far_grads = (near[0].astype(jnp.float32) + send(near[1], Z_UP).astype(jnp.float32)) + (
        send(near[2], Z_FAR).astype(jnp.float32) + send(near[3], Z_DOWN).astype(jnp.float32)
    )
    short_low = short_backward(
        qkv, start_row, short_attn, grad_attn, short_lse, cos_ordered, sin_ordered
    )
    long_dk = turned(far_grads[:, :HEAD_DIM], cos_ordered[:long_rows], -sin_ordered[:long_rows])
    long_low = jnp.concatenate(
        [
            long_dq,
            long_dk.astype(jnp.bfloat16),
            far_grads[:, HEAD_DIM:].astype(jnp.bfloat16),
        ],
        axis=1,
    )
    low_rows = from_order(
        jnp.concatenate([long_low, short_low[: group_rows - long_rows]]), core, x
    )
    grad_hidden = (
        dot(low_rows[:, :256], w_query, 1, 1) + dot(low_rows[:, 256:], w_key_value, 1, 1)
    ).astype(jnp.bfloat16)
    grad_one = scatter(grad_hidden[:half_rows], grad_hidden[half_rows:])
    out_sum = sum_groups(weight_grad(mixed_grad_rows, attn_rows), yh, core, native).T
    qkv_sum = sum_groups(weight_grad(hidden_one, low_rows), yh, core, native)
    attn_gain_part = jnp.sum(grad_one * unit_one, axis=0)
    grad_tokens = grad_mixed + norm_back(grad_one, unit_one, inv_one, attn_gain)
    grad_tokens = send(grad_tokens.astype(jnp.bfloat16), TURN)
    gains = all_sum(jnp.stack([attn_gain_part, mlp_gain_part]))
    return (
        output,
        grad_tokens,
        gains[0],
        qkv_sum[:, :256],
        qkv_sum[:, 256:320],
        qkv_sum[:, 320:],
        out_sum,
        gains[1],
        both_sum[:, :ff],
        both_sum[:, ff:],
        down_sum,
    )


def solution(mesh):
    placed = (
        P(("dp", "mp"), None),
        P("dp", None),
        P(),
        P(),
        P(None, "mp"),
        P(None, "mp"),
        P(None, "mp"),
        P("mp", None),
        P(),
        P(None, "mp"),
        P(None, "mp"),
        P("mp", None),
        P(("dp", "mp"), None),
    )
    return jax.shard_map(
        local,
        mesh=mesh,
        in_specs=placed,
        out_specs=(
            P(("dp", "mp"), None),
            P(("dp", "mp"), None),
            P(),
            P("dp", "mp"),
            P("dp", "mp"),
            P("dp", "mp"),
            P("mp", "dp"),
            P(),
            P("dp", "mp"),
            P("dp", "mp"),
            P("mp", "dp"),
        ),
        check_vma=False,
    )
```

time: 764 us -> 628 us (0.82)
  matrix products: 175 us -> 28.5 us
  Pallas kernels: 0 us -> 98.5 us
  other arithmetic: 94.7 us -> 48.9 us
  local copies, waits for them, and re-layouts: 96.5 us -> 51.3 us
  waiting for transfers between devices: 237 us -> 251 us
  starting transfers between devices: 135 us -> 123 us
    dot_general x28 -> x4, matrix products: 165 us -> 16.8 us  [dot(): lax.dot_general(left, right, (((left_dim,), (right_dim,)), ((), ())), pre...]
    pallas_call x0 -> x10, Pallas kernels: none -> 98.5 us  [the longest x4 30.5 us: weight_grad(): pl.pallas_call(weight_grad_kernel, grid=(8,), out_shape=jax.ShapeDtypeStr...]
    transpose x5 -> x0, local copies, waits for them, and re-layouts: 40.1 us -> none  [sum_groups(): grad.reshape(2, 4, 2, -1, width).transpose(1, 0, 2, 3, 4).reshape(-1, width)]
    unnamed x20 -> x3, other arithmetic: 22.4 us -> 2.9 us
    reshape x5 -> x3, local copies, waits for them, and re-layouts: 29.1 us -> 10.5 us  [sum_groups(): grad.reshape(-1, width)]
    another operation x8 -> x0, other arithmetic: 18 us -> none
    ppermute x86 -> x81, waiting for transfers between devices: 237 us -> 251 us  [send(): return lax.ppermute(values, BOTH, pairs)]
    ppermute x86 -> x81, starting transfers between devices: 135 us -> 123 us  [send(): return lax.ppermute(values, BOTH, pairs)]
  transfers between devices with their start and end apart: 91 -> 85, of which waited for: 35 -> 36; matrix products, arithmetic and copies ran while one was open for 43% -> 14% of each run, Pallas kernels for 0% -> 11%
where the time goes in v2:
time: 628 us; the launch traced here: 619 us
  waiting for transfers between devices  251 us (40%)
  starting transfers between devices  123 us (20%)
  Pallas kernels  98.5 us (16%)
  local copies, waits for them, and re-layouts  51.3 us (8%)
  other arithmetic  48.9 us (8%)
  matrix products  28.5 us (5%)
  between operations  17.3 us (3%)
    ppermute x81, waiting for transfers between devices, send(): return lax.ppermute(values, BOTH, pairs)  251 us
    ppermute x81, starting transfers between devices, send(): return lax.ppermute(values, BOTH, pairs)  123 us
    pallas_call x4, Pallas kernels, weight_grad(): pl.pallas_call(weight_grad_kernel, grid=(8,), out_shape=jax.ShapeDtypeStr...  30.5 us
    unnamed x148, local copies, waits for them, and re-layouts  29.7 us
    pallas_call x1, Pallas kernels, mlp(): pl.pallas_call(mlp_kernel, grid=(rows // block,), out_shape=(jax.ShapeDty...  25.5 us
    dot_general x4, matrix products, dot(): lax.dot_general(left, right, (((left_dim,), (right_dim,)), ((), ())), pre...  16.8 us
    pallas_call x1, Pallas kernels, long_backward(): pl.pallas_call(long_backward_kernel, out_shape=(jax.ShapeDtypeStruct((2 *...  14.4 us
  transfers between devices with their start and end apart: 85, of which 36 were waited for; matrix products, arithmetic and copies ran while one was open for 14% of the time, Pallas kernels for 11%

profile of v2, /device:TPU:1, one launch (start us, length us, event | category | flops | bytes accessed | tf_op | source)
XLA Modules:
  0.0 619.0 jit_solution(15183548054482289749)
XLA Ops:
  27.9 21.5 %collective-permute-done.1 = bf16[136,2048]{1,0:T(8,128)(2,1)S(1)} collective-permute-done((bf16[136,2048]{1,0:T(8,128)(2,1)S(1)}, bf16[136,2048]{1,0:T(8,128)(2,1)S(1)}, u32[]{:S(2)}, u32[]{:S(2)}) %collective-permute-start.1) | collective-permute-done | bytes 557088 | tf_op jit(solution)/shard_map/ppermute | solution.py:68
  96.8 11.9 %long_forward.1 = (bf16[256,256]{1,0:T(8,128)(2,1)S(1)}, f32[2,8,512]{2,1,0:T(8,128)S(1)}) custom-call(bf16[256,384]{1,0:T(8,128)(2,1)S(1)} %slice.360.q_ref, bf16[4096,128]{1,0:T(8,128)(2,1)S(1)} %constant_dynamic-update-slice_fusion.5.far_ref, s32[4,8,1024]{2,1,0:T(8,128)S(1)} %broadcast_in_dim.129.far_pos_ref, s32[256,128]{1,0:T(8,128)S(1)} %broadcast_in_dim.132.pos_ref), custom_call_target="tpu_custom_call" | custom-call | tf_op jit(solution)/shard_map/long_forward/pallas_call | solution.py:244
  134.4 12.2 %collective-permute-done.17 = bf16[136,2048]{1,0:T(8,128)(2,1)S(1)} collective-permute-done((bf16[136,2048]{1,0:T(8,128)(2,1)S(1)}, bf16[136,2048]{1,0:T(8,128)(2,1)S(1)}, u32[]{:S(2)}, u32[]{:S(2)}) %collective-permute-start.17) | collective-permute-done | bytes 557088 | tf_op jit(solution)/shard_map/ppermute | solution.py:68
  151.5 7.0 %collective-permute-done.24 = bf16[136,2048]{1,0:T(8,128)(2,1)S(1)} collective-permute-done((bf16[136,2048]{1,0:T(8,128)(2,1)S(1)}, bf16[136,2048]{1,0:T(8,128)(2,1)S(1)}, u32[]{:S(2)}, u32[]{:S(2)}) %collective-permute-start.24) | collective-permute-done | bytes 557088 | tf_op jit(solution)/shard_map/ppermute | solution.py:68
  158.6 12.4 %collective-permute-done.26 = bf16[136,2048]{1,0:T(8,128)(2,1)S(1)} collective-permute-done((bf16[136,2048]{1,0:T(8,128)(2,1)S(1)}, bf16[136,2048]{1,0:T(8,128)(2,1)S(1)}, u32[]{:S(2)}, u32[]{:S(2)}) %collective-permute-start.26) | collective-permute-done | bytes 557088 | tf_op jit(solution)/shard_map/ppermute | solution.py:68
  172.1 10.4 %collective-permute-done.19 = bf16[136,2048]{1,0:T(8,128)(2,1)S(1)} collective-permute-done((bf16[136,2048]{1,0:T(8,128)(2,1)S(1)}, bf16[136,2048]{1,0:T(8,128)(2,1)S(1)}, u32[]{:S(2)}, u32[]{:S(2)}) %collective-permute-start.19) | collective-permute-done | bytes 557088 | tf_op jit(solution)/shard_map/ppermute | solution.py:68
  187.4 7.1 %collective-permute-start.21 = (bf16[136,2048]{1,0:T(8,128)(2,1)S(1)}, bf16[136,2048]{1,0:T(8,128)(2,1)S(1)}, u32[]{:S(2)}, u32[]{:S(2)}) collective-permute-start(bf16[136,2048]{1,0:T(8,128)(2,1)S(1)} %get-tuple-element.83), channel_id=1, source_target_pairs={{0,1},{1,2},{2,3},{3,0},{4,5},{5,6},{6,7},{7,4},{8,9},{9,10},{10,1... | collective-permute-start | bytes 1671176 | tf_op jit(solution)/shard_map/ppermute | solution.py:68
  194.6 13.8 %collective-permute-done.21 = bf16[136,2048]{1,0:T(8,128)(2,1)S(1)} collective-permute-done((bf16[136,2048]{1,0:T(8,128)(2,1)S(1)}, bf16[136,2048]{1,0:T(8,128)(2,1)S(1)}, u32[]{:S(2)}, u32[]{:S(2)}) %collective-permute-start.21) | collective-permute-done | bytes 557088 | tf_op jit(solution)/shard_map/ppermute | solution.py:68
  211.3 9.8 %convolution_convert_fusion.1.grad_act_ref = bf16[1088,1024]{1,0:T(8,128)(2,1)} fusion(bf16[1088,2048]{1,0:T(8,128)(2,1)S(1)} %constant_dynamic-update-slice_fusion.17.left_ref, bf16[1024,2048]{1,0:T(8,128)(2,1)} %collective-permute-done.28), kind=kOutput, calls=%fused_computation.7 | convolution fusion | flops 4564516864 | bytes 10878976 | tf_op jit(solution)/shard_map/dot_general | solution.py:147
  221.4 10.0 %collective-permute-done.30.up_ref = bf16[2048,1024]{1,0:T(8,128)(2,1)} collective-permute-done((bf16[2048,1024]{1,0:T(8,128)(2,1)}, bf16[2048,1024]{1,0:T(8,128)(2,1)}, u32[]{:S(2)}, u32[]{:S(2)}) %collective-permute-start.30) | collective-permute-done | bytes 4194336 | tf_op jit(solution)/shard_map/ppermute | solution.py:68
  231.4 25.5 %mlp.1 = (bf16[1088,1024]{1,0:T(8,128)(2,1)}, bf16[1088,2048]{1,0:T(8,128)(2,1)}, bf16[1088,2048]{1,0:T(8,128)(2,1)}) custom-call(bf16[1088,2048]{1,0:T(8,128)(2,1)} %copy-done, bf16[1088,1024]{1,0:T(8,128)(2,1)} %convolution_convert_fusion.1.grad_act_ref, bf16[2048,1024]{1,0:T(8,128)(2,1)} %collective-permute-done.29.gate_ref, ...), custom_call_target="tpu_custom_call" | custom-call | tf_op jit(solution)/shard_map/mlp/pallas_call | solution.py:427
  256.9 7.7 %convolution_convert_fusion = bf16[1088,2048]{1,0:T(8,128)(2,1)S(1)} fusion(bf16[1088,1024]{1,0:T(8,128)(2,1)} %get-tuple-element.22.right_ref, bf16[1024,2048]{1,0:T(8,128)(2,1)} %collective-permute-done.28), kind=kOutput, calls=%fused_computation.1 | convolution fusion | flops 4565630976 | bytes 10878976 | tf_op jit(solution)/shard_map/dot_general | solution.py:594
  278.5 8.5 %collective-permute-done.32 = bf16[136,2048]{1,0:T(8,128)(2,1)S(1)} collective-permute-done((bf16[136,2048]{1,0:T(8,128)(2,1)S(1)}, bf16[136,2048]{1,0:T(8,128)(2,1)S(1)}, u32[]{:S(2)}, u32[]{:S(2)}) %collective-permute-start.32) | collective-permute-done | bytes 557088 | tf_op jit(solution)/shard_map/ppermute | solution.py:68
  288.2 11.7 %collective-permute-done.33 = bf16[136,2048]{1,0:T(8,128)(2,1)S(1)} collective-permute-done((bf16[136,2048]{1,0:T(8,128)(2,1)S(1)}, bf16[136,2048]{1,0:T(8,128)(2,1)S(1)}, u32[]{:S(2)}, u32[]{:S(2)}) %collective-permute-start.33) | collective-permute-done | bytes 557088 | tf_op jit(solution)/shard_map/ppermute | solution.py:68
  299.9 11.0 %collective-permute-done.37 = bf16[136,2048]{1,0:T(8,128)(2,1)S(1)} collective-permute-done((bf16[136,2048]{1,0:T(8,128)(2,1)S(1)}, bf16[136,2048]{1,0:T(8,128)(2,1)S(1)}, u32[]{:S(2)}, u32[]{:S(2)}) %collective-permute-start.37) | collective-permute-done | bytes 557088 | tf_op jit(solution)/shard_map/ppermute | solution.py:68
  310.9 12.9 %collective-permute-done.38 = bf16[136,2048]{1,0:T(8,128)(2,1)S(1)} collective-permute-done((bf16[136,2048]{1,0:T(8,128)(2,1)S(1)}, bf16[136,2048]{1,0:T(8,128)(2,1)S(1)}, u32[]{:S(2)}, u32[]{:S(2)}) %collective-permute-start.38) | collective-permute-done | bytes 557088 | tf_op jit(solution)/shard_map/ppermute | solution.py:68
  330.7 12.1 %collective-permute-done.40 = bf16[136,2048]{1,0:T(8,128)(2,1)S(1)} collective-permute-done((bf16[136,2048]{1,0:T(8,128)(2,1)S(1)}, bf16[136,2048]{1,0:T(8,128)(2,1)S(1)}, u32[]{:S(2)}, u32[]{:S(2)}) %collective-permute-start.40) | collective-permute-done | bytes 557088 | tf_op jit(solution)/shard_map/ppermute | solution.py:68
  345.1 12.4 %collective-permute-done.42 = bf16[136,2048]{1,0:T(8,128)(2,1)S(1)} collective-permute-done((bf16[136,2048]{1,0:T(8,128)(2,1)S(1)}, bf16[136,2048]{1,0:T(8,128)(2,1)S(1)}, u32[]{:S(2)}, u32[]{:S(2)}) %collective-permute-start.42) | collective-permute-done | bytes 557088 | tf_op jit(solution)/shard_map/ppermute | solution.py:68
  373.9 7.6 %weight_grad.7 = bf16[4,2,256,1024]{3,2,1,0:T(8,128)(2,1)S(1)} custom-call(bf16[1088,2048]{1,0:T(8,128)(2,1)S(1)} %copy-done.7, bf16[1088,1024]{1,0:T(8,128)(2,1)S(1)} %copy-done.11), custom_call_target="tpu_custom_call" | custom-call | tf_op jit(solution)/shard_map/weight_grad/pallas_call | solution.py:392
  394.7 14.2 %weight_grad.6 = bf16[4,2,256,2048]{3,2,1,0:T(8,128)(2,1)} custom-call(bf16[1088,2048]{1,0:T(8,128)(2,1)S(1)} %copy-done.1, bf16[1088,2048]{1,0:T(8,128)(2,1)S(1)} %copy-done.9), custom_call_target="tpu_custom_call" | custom-call | tf_op jit(solution)/shard_map/weight_grad/pallas_call | solution.py:392
  419.5 14.4 %long_backward.1 = (bf16[256,256]{1,0:T(8,128)(2,1)S(1)}, bf16[4096,128]{1,0:T(8,128)(2,1)S(1)}) custom-call(bf16[256,384]{1,0:T(8,128)(2,1)S(1)} %slice.360.q_ref, bf16[4096,128]{1,0:T(8,128)(2,1)S(1)} %constant_dynamic-update-slice_fusion.5.far_ref, s32[4096,128]{1,0:T(8,128)S(1)} %broadcast_in_dim.134.far_pos_ref, ...), custom_call_target="tpu_custom_call" | custom-call | tf_op jit(solution)/shard_map/long_backward/pallas_call | solution.py:372
  454.2 7.7 %short_backward.1 = bf16[896,384]{1,0:T(8,128)(2,1)S(1)} custom-call(bf16[1152,384]{1,0:T(8,128)(2,1)S(1)} %pad.8.qkv_ref, s32[8,896]{1,0:T(8,128)S(1)} %broadcast_in_dim.136.start_ref, bf16[896,256]{1,0:T(8,128)(2,1)S(1)} %copy-done.15, bf16[1152,256]{1,0:T(8,128)(2,1)S(1)} %pad.9.grad_ref, f32[7,8,512]{2,1,0:T(8,128)S(1)} %copy-done.17, ...), custom_call_target="tpu_custom_call" | custom-call | tf_op jit(solution)/shard_map/short_backward/pallas_call | solution.py:311
  507.2 12.7 %collective-permute-done.51 = bf16[136,2048]{1,0:T(8,128)(2,1)S(1)} collective-permute-done((bf16[136,2048]{1,0:T(8,128)(2,1)}, bf16[136,2048]{1,0:T(8,128)(2,1)S(1)}, u32[]{:S(2)}, u32[]{:S(2)}) %collective-permute-start.51) | collective-permute-done | bytes 557088 | tf_op jit(solution)/shard_map/ppermute | solution.py:68
  566.5 18.6 %collective-permute-done.65 = bf16[256,384]{0,1:T(8,128)(2,1)S(1)} collective-permute-done((bf16[256,384]{0,1:T(8,128)(2,1)S(1)}, bf16[256,384]{0,1:T(8,128)(2,1)S(1)}, u32[]{:S(2)}, u32[]{:S(2)}) %collective-permute-start.65) | collective-permute-done | bytes 196640 | tf_op jit(solution)/shard_map/ppermute | solution.py:68
  (432 shorter events, 308.6 us)
Async XLA Ops:
  7.2 468.2 %reduce-scatter.7.cloned.1.call-start = ((), (), s32[]{:S(2)}) async-start(), calls=%async_computation.5 | async-start | bytes 1310720 | tf_op jit(solution)/shard_map/reduce_scatter | solution.py:106
  7.2 48.5 %collective-permute-start.7 = (s32[1,3]{1,0:T(1,128)}, s32[1,3]{1,0:T(1,128)S(1)}, u32[]{:S(2)}, u32[]{:S(2)}) collective-permute-start(s32[1,3]{1,0:T(1,128)} %param.14), channel_id=1, source_target_pairs={{0,0},{1,1},{2,2},{3,3},{4,8},{5,9},{6,10},{7,11},{8,4},{9,5},{10,... | collective-permute-start | bytes 44 | tf_op jit(solution)/shard_map/ppermute | solution.py:68
  16.5 48.1 %collective-permute-start.6 = (bf16[2048,128]{1,0:T(8,128)(2,1)S(1)}, bf16[2048,128]{1,0:T(8,128)(2,1)S(1)}, u32[]{:S(2)}, u32[]{:S(2)}) collective-permute-start(bf16[2048,128]{1,0:T(8,128)(2,1)S(1)} %pad_maximum_fusion.10), channel_id=1, source_target_pairs={{0,68},{1,69},{2,70},{3,71},{4,12},{5,13},{6,14},{7,15},{8,0},{9,1... | collective-permute-start | bytes 1572872 | tf_op jit(solution)/shard_map/ppermute | solution.py:68
  49.5 60.2 %collective-permute-start.14 = (bf16[256,2048]{1,0:T(8,128)(2,1)}, bf16[256,2048]{1,0:T(8,128)(2,1)}, u32[]{:S(2)}, u32[]{:S(2)}) collective-permute-start(bf16[256,2048]{1,0:T(8,128)(2,1)} %param.20), channel_id=1, source_target_pairs={{0,68},{1,69},{2,70},{3,71},{4,12},{5,13},{6,14},{7,15},{8,0},{9,1... | collective-permute-start | bytes 3145736 | tf_op jit(solution)/shard_map/ppermute | solution.py:68
  122.1 89.2 %collective-permute-start.28 = (bf16[1024,2048]{1,0:T(8,128)(2,1)S(1)}, bf16[1024,2048]{1,0:T(8,128)(2,1)}, u32[]{:S(2)}, u32[]{:S(2)}) collective-permute-start(bf16[1024,2048]{1,0:T(8,128)(2,1)S(1)} %copy-done.59), channel_id=1, source_target_pairs={{0,4},{1,5},{2,6},{3,7},{4,12},{5,13},{6,14},{7,15},{8,0},{9,1},{1... | collective-permute-start | bytes 12582920 | tf_op jit(solution)/shard_map/ppermute | solution.py:68
  124.8 33.7 %collective-permute-start.24 = (bf16[136,2048]{1,0:T(8,128)(2,1)S(1)}, bf16[136,2048]{1,0:T(8,128)(2,1)S(1)}, u32[]{:S(2)}, u32[]{:S(2)}) collective-permute-start(bf16[136,2048]{1,0:T(8,128)(2,1)S(1)} %collective-permute-done.23), channel_id=1, source_target_pairs={{0,3},{1,0},{2,1},{3,2},{4,7},{5,4},{6,5},{7,6},{8,11},{9,8},{10,9... | collective-permute-start | bytes 1671176 | tf_op jit(solution)/shard_map/ppermute | solution.py:68
  148.4 34.1 %collective-permute-start.19 = (bf16[136,2048]{1,0:T(8,128)(2,1)S(1)}, bf16[136,2048]{1,0:T(8,128)(2,1)S(1)}, u32[]{:S(2)}, u32[]{:S(2)}) collective-permute-start(bf16[136,2048]{1,0:T(8,128)(2,1)S(1)} %get-tuple-element.83), channel_id=1, source_target_pairs={{0,3},{1,0},{2,1},{3,2},{4,7},{5,4},{6,5},{7,6},{8,11},{9,8},{10,9... | collective-permute-start | bytes 1671176 | tf_op jit(solution)/shard_map/ppermute | solution.py:68
  171.1 39.9 %collective-permute-start.27 = (bf16[544,2048]{1,0:T(8,128)(2,1)S(1)}, bf16[544,2048]{1,0:T(8,128)(2,1)S(1)}, u32[]{:S(2)}, u32[]{:S(2)}) collective-permute-start(bf16[544,2048]{1,0:T(8,128)(2,1)S(1)} %pad_maximum_fusion.2), channel_id=1, source_target_pairs={{0,8},{1,9},{2,10},{3,11},{4,12},{5,13},{6,14},{7,15},{8,0},{9,1},... | collective-permute-start | bytes 6684680 | tf_op jit(solution)/shard_map/ppermute | solution.py:68
  171.7 49.6 %collective-permute-start.29 = (bf16[2048,1024]{1,0:T(8,128)(2,1)S(1)}, bf16[2048,1024]{1,0:T(8,128)(2,1)}, u32[]{:S(2)}, u32[]{:S(2)}) collective-permute-start(bf16[2048,1024]{1,0:T(8,128)(2,1)S(1)} %copy-done.60), channel_id=1, source_target_pairs={{0,4},{1,5},{2,6},{3,7},{4,12},{5,13},{6,14},{7,15},{8,0},{9,1},{1... | collective-permute-start | bytes 12582920 | tf_op jit(solution)/shard_map/ppermute | solution.py:68
  182.5 48.9 %collective-permute-start.30 = (bf16[2048,1024]{1,0:T(8,128)(2,1)}, bf16[2048,1024]{1,0:T(8,128)(2,1)}, u32[]{:S(2)}, u32[]{:S(2)}) collective-permute-start(bf16[2048,1024]{1,0:T(8,128)(2,1)} %param.23), channel_id=1, source_target_pairs={{0,68},{1,69},{2,70},{3,71},{4,12},{5,13},{6,14},{7,15},{8,0},{9,1... | collective-permute-start | bytes 12582920 | tf_op jit(solution)/shard_map/ppermute | solution.py:68
  271.8 28.1 %collective-permute-start.33 = (bf16[136,2048]{1,0:T(8,128)(2,1)S(1)}, bf16[136,2048]{1,0:T(8,128)(2,1)S(1)}, u32[]{:S(2)}, u32[]{:S(2)}) collective-permute-start(bf16[136,2048]{1,0:T(8,128)(2,1)S(1)} %get-tuple-element.96), channel_id=1, source_target_pairs={{0,2},{1,3},{2,0},{3,1},{4,6},{5,7},{6,4},{7,5},{8,10},{9,11},{10,... | collective-permute-start | bytes 1671176 | tf_op jit(solution)/shard_map/ppermute | solution.py:68
  276.5 34.4 %collective-permute-start.37 = (bf16[136,2048]{1,0:T(8,128)(2,1)S(1)}, bf16[136,2048]{1,0:T(8,128)(2,1)S(1)}, u32[]{:S(2)}, u32[]{:S(2)}) collective-permute-start(bf16[136,2048]{1,0:T(8,128)(2,1)S(1)} %get-tuple-element.91), channel_id=1, source_target_pairs={{0,1},{1,2},{2,3},{3,0},{4,5},{5,6},{6,7},{7,4},{8,9},{9,10},{10,1... | collective-permute-start | bytes 1671176 | tf_op jit(solution)/shard_map/ppermute | solution.py:68
  278.1 45.7 %collective-permute-start.38 = (bf16[136,2048]{1,0:T(8,128)(2,1)S(1)}, bf16[136,2048]{1,0:T(8,128)(2,1)S(1)}, u32[]{:S(2)}, u32[]{:S(2)}) collective-permute-start(bf16[136,2048]{1,0:T(8,128)(2,1)S(1)} %get-tuple-element.93), channel_id=1, source_target_pairs={{0,2},{1,3},{2,0},{3,1},{4,6},{5,7},{6,4},{7,5},{8,10},{9,11},{10,... | collective-permute-start | bytes 1671176 | tf_op jit(solution)/shard_map/ppermute | solution.py:68
  287.0 36.8 %collective-permute-start.39 = (bf16[136,2048]{1,0:T(8,128)(2,1)S(1)}, bf16[136,2048]{1,0:T(8,128)(2,1)S(1)}, u32[]{:S(2)}, u32[]{:S(2)}) collective-permute-start(bf16[136,2048]{1,0:T(8,128)(2,1)S(1)} %get-tuple-element.92), channel_id=1, source_target_pairs={{0,3},{1,0},{2,1},{3,2},{4,7},{5,4},{6,5},{7,6},{8,11},{9,8},{10,9... | collective-permute-start | bytes 1671176 | tf_op jit(solution)/shard_map/ppermute | solution.py:68
  370.0 157.7 %reduce-scatter.11.cloned.1.call-start = ((), (), s32[]{:S(2)}) async-start(), calls=%async_computation.7 | async-start | bytes 5242880 | tf_op jit(solution)/shard_map/reduce_scatter | solution.py:106
  390.2 161.1 %reduce-scatter.9.cloned.1.call-start = ((), (), s32[]{:S(2)}) async-start(), calls=%async_computation.6 | async-start | bytes 10485760 | tf_op jit(solution)/shard_map/reduce_scatter | solution.py:106
  408.9 152.0 %reduce-scatter.5.cloned.1.call-start = ((), (), s32[]{:S(2)}) async-start(), calls=%async_computation.4 | async-start | bytes 1966080 | tf_op jit(solution)/shard_map/reduce_scatter | solution.py:106
  492.3 27.6 %collective-permute-start.51 = (bf16[136,2048]{1,0:T(8,128)(2,1)}, bf16[136,2048]{1,0:T(8,128)(2,1)S(1)}, u32[]{:S(2)}, u32[]{:S(2)}) collective-permute-start(bf16[136,2048]{1,0:T(8,128)(2,1)} %get-tuple-element.88), channel_id=1, source_target_pairs={{0,1},{1,2},{2,3},{3,0},{4,5},{5,6},{6,7},{7,4},{8,9},{9,10},{10,1... | collective-permute-start | bytes 1671176 | tf_op jit(solution)/shard_map/ppermute | solution.py:68
  492.3 27.6 %collective-permute-start.52 = (bf16[136,2048]{1,0:T(8,128)(2,1)}, bf16[136,2048]{1,0:T(8,128)(2,1)}, u32[]{:S(2)}, u32[]{:S(2)}) collective-permute-start(bf16[136,2048]{1,0:T(8,128)(2,1)} %get-tuple-element.90), channel_id=1, source_target_pairs={{0,2},{1,3},{2,0},{3,1},{4,6},{5,7},{6,4},{7,5},{8,10},{9,11},{10,... | collective-permute-start | bytes 1671176 | tf_op jit(solution)/shard_map/ppermute | solution.py:68
  530.0 32.1 %collective-permute-start.78 = (bf16[256,1024]{0,1:T(8,128)(2,1)}, bf16[256,1024]{0,1:T(8,128)(2,1)}, u32[]{:S(2)}, u32[]{:S(2)}) collective-permute-start(bf16[256,1024]{0,1:T(8,128)(2,1)} %get-tuple-element.104), channel_id=1, source_target_pairs={{4,64},{5,65},{6,66},{7,67},{8,76},{9,77},{10,78},{11,79},{20,80},... | collective-permute-start | bytes 1572872 | tf_op jit(solution)/shard_map/ppermute | solution.py:68
  532.6 30.8 %collective-permute-start.79 = (bf16[256,1024]{0,1:T(8,128)(2,1)}, bf16[256,1024]{0,1:T(8,128)(2,1)}, u32[]{:S(2)}, u32[]{:S(2)}) collective-permute-start(bf16[256,1024]{0,1:T(8,128)(2,1)} %get-tuple-element.104), channel_id=1, source_target_pairs={{0,64},{1,65},{2,66},{3,67},{12,76},{13,77},{14,78},{15,79},{16,80... | collective-permute-start | bytes 1572872 | tf_op jit(solution)/shard_map/ppermute | solution.py:68
  552.9 39.5 %collective-permute-start.74 = (bf16[256,2048]{1,0:T(8,128)(2,1)S(1)}, bf16[256,2048]{1,0:T(8,128)(2,1)S(1)}, u32[]{:S(2)}, u32[]{:S(2)}) collective-permute-start(bf16[256,2048]{1,0:T(8,128)(2,1)S(1)} %get-tuple-element.101), channel_id=1, source_target_pairs={{4,64},{5,65},{6,66},{7,67},{8,76},{9,77},{10,78},{11,79},{20,80},... | collective-permute-start | bytes 3145736 | tf_op jit(solution)/shard_map/ppermute | solution.py:68
  554.3 39.1 %collective-permute-start.75 = (bf16[256,2048]{1,0:T(8,128)(2,1)S(1)}, bf16[256,2048]{1,0:T(8,128)(2,1)}, u32[]{:S(2)}, u32[]{:S(2)}) collective-permute-start(bf16[256,2048]{1,0:T(8,128)(2,1)S(1)} %get-tuple-element.101), channel_id=1, source_target_pairs={{0,64},{1,65},{2,66},{3,67},{12,76},{13,77},{14,78},{15,79},{16,80... | collective-permute-start | bytes 3145736 | tf_op jit(solution)/shard_map/ppermute | solution.py:68
  556.2 34.9 %collective-permute-start.73 = (bf16[256,2048]{1,0:T(8,128)(2,1)S(1)}, bf16[256,2048]{1,0:T(8,128)(2,1)}, u32[]{:S(2)}, u32[]{:S(2)}) collective-permute-start(bf16[256,2048]{1,0:T(8,128)(2,1)S(1)} %get-tuple-element.100), channel_id=1, source_target_pairs={{4,0},{5,1},{6,2},{7,3},{8,12},{9,13},{10,14},{11,15},{20,16},{21,... | collective-permute-start | bytes 3145736 | tf_op jit(solution)/shard_map/ppermute | solution.py:68
  (123 other events, 1596.6 us)
Sparse Core Ops, SparseCore 0:
  370.1 19.4 reduce-scatter.6
  392.1 48.3 reduce-scatter.10
  443.0 82.3 reduce-scatter.8
  527.7 23.7 reduce-scatter.4

commit v3 on v2

--- a/solution.py
+++ b/solution.py
@@ -73,10 +73,8 @@
     return (own, send(own, CORE))
 
 
-def scatter(own, other):
-    total = (own.astype(jnp.float32) + send(other, CORE).astype(jnp.float32)).astype(jnp.bfloat16)
-    rows = total.shape[0] // 4
-    part = [total[k * rows : (k + 1) * rows] for k in range(4)]
+def scatter(own, other, after=()):
+    part = add_parts(own, send(other, CORE), after)
     one, two, three = send(part[1], X_UP), send(part[2], X_FAR), send(part[3], X_DOWN)
     return (part[0].astype(jnp.float32) + one.astype(jnp.float32)) + (
         two.astype(jnp.float32) + three.astype(jnp.float32)
@@ -137,10 +135,12 @@
 
 
 VMEM = pl.BlockSpec(memory_space=pltpu.VMEM)
-
-
-def params(mib):
-    return pltpu.CompilerParams(vmem_limit_bytes=mib * 1024 * 1024)
+ANY = pl.BlockSpec(memory_space=pl.ANY)
+PARAMS = pltpu.CompilerParams(vmem_limit_bytes=60 * 1024 * 1024)
+
+
+def cost(flops, nbytes):
+    return pl.CostEstimate(flops=int(flops), bytes_accessed=int(nbytes), transcendentals=0)
 
 
 def dot(left, right, left_dim=1, right_dim=0):
@@ -202,7 +202,8 @@
         ),
         in_specs=[VMEM] * 2,
         out_specs=(VMEM,) * 2,
-        compiler_params=params(40),
+        compiler_params=PARAMS,
+        cost_estimate=cost(4e9, 2e6),
         name="short_forward",
     )(qkv, start)
 
@@ -210,7 +211,8 @@
 CHUNK = 1024
 
 
-def long_forward_kernel(q_ref, far_ref, far_pos_ref, pos_ref, attn_ref, lse_ref):
+def long_forward_kernel(q_ref, far_ref, far_pos_ref, pos_ref, *refs):
+    attn_ref, lse_ref = refs[-2:]
     for half in range(2):
         rows = pl.ds(half * HALF, HALF)
         q = stacked(q_ref[rows, :256]) * jnp.bfloat16(HEAD_DIM**-0.5)
@@ -240,18 +242,19 @@
         lse_ref[half] = as_row(top + jnp.log(total))
 
 
-def long_forward(q, far, far_pos, pos):
+def long_forward(q, far, far_pos, pos, after=()):
     return pl.pallas_call(
         long_forward_kernel,
         out_shape=(
             jax.ShapeDtypeStruct((2 * HALF, 256), jnp.bfloat16),
             jax.ShapeDtypeStruct((2, 8, 4 * HALF), jnp.float32),
         ),
-        in_specs=[VMEM] * 4,
+        in_specs=[VMEM] * 4 + [ANY] * len(after),
         out_specs=(VMEM,) * 2,
-        compiler_params=params(40),
+        compiler_params=PARAMS,
+        cost_estimate=cost(10e9, 2e6),
         name="long_forward",
-    )(q, far, far_pos, pos)
+    )(q, far, far_pos, pos, *after)
 
 
 def grad_terms(q, grad, k, v, seen, lse, delta):
@@ -314,7 +317,8 @@
         in_specs=[VMEM] * 7,
         out_specs=VMEM,
         scratch_shapes=[pltpu.VMEM((rows, HEAD_DIM), jnp.float32)] * 2,
-        compiler_params=params(48),
+        compiler_params=PARAMS,
+        cost_estimate=cost(7e9, 2e6),
         name="short_backward",
     )(qkv, start, attn, grad, lse, cos_rows, sin_rows)
 
@@ -352,9 +356,14 @@
             dq, dk, dv = grad_terms(q, grad, k, v, seen, lse, delta)
             acc_ref[half] += dq
             sums.append((dk, dv))
-        far_grad_ref[keys, :] = jnp.concatenate(
+        total = jnp.concatenate(
             [sums[0][0] + sums[1][0], sums[0][1] + sums[1][1]], axis=1
         ).astype(jnp.bfloat16)
+        rows = BACK_CHUNK // 4
+        for k in range(4):
+            far_grad_ref[k, pl.ds(pl.multiple_of(i * rows, rows), rows), :] = total[
+                k * rows : (k + 1) * rows
+            ]
         return carry
 
     lax.fori_loop(0, far_ref.shape[0] // BACK_CHUNK, step, 0)
@@ -373,37 +382,114 @@
         long_backward_kernel,
         out_shape=(
             jax.ShapeDtypeStruct((2 * HALF, 256), jnp.bfloat16),
-            jax.ShapeDtypeStruct(far.shape, jnp.bfloat16),
+            jax.ShapeDtypeStruct((4, far.shape[0] // 4, far.shape[1]), jnp.bfloat16),
         ),
         in_specs=[VMEM] * 9,
         out_specs=(VMEM,) * 2,
         scratch_shapes=[pltpu.VMEM((2, 4 * HALF, HEAD_DIM), jnp.float32)],
-        compiler_params=params(48),
+        compiler_params=PARAMS,
+        cost_estimate=cost(13e9, 3e6),
         name="long_backward",
     )(q, far, far_pos, pos, attn, grad, lse, cos_rows, sin_rows)
 
 
 def weight_grad_kernel(left_ref, right_ref, out_ref):
-    out_ref[0, 0] = dot(left_ref[...], right_ref[...], 0, 0).astype(jnp.bfloat16)
+    out_ref[...] = dot(left_ref[...], right_ref[...], 0, 0).astype(jnp.bfloat16)
 
 
 def weight_grad(left, right):
     tokens, width = right.shape
+    columns = left.shape[1]
     return pl.pallas_call(
         weight_grad_kernel,
         grid=(8,),
-        out_shape=jax.ShapeDtypeStruct((4, 2, 256, width), jnp.bfloat16),
+        out_shape=jax.ShapeDtypeStruct((columns, width), jnp.bfloat16),
         in_specs=[
-            pl.BlockSpec((tokens, 256), lambda i: (0, i)),
+            pl.BlockSpec((tokens, columns // 8), lambda i: (0, i)),
             pl.BlockSpec((tokens, width), lambda i: (0, 0), pipeline_mode=pl.Buffered(1)),
         ],
-        out_specs=pl.BlockSpec((1, 1, 256, width), lambda i: (i % 4, i // 4, 0, 0)),
-        compiler_params=params(40),
+        out_specs=pl.BlockSpec((columns // 8, width), lambda i: (i % 4 * 2 + i // 4, 0)),
+        compiler_params=PARAMS,
+        cost_estimate=cost(3e9 + 2 * tokens * columns * width, 4 * columns * (tokens + width)),
         name="weight_grad",
     )(left, right)
 
 
-def mlp_kernel(hidden_ref, grad_act_ref, gate_ref, up_ref, act_ref, both_ref, back_ref):
+def add_kernel(left_ref, right_ref, *refs):
+    for k, out_ref in enumerate(refs[-4:]):
+        rows = pl.ds(k * out_ref.shape[0], out_ref.shape[0])
+        out_ref[...] = (
+            left_ref[rows, :].astype(jnp.float32) + right_ref[rows, :].astype(jnp.float32)
+        ).astype(jnp.bfloat16)
+
+
+def add_parts(left, right, after=()):
+    rows, width = left.shape
+    return pl.pallas_call(
+        add_kernel,
+        grid=(2,),
+        out_shape=(jax.ShapeDtypeStruct((rows // 4, width), jnp.bfloat16),) * 4,
+        in_specs=[pl.BlockSpec((rows, width // 2), lambda i: (0, i))] * 2 + [ANY] * len(after),
+        out_specs=(pl.BlockSpec((rows // 4, width // 2), lambda i: (0, i)),) * 4,
+        compiler_params=PARAMS,
+        cost_estimate=cost(1e6, 6 * rows * width),
+        name="add_parts",
+    )(left, right, *after)
+
+
+def hidden_grad_kernel(low_ref, query_ref, kv_ref, hidden_ref, own_ref, other_ref, gain_ref):
+    i = pl.program_id(0)
+    low = low_ref[...]
+    grad = dot(low[:, :256], query_ref[...], 1, 1) + dot(low[:, 256:], kv_ref[...], 1, 1)
+    part = jnp.sum(grad * hidden_ref[...].astype(jnp.float32), axis=0, keepdims=True)
+
+    @pl.when(i == 0)
+    def _():
+        gain_ref[...] = jnp.broadcast_to(part, gain_ref.shape)
+
+    @pl.when(i > 0)
+    def _():
+        gain_ref[...] += part
+
+    @pl.when(i < 2)
+    def _():
+        own_ref[...] = grad.astype(jnp.bfloat16)
+
+    @pl.when(i >= 2)
+    def _():
+        other_ref[...] = grad.astype(jnp.bfloat16)
+
+
+def hidden_grad(low, w_query, w_key_value, hidden):
+    rows, d = hidden.shape
+    block = rows // 4
+    return pl.pallas_call(
+        hidden_grad_kernel,
+        grid=(4,),
+        out_shape=(
+            jax.ShapeDtypeStruct((rows // 2, d), jnp.bfloat16),
+            jax.ShapeDtypeStruct((rows // 2, d), jnp.bfloat16),
+            jax.ShapeDtypeStruct((8, d), jnp.float32),
+        ),
+        in_specs=[
+            pl.BlockSpec((block, 384), lambda i: (i, 0)),
+            pl.BlockSpec((d, 256), lambda i: (0, 0), pipeline_mode=pl.Buffered(1)),
+            pl.BlockSpec((d, 128), lambda i: (0, 0), pipeline_mode=pl.Buffered(1)),
+            pl.BlockSpec((block, d), lambda i: (i, 0)),
+        ],
+        out_specs=(
+            pl.BlockSpec((block, d), lambda i: (jnp.minimum(i, 1), 0)),
+            pl.BlockSpec((block, d), lambda i: (jnp.maximum(i, 2) - 2, 0)),
+            pl.BlockSpec((8, d), lambda i: (0, 0)),
+        ),
+        compiler_params=PARAMS,
+        cost_estimate=cost(2 * rows * d * 384, 4 * rows * d),
+        name="hidden_grad",
+    )(low, w_query, w_key_value, hidden)
+
+
+def mlp_kernel(hidden_ref, grad_act_ref, gate_ref, up_ref, act_ref, both_ref, own_ref, other_ref):
+    i = pl.program_id(0)
     hidden = hidden_ref[...]
     gate = dot(hidden, gate_ref[...])
     up = dot(hidden, up_ref[...])
@@ -416,13 +502,22 @@
     width = gate.shape[1]
     both_ref[:, :width] = grad_gate
     both_ref[:, width:] = grad_up
-    back_ref[...] = (dot(grad_gate, gate_ref[...], 1, 1) + dot(grad_up, up_ref[...], 1, 1)).astype(
+    back = (dot(grad_gate, gate_ref[...], 1, 1) + dot(grad_up, up_ref[...], 1, 1)).astype(
         jnp.bfloat16
     )
 
-
-def mlp(hidden, grad_act, w_gate, w_up, block=272):
+    @pl.when(i < 2)
+    def _():
+        own_ref[...] = back
+
+    @pl.when(i >= 2)
+    def _():
+        other_ref[...] = back
+
+
+def mlp(hidden, grad_act, w_gate, w_up):
     rows, d = hidden.shape
+    block = rows // 4
     width = w_gate.shape[1]
     return pl.pallas_call(
         mlp_kernel,
@@ -430,7 +525,8 @@
         out_shape=(
             jax.ShapeDtypeStruct((rows, width), jnp.bfloat16),
             jax.ShapeDtypeStruct((rows, 2 * width), jnp.bfloat16),
-            jax.ShapeDtypeStruct((rows, d), jnp.bfloat16),
+            jax.ShapeDtypeStruct((rows // 2, d), jnp.bfloat16),
+            jax.ShapeDtypeStruct((rows // 2, d), jnp.bfloat16),
         ),
         in_specs=[
             pl.BlockSpec((block, d), lambda i: (i, 0)),
@@ -441,9 +537,11 @@
         out_specs=(
             pl.BlockSpec((block, width), lambda i: (i, 0)),
             pl.BlockSpec((block, 2 * width), lambda i: (i, 0)),
-            pl.BlockSpec((block, d), lambda i: (i, 0)),
+            pl.BlockSpec((block, d), lambda i: (jnp.minimum(i, 1), 0)),
+            pl.BlockSpec((block, d), lambda i: (jnp.maximum(i, 2) - 2, 0)),
         ),
-        compiler_params=params(56),
+        compiler_params=PARAMS,
+        cost_estimate=cost(10 * rows * width * d, 12 * rows * d),
         name="mlp",
     )(hidden, grad_act, w_gate, w_up)
 
@@ -474,7 +572,8 @@
             pl.BlockSpec((block, HEAD_DIM), lambda i: (i, 0)),
         ],
         out_specs=pl.BlockSpec((block, 384), lambda i: (i, 0)),
-        compiler_params=params(32),
+        compiler_params=PARAMS,
+        cost_estimate=cost(4 * rows * d * 384, 4 * rows * d),
         name="project_qkv",
     )(hidden, w_query, w_key_value, cos_rows, sin_rows)
 
@@ -560,9 +659,9 @@
     pos_column = jnp.broadcast_to(long_pos[:, None], (long_rows, 128))
     pos_row = jnp.broadcast_to(long_pos[None, :], (8, long_rows))
     step = jnp.arange(16, dtype=jnp.int32)
-    far_yh = jnp.where(step // 4 >= 2, 1 - yh, yh)
-    far_yl = jnp.where((step // 4 == 1) | (step // 4 == 2), 1 - yl, yl)
-    far_group = (far_yh * 4 + (z + step) % 4) * 2 + far_yl
+    far_yh = jnp.where(step % 4 >= 2, 1 - yh, yh)
+    far_yl = jnp.where((step % 4 == 1) | (step % 4 == 2), 1 - yl, yl)
+    far_group = (far_yh * 4 + (z + step // 4) % 4) * 2 + far_yl
     far_half = place_at(2 * far_group[:, None] + jnp.arange(2, dtype=jnp.int32)[None, :])
     far_pos = (
         far_half.reshape(-1, 1) * HALF + jnp.arange(HALF, dtype=jnp.int32)[None, :]
@@ -578,14 +677,17 @@
     qkv = jnp.pad(in_order(qkv, core, x), ((0, padded_rows - group_rows), (0, 0)))
     near_rows = qkv[:long_rows, 256:]
     ring_rows = jnp.concatenate(
-        [near_rows, send(near_rows, Z_DOWN), send(near_rows, Z_FAR), send(near_rows, Z_UP)]
+        [near_rows, send(near_rows, Y_LOW), send(near_rows, Y_HIGH), send(near_rows, Y_FAR)]
     )
     far_rows = jnp.concatenate(
-        [ring_rows, send(ring_rows, Y_LOW), send(ring_rows, Y_HIGH), send(ring_rows, Y_FAR)]
-    )
+        [ring_rows, send(ring_rows, Z_DOWN), send(ring_rows, Z_FAR), send(ring_rows, Z_UP)]
+    )
+    grad_own, grad_other = gather(out_grad)
     long_q = qkv[:long_rows]
     short_attn, short_lse = short_forward(qkv, start_column)
-    long_attn, long_lse = long_forward(long_q, far_rows, far_row, pos_column)
+    long_attn, long_lse = long_forward(
+        long_q, far_rows, far_row, pos_column, (grad_own, w_gate, w_up)
+    )
     attn_rows = from_order(
         jnp.concatenate([long_attn, short_attn[: group_rows - long_rows]]), core, x
     )
@@ -598,22 +700,21 @@
     )
     inv_two = lax.rsqrt(jnp.mean(mixed * mixed, axis=-1, keepdims=True) + EPS)
     unit_two = mixed * inv_two
-    grad_rows = jnp.concatenate(gather(out_grad))
+    grad_rows = jnp.concatenate([grad_own, grad_other])
     grad_act = dot(grad_rows, w_down, 1, 1).astype(jnp.bfloat16)
     hidden_two = jnp.concatenate(gather((unit_two * mlp_gain).astype(jnp.bfloat16)))
 
-    act, grad_both, grad_hidden = mlp(hidden_two, grad_act, w_gate, w_up)
-    grad_two = scatter(grad_hidden[:half_rows], grad_hidden[half_rows:])
+    act, grad_both, back_own, back_other = mlp(hidden_two, grad_act, w_gate, w_up)
+    grad_two = scatter(back_own, back_other)
     down_sum = sum_groups(weight_grad(grad_rows, act), yh, core, native).T
     both_sum = sum_groups(weight_grad(hidden_two, grad_both), yh, core, native)
     ff = act.shape[1]
     down_rows = project(act, w_down)
-    output = mixed + scatter(down_rows[:half_rows], down_rows[half_rows:])
-    output = send(output.astype(jnp.bfloat16), TURN)
-
     grad_mixed = out_grad.astype(jnp.float32) + norm_back(grad_two, unit_two, inv_two, mlp_gain)
     mixed_grad_rows = jnp.concatenate(gather(grad_mixed.astype(jnp.bfloat16)))
     mlp_gain_part = jnp.sum(grad_two * unit_two, axis=0)
+    output = mixed + scatter(down_rows[:half_rows], down_rows[half_rows:], (mixed_grad_rows,))
+    output = send(output.astype(jnp.bfloat16), TURN)
     grad_attn = in_order(dot(mixed_grad_rows, w_out, 1, 1).astype(jnp.bfloat16), core, x)
     grad_attn = jnp.pad(grad_attn, ((0, padded_rows - group_rows), (0, 0)))
     long_dq, far_terms = long_backward(
@@ -627,7 +728,7 @@
         cos_ordered[:long_rows],
         sin_ordered[:long_rows],
     )
-    ring = far_terms.reshape(4, 4 * long_rows, -1)
+    ring = far_terms
     ring_terms = (
         (ring[0].astype(jnp.float32) + send(ring[1], Y_LOW).astype(jnp.float32))
         + (send(ring[2], Y_HIGH).astype(jnp.float32) + send(ring[3], Y_FAR).astype(jnp.float32))
@@ -651,16 +752,15 @@
     low_rows = from_order(
         jnp.concatenate([long_low, short_low[: group_rows - long_rows]]), core, x
     )
-    grad_hidden = (
-        dot(low_rows[:, :256], w_query, 1, 1) + dot(low_rows[:, 256:], w_key_value, 1, 1)
-    ).astype(jnp.bfloat16)
-    grad_one = scatter(grad_hidden[:half_rows], grad_hidden[half_rows:])
+    back_own, back_other, attn_gain_part = hidden_grad(
+        low_rows, w_query, w_key_value, hidden_one
+    )
+    grad_one = scatter(back_own, back_other)
+    gains = all_sum(jnp.stack([attn_gain_part[0] / attn_gain, mlp_gain_part]))
     out_sum = sum_groups(weight_grad(mixed_grad_rows, attn_rows), yh, core, native).T
     qkv_sum = sum_groups(weight_grad(hidden_one, low_rows), yh, core, native)
-    attn_gain_part = jnp.sum(grad_one * unit_one, axis=0)
     grad_tokens = grad_mixed + norm_back(grad_one, unit_one, inv_one, attn_gain)
     grad_tokens = send(grad_tokens.astype(jnp.bfloat16), TURN)
-    gains = all_sum(jnp.stack([attn_gain_part, mlp_gain_part]))
     return (
         output,
         grad_tokens,

time: 628 us -> 657 us (1.046)
  Pallas kernels: 98.5 us -> 147 us
  waiting for transfers between devices: 251 us -> 224 us
    ppermute x81, waiting for transfers between devices: 251 us -> 224 us  [send(): return lax.ppermute(values, BOTH, pairs)]
    pallas_call x0 -> x5, Pallas kernels: none -> 21.8 us  [the longest x4 14 us: add_parts(): pl.pallas_call(add_kernel, grid=(2,), out_shape=(jax.ShapeDtypeStruct((ro...]
    pallas_call x4, Pallas kernels: 30.5 us -> 43 us  [weight_grad(): pl.pallas_call(weight_grad_kernel, grid=(8,), out_shape=jax.ShapeDtypeStr...]
    reshape x3 -> x0, local copies, waits for them, and re-layouts: 10.5 us -> none  [sum_groups(): grad.reshape(-1, width)]
    unnamed x148 -> x81, local copies, waits for them, and re-layouts: 29.7 us -> 22.9 us
    dot_general x4 -> x2, matrix products: 16.8 us -> 13.5 us  [dot(): lax.dot_general(left, right, (((left_dim,), (right_dim,)), ((), ())), pre...]
  transfers between devices with their start and end apart: 85 -> 85, of which waited for: 36 -> 33; matrix products, arithmetic and copies ran while one was open for 14% -> 17% of each run, Pallas kernels for 11% -> 17%
where the time goes in v3:
time: 657 us; the launch traced here: 645 us
  waiting for transfers between devices  224 us (34%)
  Pallas kernels  147 us (22%)
  starting transfers between devices  129 us (20%)
  local copies, waits for them, and re-layouts  51.9 us (8%)
  other arithmetic  51.9 us (8%)
  matrix products  25.1 us (4%)
  between operations  16.4 us (2%)
    ppermute x81, waiting for transfers between devices, send(): return lax.ppermute(values, BOTH, pairs)  224 us
    ppermute x81, starting transfers between devices, send(): return lax.ppermute(values, BOTH, pairs)  129 us
    pallas_call x4, Pallas kernels, weight_grad(): pl.pallas_call(weight_grad_kernel, grid=(8,), out_shape=jax.ShapeDtypeStr...  43 us
    pallas_call x1, Pallas kernels, mlp(): pl.pallas_call(mlp_kernel, grid=(rows // block,), out_shape=(jax.ShapeDty...  26.9 us
    unnamed x81, local copies, waits for them, and re-layouts  22.9 us
    pallas_call x1, Pallas kernels, long_backward(): pl.pallas_call(long_backward_kernel, out_shape=(jax.ShapeDtypeStruct((2 *...  17.2 us
    pallas_call x4, Pallas kernels, add_parts(): pl.pallas_call(add_kernel, grid=(2,), out_shape=(jax.ShapeDtypeStruct((ro...  14 us
    pallas_call x1, Pallas kernels, long_forward(): pl.pallas_call(long_forward_kernel, out_shape=(jax.ShapeDtypeStruct((2 *...  13.8 us
  transfers between devices with their start and end apart: 85, of which 33 were waited for; matrix products, arithmetic and copies ran while one was open for 17% of the time, Pallas kernels for 17%

profile of v3, /device:TPU:1, one launch (start us, length us, event | category | flops | bytes accessed | tf_op | source)
XLA Modules:
  0.0 645.2 jit_solution(13922634371686120953)
XLA Ops:
  33.7 14.7 %collective-permute-done.1 = bf16[136,2048]{1,0:T(8,128)(2,1)S(1)} collective-permute-done((bf16[136,2048]{1,0:T(8,128)(2,1)S(1)}, bf16[136,2048]{1,0:T(8,128)(2,1)S(1)}, u32[]{:S(2)}, u32[]{:S(2)}) %collective-permute-start.1) | collective-permute-done | bytes 557088 | tf_op jit(solution)/shard_map/ppermute | solution.py:68
  60.0 9.2 %collective-permute-done.15 = bf16[136,2048]{1,0:T(8,128)(2,1)S(1)} collective-permute-done((bf16[136,2048]{1,0:T(8,128)(2,1)S(1)}, bf16[136,2048]{1,0:T(8,128)(2,1)S(1)}, u32[]{:S(2)}, u32[]{:S(2)}) %collective-permute-start.15) | collective-permute-done | bytes 557088 | tf_op jit(solution)/shard_map/ppermute | solution.py:68
  81.2 11.4 %collective-permute-start.6 = (bf16[2048,128]{1,0:T(8,128)(2,1)S(1)}, bf16[2048,128]{1,0:T(8,128)(2,1)S(1)}, u32[]{:S(2)}, u32[]{:S(2)}) collective-permute-start(bf16[2048,128]{1,0:T(8,128)(2,1)S(1)} %copy-done.12), channel_id=1, source_target_pairs={{0,68},{1,69},{2,70},{3,71},{4,12},{5,13},{6,14},{7,15},{8,0},{9,1... | collective-permute-start | bytes 1572872 | tf_op jit(solution)/shard_map/ppermute | solution.py:68
  131.6 9.3 %collective-permute-done.11 = bf16[1024,128]{1,0:T(8,128)(2,1)S(1)} collective-permute-done((bf16[1024,128]{1,0:T(8,128)(2,1)S(1)}, bf16[1024,128]{1,0:T(8,128)(2,1)S(1)}, u32[]{:S(2)}, u32[]{:S(2)}) %collective-permute-start.11) | collective-permute-done | bytes 262176 | tf_op jit(solution)/shard_map/ppermute | solution.py:68
  147.2 13.8 %long_forward.1 = (bf16[256,256]{1,0:T(8,128)(2,1)}, f32[2,8,512]{2,1,0:T(8,128)}) custom-call(bf16[256,384]{1,0:T(8,128)(2,1)} %slice.272.q_ref, bf16[4096,128]{1,0:T(8,128)(2,1)} %copy-done.24, s32[4,8,1024]{2,1,0:T(8,128)} %broadcast_in_dim.129.far_pos_ref, s32[256,128]{1,0:T(8,128)} %broadcast_in_dim.132.pos_ref, bf16[544,2048]{1,0:T(8,128)(2,1)} %copy-done.16, ...), custom_call_target="tpu_custom_call" | custom-call | flops 10000000000 | bytes 2000000 | tf_op jit(solution)/shard_map/long_forward/pallas_call | solution.py:246
  179.1 10.8 %collective-permute-done.22 = bf16[136,2048]{1,0:T(8,128)(2,1)S(1)} collective-permute-done((bf16[136,2048]{1,0:T(8,128)(2,1)}, bf16[136,2048]{1,0:T(8,128)(2,1)S(1)}, u32[]{:S(2)}, u32[]{:S(2)}) %collective-permute-start.22) | collective-permute-done | bytes 557088 | tf_op jit(solution)/shard_map/ppermute | solution.py:68
  189.9 12.8 %collective-permute-done.23 = bf16[136,2048]{1,0:T(8,128)(2,1)S(1)} collective-permute-done((bf16[136,2048]{1,0:T(8,128)(2,1)}, bf16[136,2048]{1,0:T(8,128)(2,1)S(1)}, u32[]{:S(2)}, u32[]{:S(2)}) %collective-permute-start.23) | collective-permute-done | bytes 557088 | tf_op jit(solution)/shard_map/ppermute | solution.py:68
  208.4 12.5 %collective-permute-done.25 = bf16[136,2048]{1,0:T(8,128)(2,1)S(1)} collective-permute-done((bf16[136,2048]{1,0:T(8,128)(2,1)S(1)}, bf16[136,2048]{1,0:T(8,128)(2,1)S(1)}, u32[]{:S(2)}, u32[]{:S(2)}) %collective-permute-start.25) | collective-permute-done | bytes 557088 | tf_op jit(solution)/shard_map/ppermute | solution.py:68
  222.8 12.4 %collective-permute-done.27 = bf16[136,2048]{1,0:T(8,128)(2,1)S(1)} collective-permute-done((bf16[136,2048]{1,0:T(8,128)(2,1)S(1)}, bf16[136,2048]{1,0:T(8,128)(2,1)S(1)}, u32[]{:S(2)}, u32[]{:S(2)}) %collective-permute-start.27) | collective-permute-done | bytes 557088 | tf_op jit(solution)/shard_map/ppermute | solution.py:68
  237.9 9.8 %convolution_convert_fusion.1.grad_act_ref = bf16[1088,1024]{1,0:T(8,128)(2,1)} fusion(bf16[1088,2048]{1,0:T(8,128)(2,1)} %constant_dynamic-update-slice_fusion.21.left_ref, bf16[1024,2048]{1,0:T(8,128)(2,1)} %collective-permute-done.30), kind=kOutput, calls=%fused_computation.1 | convolution fusion | flops 4564516864 | bytes 10878976 | tf_op jit(solution)/shard_map/dot_general | solution.py:147
  251.8 26.9 %mlp.1 = (bf16[1088,1024]{1,0:T(8,128)(2,1)}, bf16[1088,2048]{1,0:T(8,128)(2,1)}, bf16[544,2048]{1,0:T(8,128)(2,1)}, bf16[544,2048]{1,0:T(8,128)(2,1)}) custom-call(bf16[1088,2048]{1,0:T(8,128)(2,1)} %constant_dynamic-update-slice_fusion.16.hidden_ref.left_ref, bf16[1088,1024]{1,0:T(8,128)(2,1)} %convolution_convert_fusion.1.grad_act_ref, ...), custom_call_target="tpu_custom_call" | custom-call | flops 22817013760 | bytes 26738688 | tf_op jit(solution)/shard_map/mlp/pallas_call | solution.py:522
  289.6 24.8 %collective-permute-done.33 = bf16[136,2048]{1,0:T(8,128)(2,1)S(1)} collective-permute-done((bf16[136,2048]{1,0:T(8,128)(2,1)}, bf16[136,2048]{1,0:T(8,128)(2,1)S(1)}, u32[]{:S(2)}, u32[]{:S(2)}) %collective-permute-start.33) | collective-permute-done | bytes 557088 | tf_op jit(solution)/shard_map/ppermute | solution.py:68
  321.4 11.6 %collective-permute-done.36 = bf16[136,2048]{1,0:T(8,128)(2,1)S(1)} collective-permute-done((bf16[136,2048]{1,0:T(8,128)(2,1)S(1)}, bf16[136,2048]{1,0:T(8,128)(2,1)S(1)}, u32[]{:S(2)}, u32[]{:S(2)}) %collective-permute-start.36) | collective-permute-done | bytes 557088 | tf_op jit(solution)/shard_map/ppermute | solution.py:68
  335.5 12.9 %collective-permute-done.38 = bf16[136,2048]{1,0:T(8,128)(2,1)S(1)} collective-permute-done((bf16[136,2048]{1,0:T(8,128)(2,1)S(1)}, bf16[136,2048]{1,0:T(8,128)(2,1)S(1)}, u32[]{:S(2)}, u32[]{:S(2)}) %collective-permute-start.38) | collective-permute-done | bytes 557088 | tf_op jit(solution)/shard_map/ppermute | solution.py:68
  362.5 11.1 %weight_grad.7 = bf16[2048,1024]{1,0:T(8,128)(2,1)} custom-call(bf16[1088,2048]{1,0:T(8,128)(2,1)} %constant_dynamic-update-slice_fusion.21.left_ref, bf16[1088,1024]{1,0:T(8,128)(2,1)} %get-tuple-element.46.right_ref), custom_call_target="tpu_custom_call" | custom-call | flops 7563402752 | bytes 17301504 | tf_op jit(solution)/shard_map/weight_grad/pallas_call | solution.py:403
  373.6 16.2 %weight_grad.6 = bf16[2048,2048]{1,0:T(8,128)(2,1)} custom-call(bf16[1088,2048]{1,0:T(8,128)(2,1)} %constant_dynamic-update-slice_fusion.16.hidden_ref.left_ref, bf16[1088,2048]{1,0:T(8,128)(2,1)} %get-tuple-element.68.right_ref), custom_call_target="tpu_custom_call" | custom-call | flops 12126806016 | bytes 25690112 | tf_op jit(solution)/shard_map/weight_grad/pallas_call | solution.py:403
  396.3 8.7 %convolution_convert_fusion = bf16[1088,2048]{1,0:T(8,128)(2,1)} fusion(bf16[1088,1024]{1,0:T(8,128)(2,1)S(1)} %copy-done.26, bf16[1024,2048]{1,0:T(8,128)(2,1)} %collective-permute-done.30), kind=kOutput, calls=%fused_computation | convolution fusion | flops 4565630976 | bytes 10878976 | tf_op jit(solution)/shard_map/dot_general | solution.py:696
  413.9 17.2 %long_backward.1 = (bf16[256,256]{1,0:T(8,128)(2,1)}, bf16[4,1024,128]{2,1,0:T(8,128)(2,1)}) custom-call(bf16[256,384]{1,0:T(8,128)(2,1)} %slice.272.q_ref, bf16[4096,128]{1,0:T(8,128)(2,1)} %copy-done.24, s32[4096,128]{1,0:T(8,128)} %broadcast_in_dim.134.far_pos_ref, s32[8,256]{1,0:T(8,128)} %broadcast_in_dim.135.pos_ref, ...), custom_call_target="tpu_custom_call" | custom-call | flops 12999999488 | bytes 3000000 | tf_op jit(solution)/shard_map/long_backward/pallas_call | solution.py:381
  451.5 10.5 %short_backward.1 = bf16[896,384]{1,0:T(8,128)(2,1)} custom-call(bf16[1152,384]{1,0:T(8,128)(2,1)} %pad.8.qkv_ref, s32[8,896]{1,0:T(8,128)} %broadcast_in_dim.136.start_ref, bf16[896,256]{1,0:T(8,128)(2,1)} %get-tuple-element.41.attn_ref, bf16[1152,256]{1,0:T(8,128)(2,1)} %pad.9.grad_ref, f32[7,8,512]{2,1,0:T(8,128)} %get-tuple-element.60.lse_ref, ...), custom_call_target="tpu_custom_call" | custom-call | flops 7000000000 | bytes 2000000 | tf_op jit(solution)/shard_map/short_backward/pallas_call | solution.py:314
  465.4 7.8 %hidden_grad.1 = (bf16[544,2048]{1,0:T(8,128)(2,1)}, bf16[544,2048]{1,0:T(8,128)(2,1)}, f32[8,2048]{1,0:T(8,128)}) custom-call(bf16[1088,384]{1,0:T(8,128)(2,1)} %bitcast.60, bf16[2048,256]{1,0:T(8,128)(2,1)} %collective-permute-done.5.query_ref, bf16[2048,128]{1,0:T(8,128)(2,1)} %copy-done.15, ...), custom_call_target="tpu_custom_call" | custom-call | flops 1711276032 | bytes 8912896 | tf_op jit(solution)/shard_map/hidden_grad/pallas_call | solution.py:466
  497.5 8.3 %weight_grad.4 = bf16[2048,384]{1,0:T(8,128)(2,1)} custom-call(bf16[1088,2048]{1,0:T(8,128)(2,1)} %constant_dynamic-update-slice_fusion.hidden_ref.left_ref, bf16[1088,384]{1,0:T(8,128)(2,1)} %bitcast.61), custom_call_target="tpu_custom_call" | custom-call | flops 4711276032 | bytes 12058624 | tf_op jit(solution)/shard_map/weight_grad/pallas_call | solution.py:403
  522.8 10.7 %collective-permute-done.42 = bf16[136,2048]{1,0:T(8,128)(2,1)} collective-permute-done((bf16[136,2048]{1,0:T(8,128)(2,1)}, bf16[136,2048]{1,0:T(8,128)(2,1)}, u32[]{:S(2)}, u32[]{:S(2)}) %collective-permute-start.42) | collective-permute-done | bytes 557088 | tf_op jit(solution)/shard_map/ppermute | solution.py:68
  551.9 7.7 %collective-permute-start.78 = (bf16[256,1024]{1,0:T(8,128)(2,1)}, bf16[256,1024]{1,0:T(8,128)(2,1)}, u32[]{:S(2)}, u32[]{:S(2)}) collective-permute-start(bf16[256,1024]{1,0:T(8,128)(2,1)} %get-tuple-element.131), channel_id=1, source_target_pairs={{4,64},{5,65},{6,66},{7,67},{8,76},{9,77},{10,78},{11,79},{20,80},... | collective-permute-start | bytes 1572872 | tf_op jit(solution)/shard_map/ppermute | solution.py:68
  593.9 17.5 %collective-permute-done.65 = bf16[256,384]{1,0:T(8,128)(2,1)S(1)} collective-permute-done((bf16[256,384]{1,0:T(8,128)(2,1)S(1)}, bf16[256,384]{1,0:T(8,128)(2,1)S(1)}, u32[]{:S(2)}, u32[]{:S(2)}) %collective-permute-start.65) | collective-permute-done | bytes 196640 | tf_op jit(solution)/shard_map/ppermute | solution.py:68
  (358 shorter events, 320.4 us)
Async XLA Ops:
  7.2 501.7 %reduce-scatter.7.cloned.1.call-start = ((), (), s32[]{:S(2)}) async-start(), calls=%async_computation.5 | async-start | bytes 1310720 | tf_op jit(solution)/shard_map/reduce_scatter | solution.py:104
  13.8 41.3 %collective-permute-start.14 = (bf16[136,2048]{1,0:T(8,128)(2,1)}, bf16[136,2048]{1,0:T(8,128)(2,1)S(1)}, u32[]{:S(2)}, u32[]{:S(2)}) collective-permute-start(bf16[136,2048]{1,0:T(8,128)(2,1)} %param.25), channel_id=1, source_target_pairs={{0,0},{1,1},{2,2},{3,3},{4,8},{5,9},{6,10},{7,11},{8,4},{9,5},{10,... | collective-permute-start | bytes 1671176 | tf_op jit(solution)/shard_map/ppermute | solution.py:68
  29.9 115.7 %collective-permute-start.18 = (bf16[2048,1024]{1,0:T(8,128)(2,1)}, bf16[2048,1024]{1,0:T(8,128)(2,1)}, u32[]{:S(2)}, u32[]{:S(2)}) collective-permute-start(bf16[2048,1024]{1,0:T(8,128)(2,1)} %param.22), channel_id=1, source_target_pairs={{0,4},{1,5},{2,6},{3,7},{4,12},{5,13},{6,14},{7,15},{8,0},{9,1},{1... | collective-permute-start | bytes 12582920 | tf_op jit(solution)/shard_map/ppermute | solution.py:68
  48.4 97.2 %collective-permute-start.19 = (bf16[2048,1024]{1,0:T(8,128)(2,1)}, bf16[2048,1024]{1,0:T(8,128)(2,1)}, u32[]{:S(2)}, u32[]{:S(2)}) collective-permute-start(bf16[2048,1024]{1,0:T(8,128)(2,1)} %param.23), channel_id=1, source_target_pairs={{0,68},{1,69},{2,70},{3,71},{4,12},{5,13},{6,14},{7,15},{8,0},{9,1... | collective-permute-start | bytes 12582920 | tf_op jit(solution)/shard_map/ppermute | solution.py:68
  52.6 42.5 %collective-permute-start.4 = (bf16[544,2048]{1,0:T(8,128)(2,1)S(1)}, bf16[544,2048]{1,0:T(8,128)(2,1)S(1)}, u32[]{:S(2)}, u32[]{:S(2)}) collective-permute-start(bf16[544,2048]{1,0:T(8,128)(2,1)S(1)} %pad_maximum_fusion), channel_id=1, source_target_pairs={{0,8},{1,9},{2,10},{3,11},{4,12},{5,13},{6,14},{7,15},{8,0},{9,1},... | collective-permute-start | bytes 6684680 | tf_op jit(solution)/shard_map/ppermute | solution.py:68
  73.3 29.5 %collective-permute-start.5 = (bf16[2048,256]{1,0:T(8,128)(2,1)S(1)}, bf16[2048,256]{1,0:T(8,128)(2,1)}, u32[]{:S(2)}, u32[]{:S(2)}) collective-permute-start(bf16[2048,256]{1,0:T(8,128)(2,1)S(1)} %copy-done.25), channel_id=1, source_target_pairs={{0,4},{1,5},{2,6},{3,7},{4,12},{5,13},{6,14},{7,15},{8,0},{9,1},{1... | collective-permute-start | bytes 3145736 | tf_op jit(solution)/shard_map/ppermute | solution.py:68
  164.5 73.4 %collective-permute-start.30 = (bf16[1024,2048]{1,0:T(8,128)(2,1)}, bf16[1024,2048]{1,0:T(8,128)(2,1)}, u32[]{:S(2)}, u32[]{:S(2)}) collective-permute-start(bf16[1024,2048]{1,0:T(8,128)(2,1)} %param.24), channel_id=1, source_target_pairs={{0,4},{1,5},{2,6},{3,7},{4,12},{5,13},{6,14},{7,15},{8,0},{9,1},{1... | collective-permute-start | bytes 12582920 | tf_op jit(solution)/shard_map/ppermute | solution.py:68
  173.9 28.8 %collective-permute-start.23 = (bf16[136,2048]{1,0:T(8,128)(2,1)}, bf16[136,2048]{1,0:T(8,128)(2,1)S(1)}, u32[]{:S(2)}, u32[]{:S(2)}) collective-permute-start(bf16[136,2048]{1,0:T(8,128)(2,1)} %get-tuple-element.44), channel_id=1, source_target_pairs={{0,2},{1,3},{2,0},{3,1},{4,6},{5,7},{6,4},{7,5},{8,10},{9,11},{10,... | collective-permute-start | bytes 1671176 | tf_op jit(solution)/shard_map/ppermute | solution.py:68
  178.2 58.2 %collective-permute-start.29 = (bf16[544,2048]{1,0:T(8,128)(2,1)}, bf16[544,2048]{1,0:T(8,128)(2,1)S(1)}, u32[]{:S(2)}, u32[]{:S(2)}) collective-permute-start(bf16[544,2048]{1,0:T(8,128)(2,1)} %copy-done.16), channel_id=1, source_target_pairs={{0,8},{1,9},{2,10},{3,11},{4,12},{5,13},{6,14},{7,15},{8,0},{9,1},... | collective-permute-start | bytes 6684680 | tf_op jit(solution)/shard_map/ppermute | solution.py:68
  207.9 27.4 %collective-permute-start.27 = (bf16[136,2048]{1,0:T(8,128)(2,1)S(1)}, bf16[136,2048]{1,0:T(8,128)(2,1)S(1)}, u32[]{:S(2)}, u32[]{:S(2)}) collective-permute-start(bf16[136,2048]{1,0:T(8,128)(2,1)S(1)} %get-tuple-element.121), channel_id=1, source_target_pairs={{0,1},{1,2},{2,3},{3,0},{4,5},{5,6},{6,7},{7,4},{8,9},{9,10},{10,1... | collective-permute-start | bytes 1671176 | tf_op jit(solution)/shard_map/ppermute | solution.py:68
  286.8 27.5 %collective-permute-start.33 = (bf16[136,2048]{1,0:T(8,128)(2,1)}, bf16[136,2048]{1,0:T(8,128)(2,1)S(1)}, u32[]{:S(2)}, u32[]{:S(2)}) collective-permute-start(bf16[136,2048]{1,0:T(8,128)(2,1)} %get-tuple-element.50), channel_id=1, source_target_pairs={{0,1},{1,2},{2,3},{3,0},{4,5},{5,6},{6,7},{7,4},{8,9},{9,10},{10,1... | collective-permute-start | bytes 1671176 | tf_op jit(solution)/shard_map/ppermute | solution.py:68
  286.9 27.4 %collective-permute-start.34 = (bf16[136,2048]{1,0:T(8,128)(2,1)}, bf16[136,2048]{1,0:T(8,128)(2,1)S(1)}, u32[]{:S(2)}, u32[]{:S(2)}) collective-permute-start(bf16[136,2048]{1,0:T(8,128)(2,1)} %get-tuple-element.51), channel_id=1, source_target_pairs={{0,2},{1,3},{2,0},{3,1},{4,6},{5,7},{6,4},{7,5},{8,10},{9,11},{10,... | collective-permute-start | bytes 1671176 | tf_op jit(solution)/shard_map/ppermute | solution.py:68
  320.8 27.6 %collective-permute-start.38 = (bf16[136,2048]{1,0:T(8,128)(2,1)S(1)}, bf16[136,2048]{1,0:T(8,128)(2,1)S(1)}, u32[]{:S(2)}, u32[]{:S(2)}) collective-permute-start(bf16[136,2048]{1,0:T(8,128)(2,1)S(1)} %get-tuple-element.118), channel_id=1, source_target_pairs={{0,1},{1,2},{2,3},{3,0},{4,5},{5,6},{6,7},{7,4},{8,9},{9,10},{10,1... | collective-permute-start | bytes 1671176 | tf_op jit(solution)/shard_map/ppermute | solution.py:68
  362.4 187.3 %reduce-scatter.11.cloned.1.call-start = ((), (), s32[]{:S(2)}) async-start(), calls=%async_computation.7 | async-start | bytes 5242880 | tf_op jit(solution)/shard_map/reduce_scatter | solution.py:104
  373.6 203.1 %reduce-scatter.9.cloned.1.call-start = ((), (), s32[]{:S(2)}) async-start(), calls=%async_computation.6 | async-start | bytes 10485760 | tf_op jit(solution)/shard_map/reduce_scatter | solution.py:104
  389.8 198.6 %reduce-scatter.5.cloned.1.call-start = ((), (), s32[]{:S(2)}) async-start(), calls=%async_computation.4 | async-start | bytes 1966080 | tf_op jit(solution)/shard_map/reduce_scatter | solution.py:104
  440.6 47.1 %collective-permute-start.31 = (bf16[544,2048]{1,0:T(8,128)(2,1)}, bf16[544,2048]{1,0:T(8,128)(2,1)}, u32[]{:S(2)}, u32[]{:S(2)}) collective-permute-start(bf16[544,2048]{1,0:T(8,128)(2,1)} %get-tuple-element.126), channel_id=1, source_target_pairs={{0,8},{1,9},{2,10},{3,11},{4,12},{5,13},{6,14},{7,15},{8,0},{9,1},... | collective-permute-start | bytes 6684680 | tf_op jit(solution)/shard_map/ppermute | solution.py:68
  491.3 50.1 %collective-permute-start.50 = (bf16[544,2048]{1,0:T(8,128)(2,1)}, bf16[544,2048]{1,0:T(8,128)(2,1)}, u32[]{:S(2)}, u32[]{:S(2)}) collective-permute-start(bf16[544,2048]{1,0:T(8,128)(2,1)} %get-tuple-element.62), channel_id=1, source_target_pairs={{0,8},{1,9},{2,10},{3,11},{4,12},{5,13},{6,14},{7,15},{8,0},{9,1},... | collective-permute-start | bytes 6684680 | tf_op jit(solution)/shard_map/ppermute | solution.py:68
  509.9 30.0 %collective-permute-start.70 = (bf16[256,256]{1,0:T(8,128)(2,1)S(1)}, bf16[256,256]{1,0:T(8,128)(2,1)S(1)}, u32[]{:S(2)}, u32[]{:S(2)}) collective-permute-start(bf16[256,256]{1,0:T(8,128)(2,1)S(1)} %get-tuple-element.154), channel_id=1, source_target_pairs={{4,64},{5,65},{6,66},{7,67},{8,76},{9,77},{10,78},{11,79},{20,80},... | collective-permute-start | bytes 393224 | tf_op jit(solution)/shard_map/ppermute | solution.py:68
  551.9 37.5 %collective-permute-start.78 = (bf16[256,1024]{1,0:T(8,128)(2,1)}, bf16[256,1024]{1,0:T(8,128)(2,1)}, u32[]{:S(2)}, u32[]{:S(2)}) collective-permute-start(bf16[256,1024]{1,0:T(8,128)(2,1)} %get-tuple-element.131), channel_id=1, source_target_pairs={{4,64},{5,65},{6,66},{7,67},{8,76},{9,77},{10,78},{11,79},{20,80},... | collective-permute-start | bytes 1572872 | tf_op jit(solution)/shard_map/ppermute | solution.py:68
  559.6 31.1 %collective-permute-start.79 = (bf16[256,1024]{1,0:T(8,128)(2,1)}, bf16[256,1024]{1,0:T(8,128)(2,1)}, u32[]{:S(2)}, u32[]{:S(2)}) collective-permute-start(bf16[256,1024]{1,0:T(8,128)(2,1)} %get-tuple-element.131), channel_id=1, source_target_pairs={{0,64},{1,65},{2,66},{3,67},{12,76},{13,77},{14,78},{15,79},{16,80... | collective-permute-start | bytes 1572872 | tf_op jit(solution)/shard_map/ppermute | solution.py:68
  578.3 38.5 %collective-permute-start.74 = (bf16[256,2048]{1,0:T(8,128)(2,1)S(1)}, bf16[256,2048]{1,0:T(8,128)(2,1)}, u32[]{:S(2)}, u32[]{:S(2)}) collective-permute-start(bf16[256,2048]{1,0:T(8,128)(2,1)S(1)} %get-tuple-element.129), channel_id=1, source_target_pairs={{4,64},{5,65},{6,66},{7,67},{8,76},{9,77},{10,78},{11,79},{20,80},... | collective-permute-start | bytes 3145736 | tf_op jit(solution)/shard_map/ppermute | solution.py:68
  584.5 32.4 %collective-permute-start.75 = (bf16[256,2048]{1,0:T(8,128)(2,1)S(1)}, bf16[256,2048]{1,0:T(8,128)(2,1)}, u32[]{:S(2)}, u32[]{:S(2)}) collective-permute-start(bf16[256,2048]{1,0:T(8,128)(2,1)S(1)} %get-tuple-element.129), channel_id=1, source_target_pairs={{0,64},{1,65},{2,66},{3,67},{12,76},{13,77},{14,78},{15,79},{16,80... | collective-permute-start | bytes 3145736 | tf_op jit(solution)/shard_map/ppermute | solution.py:68
  586.1 29.4 %collective-permute-start.73 = (bf16[256,2048]{1,0:T(8,128)(2,1)S(1)}, bf16[256,2048]{1,0:T(8,128)(2,1)}, u32[]{:S(2)}, u32[]{:S(2)}) collective-permute-start(bf16[256,2048]{1,0:T(8,128)(2,1)S(1)} %get-tuple-element.128), channel_id=1, source_target_pairs={{4,0},{5,1},{6,2},{7,3},{8,12},{9,13},{10,14},{11,15},{20,16},{21,... | collective-permute-start | bytes 3145736 | tf_op jit(solution)/shard_map/ppermute | solution.py:68
  (89 other events, 1206.3 us)
Sparse Core Ops, SparseCore 0:
  362.5 17.4 reduce-scatter.6
  382.6 48.4 reduce-scatter.10
  433.6 83.7 reduce-scatter.8
  519.7 24.6 reduce-scatter.4

commit v4 on v3

--- a/solution.py
+++ b/solution.py
@@ -1,3 +1,5 @@
+import functools
+
 import jax
 import jax.numpy as jnp
 from jax import lax
@@ -64,29 +66,44 @@
 ]
 
 
+CHIP_GROUPS = [
+    [place_of(yh, z, c, yl, x) for c in range(2) for x in range(4)]
+    for yh in range(2)
+    for z in range(4)
+    for yl in range(2)
+]
+
+
 def send(values, pairs):
     return lax.ppermute(values, BOTH, pairs)
 
 
-def gather(rows):
-    own = jnp.concatenate([rows, send(rows, X_DOWN), send(rows, X_FAR), send(rows, X_UP)])
-    return (own, send(own, CORE))
-
-
-def scatter(own, other, after=()):
-    part = add_parts(own, send(other, CORE), after)
-    one, two, three = send(part[1], X_UP), send(part[2], X_FAR), send(part[3], X_DOWN)
-    return (part[0].astype(jnp.float32) + one.astype(jnp.float32)) + (
-        two.astype(jnp.float32) + three.astype(jnp.float32)
-    )
-
-
-def in_order(values, core, x):
-    half = values.shape[0] // 2
+def gather(rows, after=(), passed=()):
+    pieces = (rows, send(rows, X_DOWN), send(rows, X_FAR), send(rows, X_UP))
+    own, *passed = join(pieces, after, passed)
+    return (own, send(own, CORE), *passed)
+
+
+def scatter(parts):
+    return (
+        parts[0],
+        send(parts[1], X_UP),
+        send(parts[2], X_FAR),
+        send(parts[3], X_DOWN),
+    )
+
+
+def total_of(parts):
+    one, two, three, four = [part.astype(jnp.float32) for part in parts]
+    return (one + two) + (three + four)
+
+
+def in_order(own, other, core, x):
+    half = own.shape[0]
+    pair = jnp.stack([own, other])
     start = (4 - x) % 4 * (half // 4)
-    pair = jnp.stack([values[:half], values[half:]])
     pair = lax.dynamic_slice_in_dim(jnp.concatenate([pair, pair], axis=1), start, half, axis=1)
-    return jnp.where(core == 0, pair, pair[::-1]).reshape(values.shape)
+    return jnp.where(core == 0, pair, pair[::-1]).reshape(2 * half, -1)
 
 
 def from_order(values, core, x):
@@ -96,7 +113,7 @@
     pair = lax.dynamic_slice_in_dim(
         jnp.concatenate([pair, pair], axis=1), x * (half // 4), half, axis=1
     )
-    return pair.reshape(values.shape)
+    return pair[0], pair[1]
 
 
 def sum_groups(grad, yh, core, native):
@@ -274,8 +291,9 @@
 
 
 def short_backward_kernel(
-    qkv_ref, start_ref, attn_ref, grad_ref, lse_ref, cos_ref, sin_ref, out_ref, dk_ref, dv_ref
+    qkv_ref, start_ref, attn_ref, grad_ref, lse_ref, cos_ref, sin_ref, *refs
 ):
+    out_ref, dk_ref, dv_ref = refs[-3:]
     blocks = attn_ref.shape[0] // HALF
     scale = HEAD_DIM**-0.5
     dk_ref[...] = jnp.zeros_like(dk_ref)
@@ -309,27 +327,27 @@
     out_ref[:, 256:] = jnp.concatenate([dk, dv_ref[...]], axis=1).astype(jnp.bfloat16)
 
 
-def short_backward(qkv, start, attn, grad, lse, cos_rows, sin_rows):
+def short_backward(qkv, start, attn, grad, lse, cos_rows, sin_rows, after=()):
     rows = attn.shape[0]
     return pl.pallas_call(
         short_backward_kernel,
         out_shape=jax.ShapeDtypeStruct((rows, 384), jnp.bfloat16),
-        in_specs=[VMEM] * 7,
+        in_specs=[VMEM] * 7 + [ANY] * len(after),
         out_specs=VMEM,
         scratch_shapes=[pltpu.VMEM((rows, HEAD_DIM), jnp.float32)] * 2,
         compiler_params=PARAMS,
         cost_estimate=cost(7e9, 2e6),
         name="short_backward",
-    )(qkv, start, attn, grad, lse, cos_rows, sin_rows)
+    )(qkv, start, attn, grad, lse, cos_rows, sin_rows, *after)
 
 
 BACK_CHUNK = 1024
 
 
 def long_backward_kernel(
-    q_ref, far_ref, far_pos_ref, pos_ref, attn_ref, grad_ref, lse_ref, cos_ref, sin_ref,
-    dq_ref, far_grad_ref, acc_ref,
+    q_ref, far_ref, far_pos_ref, pos_ref, attn_ref, grad_ref, lse_ref, cos_ref, sin_ref, *refs
 ):
+    dq_ref, far_grad_ref, acc_ref = refs[-3:]
     scale = HEAD_DIM**-0.5
     acc_ref[...] = jnp.zeros_like(acc_ref)
     queries = []
@@ -377,42 +395,87 @@
         dq_ref[rows, :] = unstacked(dq).astype(jnp.bfloat16)
 
 
-def long_backward(q, far, far_pos, pos, attn, grad, lse, cos_rows, sin_rows):
+def long_backward(q, far, far_pos, pos, attn, grad, lse, cos_rows, sin_rows, after=()):
     return pl.pallas_call(
         long_backward_kernel,
         out_shape=(
             jax.ShapeDtypeStruct((2 * HALF, 256), jnp.bfloat16),
             jax.ShapeDtypeStruct((4, far.shape[0] // 4, far.shape[1]), jnp.bfloat16),
         ),
-        in_specs=[VMEM] * 9,
+        in_specs=[VMEM] * 9 + [ANY] * len(after),
         out_specs=(VMEM,) * 2,
         scratch_shapes=[pltpu.VMEM((2, 4 * HALF, HEAD_DIM), jnp.float32)],
         compiler_params=PARAMS,
         cost_estimate=cost(13e9, 3e6),
         name="long_backward",
-    )(q, far, far_pos, pos, attn, grad, lse, cos_rows, sin_rows)
-
-
-def weight_grad_kernel(left_ref, right_ref, out_ref):
-    out_ref[...] = dot(left_ref[...], right_ref[...], 0, 0).astype(jnp.bfloat16)
-
-
-def weight_grad(left, right):
-    tokens, width = right.shape
-    columns = left.shape[1]
+    )(q, far, far_pos, pos, attn, grad, lse, cos_rows, sin_rows, *after)
+
+
+def weight_grad_kernel(left_ref, other_left_ref, right_ref, other_right_ref, *refs):
+    out_ref, width = refs[-1], right_ref.shape[1]
+    out_ref[:, :width] = (
+        dot(left_ref[...], right_ref[...], 0, 0)
+        + dot(other_left_ref[...], other_right_ref[...], 0, 0)
+    ).astype(jnp.bfloat16)
+    if out_ref.shape[1] > width:
+        out_ref[:, width:] = refs[0][...]
+
+
+def weight_grad(left, right, after=(), beside=()):
+    tokens, width = right[0].shape
+    columns = left[0].shape[1]
+    whole = width + sum(array.shape[1] for array in beside)
+    once = pl.BlockSpec((tokens, width), lambda i: (0, 0), pipeline_mode=pl.Buffered(1))
+
+    def out_block(n):
+        return pl.BlockSpec((columns // 8, n), lambda i: (i % 4 * 2 + i // 4, 0))
+
     return pl.pallas_call(
         weight_grad_kernel,
         grid=(8,),
-        out_shape=jax.ShapeDtypeStruct((columns, width), jnp.bfloat16),
-        in_specs=[
-            pl.BlockSpec((tokens, columns // 8), lambda i: (0, i)),
-            pl.BlockSpec((tokens, width), lambda i: (0, 0), pipeline_mode=pl.Buffered(1)),
-        ],
-        out_specs=pl.BlockSpec((columns // 8, width), lambda i: (i % 4 * 2 + i // 4, 0)),
-        compiler_params=PARAMS,
-        cost_estimate=cost(3e9 + 2 * tokens * columns * width, 4 * columns * (tokens + width)),
+        out_shape=jax.ShapeDtypeStruct((columns, whole), jnp.bfloat16),
+        in_specs=[pl.BlockSpec((tokens, columns // 8), lambda i: (0, i))] * 2
+        + [once] * 2
+        + [out_block(array.shape[1]) for array in beside]
+        + [ANY] * len(after),
+        out_specs=out_block(whole),
+        compiler_params=PARAMS,
+        cost_estimate=cost(3e9 + 4 * tokens * columns * width, 4 * columns * (tokens + width)),
         name="weight_grad",
-    )(left, right)
+    )(*left, *right, *beside, *after)
+
+
+def join_kernel(count, after, passed, *refs):
+    sources = refs[:count]
+    inputs = refs[count + after : count + after + passed]
+    outs = refs[count + after + passed :]
+    for k, ref in enumerate(sources):
+        outs[0][k] = ref[...]
+    for ref, out in zip(inputs, outs[1:]):
+        out[...] = ref[...]
+
+
+def join(pieces, after=(), passed=()):
+    rows, width = pieces[0].shape
+    count = len(pieces)
+    block = pl.BlockSpec((rows, width // 4), lambda i: (0, i))
+    joined, *copied = pl.pallas_call(
+        functools.partial(join_kernel, count, len(after), len(passed)),
+        grid=(4,),
+        out_shape=(
+            jax.ShapeDtypeStruct((count, rows, width), pieces[0].dtype),
+            *[jax.ShapeDtypeStruct(array.shape, array.dtype) for array in passed],
+        ),
+        in_specs=[block] * count + [ANY] * len(after) + [block] * len(passed),
+        out_specs=(
+            pl.BlockSpec((count, rows, width // 4), lambda i: (0, 0, i)),
+            *[block for _ in passed],
+        ),
+        compiler_params=PARAMS,
+        cost_estimate=cost(1e6, 4 * count * rows * width),
+        name="join",
+    )(*pieces, *after, *passed)
+    return (joined.reshape(count * rows, width), *copied)
 
 
 def add_kernel(left_ref, right_ref, *refs):
@@ -427,69 +490,182 @@
     rows, width = left.shape
     return pl.pallas_call(
         add_kernel,
-        grid=(2,),
+        grid=(4,),
         out_shape=(jax.ShapeDtypeStruct((rows // 4, width), jnp.bfloat16),) * 4,
-        in_specs=[pl.BlockSpec((rows, width // 2), lambda i: (0, i))] * 2 + [ANY] * len(after),
-        out_specs=(pl.BlockSpec((rows // 4, width // 2), lambda i: (0, i)),) * 4,
+        in_specs=[pl.BlockSpec((rows, width // 4), lambda i: (0, i))] * 2 + [ANY] * len(after),
+        out_specs=(pl.BlockSpec((rows // 4, width // 4), lambda i: (0, i)),) * 4,
         compiler_params=PARAMS,
         cost_estimate=cost(1e6, 6 * rows * width),
         name="add_parts",
     )(left, right, *after)
 
 
-def hidden_grad_kernel(low_ref, query_ref, kv_ref, hidden_ref, own_ref, other_ref, gain_ref):
-    i = pl.program_id(0)
+def product_kernel(turned_right, left_ref, right_ref, *refs):
+    refs[-1][...] = dot(left_ref[...], right_ref[...], 1, 1 if turned_right else 0).astype(
+        jnp.bfloat16
+    )
+
+
+def product(left, right, after=(), turned_right=False, block=272):
+    rows, depth = left.shape
+    width = right.shape[0] if turned_right else right.shape[1]
+    return pl.pallas_call(
+        functools.partial(product_kernel, turned_right),
+        grid=(rows // block,),
+        out_shape=jax.ShapeDtypeStruct((rows, width), jnp.bfloat16),
+        in_specs=[
+            pl.BlockSpec((block, depth), lambda i: (i, 0)),
+            pl.BlockSpec(right.shape, lambda i: (0, 0), pipeline_mode=pl.Buffered(1)),
+        ]
+        + [ANY] * len(after),
+        out_specs=pl.BlockSpec((block, width), lambda i: (i, 0)),
+        compiler_params=PARAMS,
+        cost_estimate=cost(2 * rows * depth * width, 2 * (depth + rows) * width),
+        name="product",
+    )(left, right, *after)
+
+
+def parts_kernel(terms, turned_right, *refs):
+    outs, sent_ref = refs[-4:], refs[2 * terms]
+    total = sent_ref[...].astype(jnp.float32)
+    for k in range(terms):
+        total += dot(refs[2 * k][...], refs[2 * k + 1][...], 1, 1 if turned_right else 0)
+    rows = outs[0].shape[0]
+    for k, out_ref in enumerate(outs):
+        out_ref[...] = total[k * rows : (k + 1) * rows].astype(jnp.bfloat16)
+
+
+def product_parts(pairs, sent, turned_right=False, after=()):
+    rows, width = sent.shape
+    block = width // 4
+    specs = []
+    for left, right in pairs:
+        specs.append(pl.BlockSpec(left.shape, lambda i: (0, 0), pipeline_mode=pl.Buffered(1)))
+        if turned_right:
+            specs.append(pl.BlockSpec((block, right.shape[1]), lambda i: (i, 0)))
+        else:
+            specs.append(pl.BlockSpec((right.shape[0], block), lambda i: (0, i)))
+    return pl.pallas_call(
+        functools.partial(parts_kernel, len(pairs), turned_right),
+        grid=(4,),
+        out_shape=(jax.ShapeDtypeStruct((rows // 4, width), jnp.bfloat16),) * 4,
+        in_specs=specs + [pl.BlockSpec((rows, block), lambda i: (0, i))] + [ANY] * len(after),
+        out_specs=(pl.BlockSpec((rows // 4, block), lambda i: (0, i)),) * 4,
+        compiler_params=PARAMS,
+        cost_estimate=cost(
+            sum(2 * rows * width * left.shape[1] for left, _ in pairs), 6 * rows * width
+        ),
+        name="product_parts",
+    )(*[array for pair in pairs for array in pair], sent, *after)
+
+
+def mix_kernel(tokens_ref, gain_ref, *refs):
+    parts, (mixed_ref, hidden_ref) = refs[:4], refs[-2:]
+    mixed = tokens_ref[...].astype(jnp.float32) + total_of([ref[...] for ref in parts])
+    inv = lax.rsqrt(jnp.mean(mixed * mixed, axis=-1, keepdims=True) + EPS)
+    mixed_ref[...] = mixed
+    hidden_ref[...] = (mixed * inv * gain_ref[...]).astype(jnp.bfloat16)
+
+
+def mix(tokens, gain, parts, after):
+    rows, d = tokens.shape
+    return pl.pallas_call(
+        mix_kernel,
+        out_shape=(
+            jax.ShapeDtypeStruct((rows, d), jnp.float32),
+            jax.ShapeDtypeStruct((rows, d), jnp.bfloat16),
+        ),
+        in_specs=[VMEM] * 6 + [ANY] * len(after),
+        out_specs=(VMEM,) * 2,
+        compiler_params=PARAMS,
+        cost_estimate=cost(1e6, 16 * rows * d),
+        name="mix",
+    )(tokens, gain.reshape(1, d), *parts, *after)
+
+
+def norm_back(grad_in, values, gain):
+    inv = lax.rsqrt(jnp.mean(values * values, axis=-1, keepdims=True) + EPS)
+    unit = values * inv
+    scaled = grad_in * gain
+    return inv * (scaled - unit * jnp.mean(scaled * unit, axis=-1, keepdims=True)), unit
+
+
+def mix_back_kernel(grad_ref, mixed_ref, gain_ref, *refs):
+    parts, (total_ref, low_ref, part_ref) = refs[:4], refs[-3:]
+    grad_in = total_of([ref[...] for ref in parts])
+    back, unit = norm_back(grad_in, mixed_ref[...], gain_ref[...])
+    total = grad_ref[...].astype(jnp.float32) + back
+    total_ref[...] = total
+    low_ref[...] = total.astype(jnp.bfloat16)
+    part_ref[...] = jnp.sum(grad_in * unit, axis=0, keepdims=True)
+
+
+def mix_back(grad, mixed, gain, parts, after):
+    rows, d = grad.shape
+    return pl.pallas_call(
+        mix_back_kernel,
+        out_shape=(
+            jax.ShapeDtypeStruct((rows, d), jnp.float32),
+            jax.ShapeDtypeStruct((rows, d), jnp.bfloat16),
+            jax.ShapeDtypeStruct((1, d), jnp.float32),
+        ),
+        in_specs=[VMEM] * 7 + [ANY] * len(after),
+        out_specs=(VMEM,) * 3,
+        compiler_params=PARAMS,
+        cost_estimate=cost(1e6, 20 * rows * d),
+        name="mix_back",
+    )(grad, mixed, gain.reshape(1, d), *parts, *after)
+
+
+def hidden_grad_kernel(with_sent, low_ref, query_ref, kv_ref, hidden_ref, *refs):
     low = low_ref[...]
     grad = dot(low[:, :256], query_ref[...], 1, 1) + dot(low[:, 256:], kv_ref[...], 1, 1)
-    part = jnp.sum(grad * hidden_ref[...].astype(jnp.float32), axis=0, keepdims=True)
-
-    @pl.when(i == 0)
-    def _():
-        gain_ref[...] = jnp.broadcast_to(part, gain_ref.shape)
-
-    @pl.when(i > 0)
-    def _():
-        gain_ref[...] += part
-
-    @pl.when(i < 2)
-    def _():
-        own_ref[...] = grad.astype(jnp.bfloat16)
-
-    @pl.when(i >= 2)
-    def _():
-        other_ref[...] = grad.astype(jnp.bfloat16)
-
-
-def hidden_grad(low, w_query, w_key_value, hidden):
+    refs[-1][...] = jnp.sum(grad * hidden_ref[...].astype(jnp.float32), axis=0, keepdims=True)
+    if with_sent:
+        grad += refs[0][...].astype(jnp.float32)
+        rows = refs[1].shape[0]
+        for k, out_ref in enumerate(refs[1:-1]):
+            out_ref[...] = grad[k * rows : (k + 1) * rows].astype(jnp.bfloat16)
+    else:
+        refs[0][...] = grad.astype(jnp.bfloat16)
+
+
+def hidden_grad(low, w_query, w_key_value, hidden, sent=None, after=()):
     rows, d = hidden.shape
-    block = rows // 4
-    return pl.pallas_call(
-        hidden_grad_kernel,
+    block = d // 4
+    wide = pl.BlockSpec((rows, block), lambda i: (0, i))
+    gain = jax.ShapeDtypeStruct((1, d), jnp.float32)
+    if sent is None:
+        shapes = (jax.ShapeDtypeStruct((rows, d), jnp.bfloat16), gain)
+        outs, extra = (wide,), ()
+    else:
+        shapes = (jax.ShapeDtypeStruct((rows // 4, d), jnp.bfloat16),) * 4 + (gain,)
+        outs, extra = (pl.BlockSpec((rows // 4, block), lambda i: (0, i)),) * 4, (sent,)
+
+    def kernel(*refs):
+        refs = refs[: 4 + len(extra)] + refs[4 + len(extra) + len(after) :]
+        hidden_grad_kernel(sent is not None, *refs)
+
+    return pl.pallas_call(
+        kernel,
         grid=(4,),
-        out_shape=(
-            jax.ShapeDtypeStruct((rows // 2, d), jnp.bfloat16),
-            jax.ShapeDtypeStruct((rows // 2, d), jnp.bfloat16),
-            jax.ShapeDtypeStruct((8, d), jnp.float32),
-        ),
+        out_shape=shapes,
         in_specs=[
-            pl.BlockSpec((block, 384), lambda i: (i, 0)),
-            pl.BlockSpec((d, 256), lambda i: (0, 0), pipeline_mode=pl.Buffered(1)),
-            pl.BlockSpec((d, 128), lambda i: (0, 0), pipeline_mode=pl.Buffered(1)),
-            pl.BlockSpec((block, d), lambda i: (i, 0)),
-        ],
-        out_specs=(
-            pl.BlockSpec((block, d), lambda i: (jnp.minimum(i, 1), 0)),
-            pl.BlockSpec((block, d), lambda i: (jnp.maximum(i, 2) - 2, 0)),
-            pl.BlockSpec((8, d), lambda i: (0, 0)),
-        ),
+            pl.BlockSpec((rows, 384), lambda i: (0, 0), pipeline_mode=pl.Buffered(1)),
+            pl.BlockSpec((block, 256), lambda i: (i, 0)),
+            pl.BlockSpec((block, 128), lambda i: (i, 0)),
+            wide,
+        ]
+        + [wide] * len(extra)
+        + [ANY] * len(after),
+        out_specs=outs + (pl.BlockSpec((1, block), lambda i: (0, i)),),
         compiler_params=PARAMS,
         cost_estimate=cost(2 * rows * d * 384, 4 * rows * d),
         name="hidden_grad",
-    )(low, w_query, w_key_value, hidden)
-
-
-def mlp_kernel(hidden_ref, grad_act_ref, gate_ref, up_ref, act_ref, both_ref, own_ref, other_ref):
-    i = pl.program_id(0)
+    )(low, w_query, w_key_value, hidden, *extra, *after)
+
+
+def mlp_kernel(hidden_ref, grad_act_ref, gate_ref, up_ref, act_ref, both_ref, *refs):
     hidden = hidden_ref[...]
     gate = dot(hidden, gate_ref[...])
     up = dot(hidden, up_ref[...])
@@ -502,46 +678,30 @@
     width = gate.shape[1]
     both_ref[:, :width] = grad_gate
     both_ref[:, width:] = grad_up
-    back = (dot(grad_gate, gate_ref[...], 1, 1) + dot(grad_up, up_ref[...], 1, 1)).astype(
-        jnp.bfloat16
-    )
-
-    @pl.when(i < 2)
-    def _():
-        own_ref[...] = back
-
-    @pl.when(i >= 2)
-    def _():
-        other_ref[...] = back
-
-
-def mlp(hidden, grad_act, w_gate, w_up):
+    if refs:
+        refs[0][...] = (
+            dot(grad_gate, gate_ref[...], 1, 1) + dot(grad_up, up_ref[...], 1, 1)
+        ).astype(jnp.bfloat16)
+
+
+def mlp(hidden, grad_act, w_gate, w_up, with_back):
     rows, d = hidden.shape
-    block = rows // 4
+    block = rows // 2
     width = w_gate.shape[1]
+    widths = (width, 2 * width) + ((d,) if with_back else ())
     return pl.pallas_call(
         mlp_kernel,
         grid=(rows // block,),
-        out_shape=(
-            jax.ShapeDtypeStruct((rows, width), jnp.bfloat16),
-            jax.ShapeDtypeStruct((rows, 2 * width), jnp.bfloat16),
-            jax.ShapeDtypeStruct((rows // 2, d), jnp.bfloat16),
-            jax.ShapeDtypeStruct((rows // 2, d), jnp.bfloat16),
-        ),
+        out_shape=tuple(jax.ShapeDtypeStruct((rows, n), jnp.bfloat16) for n in widths),
         in_specs=[
             pl.BlockSpec((block, d), lambda i: (i, 0)),
             pl.BlockSpec((block, width), lambda i: (i, 0)),
             pl.BlockSpec((d, width), lambda i: (0, 0), pipeline_mode=pl.Buffered(1)),
             pl.BlockSpec((d, width), lambda i: (0, 0), pipeline_mode=pl.Buffered(1)),
         ],
-        out_specs=(
-            pl.BlockSpec((block, width), lambda i: (i, 0)),
-            pl.BlockSpec((block, 2 * width), lambda i: (i, 0)),
-            pl.BlockSpec((block, d), lambda i: (jnp.minimum(i, 1), 0)),
-            pl.BlockSpec((block, d), lambda i: (jnp.maximum(i, 2) - 2, 0)),
-        ),
-        compiler_params=PARAMS,
-        cost_estimate=cost(10 * rows * width * d, 12 * rows * d),
+        out_specs=tuple(pl.BlockSpec((block, n), lambda i: (i, 0)) for n in widths),
+        compiler_params=PARAMS,
+        cost_estimate=cost((8 if with_back else 4) * rows * width * d, 12 * rows * d),
         name="mlp",
     )(hidden, grad_act, w_gate, w_up)
 
@@ -576,11 +736,6 @@
         cost_estimate=cost(4 * rows * d * 384, 4 * rows * d),
         name="project_qkv",
     )(hidden, w_query, w_key_value, cos_rows, sin_rows)
-
-
-def norm_back(grad_in, unit_rows, inv_rms, gain):
-    scaled = grad_in * gain
-    return inv_rms * (scaled - unit_rows * jnp.mean(scaled * unit_rows, axis=-1, keepdims=True))
 
 
 def all_sum(values):
@@ -671,10 +826,21 @@
 
     residual = tokens.astype(jnp.float32)
     inv_one = lax.rsqrt(jnp.mean(residual * residual, axis=-1, keepdims=True) + EPS)
-    unit_one = residual * inv_one
-    hidden_one = jnp.concatenate(gather((unit_one * attn_gain).astype(jnp.bfloat16)))
-    qkv = project_qkv(hidden_one, w_query, w_key_value, cos_gathered, sin_gathered)
-    qkv = jnp.pad(in_order(qkv, core, x), ((0, padded_rows - group_rows), (0, 0)))
+    hidden_one = (residual * inv_one * attn_gain).astype(jnp.bfloat16)
+    *hidden_one, grad_copy = gather(hidden_one, (w_query, w_key_value), (out_grad,))
+    qkv = in_order(
+        *[
+            project_qkv(half, w_query, w_key_value, cos_rows, sin_rows)
+            for half, cos_rows, sin_rows in zip(
+                hidden_one,
+                (cos_gathered[:half_rows], cos_gathered[half_rows:]),
+                (sin_gathered[:half_rows], sin_gathered[half_rows:]),
+            )
+        ],
+        core,
+        x,
+    )
+    qkv = jnp.pad(qkv, ((0, padded_rows - group_rows), (0, 0)))
     near_rows = qkv[:long_rows, 256:]
     ring_rows = jnp.concatenate(
         [near_rows, send(near_rows, Y_LOW), send(near_rows, Y_HIGH), send(near_rows, Y_FAR)]
@@ -682,40 +848,47 @@
     far_rows = jnp.concatenate(
         [ring_rows, send(ring_rows, Z_DOWN), send(ring_rows, Z_FAR), send(ring_rows, Z_UP)]
     )
-    grad_own, grad_other = gather(out_grad)
+    grad_rows = from_order(
+        lax.all_gather(grad_copy, BOTH, axis=0, tiled=True, axis_index_groups=CHIP_GROUPS), core, x
+    )
     long_q = qkv[:long_rows]
     short_attn, short_lse = short_forward(qkv, start_column)
     long_attn, long_lse = long_forward(
-        long_q, far_rows, far_row, pos_column, (grad_own, w_gate, w_up)
+        long_q, far_rows, far_row, pos_column, (w_down, w_out)
     )
     attn_rows = from_order(
         jnp.concatenate([long_attn, short_attn[: group_rows - long_rows]]), core, x
     )
-
-    def project(left, right):
-        return jnp.dot(left, right, preferred_element_type=jnp.float32).astype(jnp.bfloat16)
-
-    mixed = residual + scatter(
-        project(attn_rows[:half_rows], w_out), project(attn_rows[half_rows:], w_out)
-    )
-    inv_two = lax.rsqrt(jnp.mean(mixed * mixed, axis=-1, keepdims=True) + EPS)
-    unit_two = mixed * inv_two
-    grad_rows = jnp.concatenate([grad_own, grad_other])
-    grad_act = dot(grad_rows, w_down, 1, 1).astype(jnp.bfloat16)
-    hidden_two = jnp.concatenate(gather((unit_two * mlp_gain).astype(jnp.bfloat16)))
-
-    act, grad_both, back_own, back_other = mlp(hidden_two, grad_act, w_gate, w_up)
-    grad_two = scatter(back_own, back_other)
-    down_sum = sum_groups(weight_grad(grad_rows, act), yh, core, native).T
-    both_sum = sum_groups(weight_grad(hidden_two, grad_both), yh, core, native)
-    ff = act.shape[1]
-    down_rows = project(act, w_down)
-    grad_mixed = out_grad.astype(jnp.float32) + norm_back(grad_two, unit_two, inv_two, mlp_gain)
-    mixed_grad_rows = jnp.concatenate(gather(grad_mixed.astype(jnp.bfloat16)))
-    mlp_gain_part = jnp.sum(grad_two * unit_two, axis=0)
-    output = mixed + scatter(down_rows[:half_rows], down_rows[half_rows:], (mixed_grad_rows,))
+    sent = send(product(attn_rows[1], w_out), CORE)
+    parts = product_parts([(attn_rows[0], w_out)], sent)
+    mixed_parts = scatter(parts)
+    grad_act = [product(half, w_down, parts[:1], True) for half in grad_rows]
+    mixed, hidden_two = mix(tokens, mlp_gain, mixed_parts, (*grad_act, w_gate, w_up))
+    hidden_two = gather(hidden_two)
+
+    act_other, both_other, back = mlp(hidden_two[1], grad_act[1], w_gate, w_up, True)
+    act_own, both_own = mlp(hidden_two[0], grad_act[0], w_gate, w_up, False)
+    act, grad_both, ff = (act_own, act_other), (both_own, both_other), act_own.shape[1]
+    parts = product_parts(
+        [(both_own[:, :ff], w_gate), (both_own[:, ff:], w_up)], send(back, CORE), True
+    )
+    hidden_parts = scatter(parts)
+    down_part = weight_grad(grad_rows, act, parts[:1])
+    both_part = weight_grad(hidden_two, grad_both, (down_part,))
+    down_sum = sum_groups(down_part, yh, core, native).T
+    both_sum = sum_groups(both_part, yh, core, native)
+
+    grad_mixed, grad_low, mlp_gain_part = mix_back(
+        out_grad, mixed, mlp_gain, hidden_parts, (both_part,)
+    )
+    down_rows = [product(half, w_down, (grad_low,)) for half in act]
+    mixed_grad_rows = gather(grad_low, down_rows)
+    grad_attn = in_order(
+        *[dot(half, w_out, 1, 1).astype(jnp.bfloat16) for half in mixed_grad_rows], core, x
+    )
+    out_parts = add_parts(down_rows[0], send(down_rows[1], CORE), mixed_grad_rows[1:])
+    output = mixed + total_of(scatter(out_parts))
     output = send(output.astype(jnp.bfloat16), TURN)
-    grad_attn = in_order(dot(mixed_grad_rows, w_out, 1, 1).astype(jnp.bfloat16), core, x)
     grad_attn = jnp.pad(grad_attn, ((0, padded_rows - group_rows), (0, 0)))
     long_dq, far_terms = long_backward(
         long_q,
@@ -727,18 +900,23 @@
         long_lse,
         cos_ordered[:long_rows],
         sin_ordered[:long_rows],
-    )
-    ring = far_terms
-    ring_terms = (
-        (ring[0].astype(jnp.float32) + send(ring[1], Y_LOW).astype(jnp.float32))
-        + (send(ring[2], Y_HIGH).astype(jnp.float32) + send(ring[3], Y_FAR).astype(jnp.float32))
+        out_parts[:1],
+    )
+    ring_terms = total_of(
+        (
+            far_terms[0],
+            send(far_terms[1], Y_LOW),
+            send(far_terms[2], Y_HIGH),
+            send(far_terms[3], Y_FAR),
+        )
     ).astype(jnp.bfloat16)
     near = ring_terms.reshape(4, long_rows, -1)
-    far_grads = (near[0].astype(jnp.float32) + send(near[1], Z_UP).astype(jnp.float32)) + (
-        send(near[2], Z_FAR).astype(jnp.float32) + send(near[3], Z_DOWN).astype(jnp.float32)
-    )
+    far_grads = total_of(
+        (near[0], send(near[1], Z_UP), send(near[2], Z_FAR), send(near[3], Z_DOWN))
+    )
+    out_part = weight_grad(mixed_grad_rows, attn_rows, (long_dq,))
     short_low = short_backward(
-        qkv, start_row, short_attn, grad_attn, short_lse, cos_ordered, sin_ordered
+        qkv, start_row, short_attn, grad_attn, short_lse, cos_ordered, sin_ordered, (out_part,)
     )
     long_dk = turned(far_grads[:, :HEAD_DIM], cos_ordered[:long_rows], -sin_ordered[:long_rows])
     long_low = jnp.concatenate(
@@ -752,14 +930,16 @@
     low_rows = from_order(
         jnp.concatenate([long_low, short_low[: group_rows - long_rows]]), core, x
     )
-    back_own, back_other, attn_gain_part = hidden_grad(
-        low_rows, w_query, w_key_value, hidden_one
-    )
-    grad_one = scatter(back_own, back_other)
-    gains = all_sum(jnp.stack([attn_gain_part[0] / attn_gain, mlp_gain_part]))
-    out_sum = sum_groups(weight_grad(mixed_grad_rows, attn_rows), yh, core, native).T
-    qkv_sum = sum_groups(weight_grad(hidden_one, low_rows), yh, core, native)
-    grad_tokens = grad_mixed + norm_back(grad_one, unit_one, inv_one, attn_gain)
+    back, gain_other = hidden_grad(low_rows[1], w_query, w_key_value, hidden_one[1])
+    last_part = weight_grad(hidden_one, low_rows, (back,), (out_part,))
+    *parts, gain_own = hidden_grad(
+        low_rows[0], w_query, w_key_value, hidden_one[0], send(back, CORE), (last_part,)
+    )
+    grad_parts = scatter(parts)
+    gains = all_sum(jnp.concatenate([(gain_own + gain_other) / attn_gain, mlp_gain_part]))
+    last_sum = sum_groups(last_part, yh, core, native)
+    qkv_sum, out_sum = last_sum[:, :384], last_sum[:, 384:].T
+    grad_tokens = grad_mixed + norm_back(total_of(grad_parts), residual, attn_gain)[0]
     grad_tokens = send(grad_tokens.astype(jnp.bfloat16), TURN)
     return (
         output,

time: 657 us -> 606 us (0.922)
  Pallas kernels: 147 us -> 206 us
  waiting for transfers between devices: 224 us -> 170 us
  starting transfers between devices: 129 us -> 104 us
  matrix products: 25.1 us -> 3.35 us
  local copies, waits for them, and re-layouts: 51.9 us -> 43.3 us
    ppermute x81 -> x73, waiting for transfers between devices: 224 us -> 151 us  [send(): return lax.ppermute(values, BOTH, pairs)]
    pallas_call x6 -> x17, Pallas kernels: 48.7 us -> 103 us  [the longest x5 28.2 us: product(): pl.pallas_call(functools.partial(product_kernel, turned_right), grid=(row...]
    ppermute x81 -> x73, starting transfers between devices: 129 us -> 104 us  [send(): return lax.ppermute(values, BOTH, pairs)]
    reduce_scatter x4 -> x3, waiting for transfers between devices: 0.03 us -> 18.1 us  [sum_groups(): lax.psum_scatter(grad.reshape(-1, width), BOTH, scatter_dimension=0, tile...]
    dot_general x3 -> x0, matrix products: 11.5 us -> none  [project(): jnp.dot(left, right, preferred_element_type=jnp.float32)]
    dot_general x2, matrix products: 13.5 us -> 3.35 us  [dot(): lax.dot_general(left, right, (((left_dim,), (right_dim,)), ((), ())), pre...]
    unnamed x81 -> x92, local copies, waits for them, and re-layouts: 22.9 us -> 19.5 us
  transfers between devices with their start and end apart: 85 -> 77, of which waited for: 33 -> 27; matrix products, arithmetic and copies ran while one was open for 17% -> 14% of each run, Pallas kernels for 17% -> 29%
where the time goes in v4:
time: 606 us; the launch traced here: 594 us
  Pallas kernels  206 us (34%)
  waiting for transfers between devices  170 us (28%)
  starting transfers between devices  104 us (17%)
  other arithmetic  51.5 us (8%)
  local copies, waits for them, and re-layouts  43.3 us (7%)
  between operations  16.2 us (3%)
    ppermute x73, waiting for transfers between devices, send(): return lax.ppermute(values, BOTH, pairs)  151 us
    ppermute x73, starting transfers between devices, send(): return lax.ppermute(values, BOTH, pairs)  104 us
    pallas_call x4, Pallas kernels, weight_grad(): pl.pallas_call(weight_grad_kernel, grid=(8,), out_shape=jax.ShapeDtypeStr...  46.3 us
    pallas_call x5, Pallas kernels, product(): pl.pallas_call(functools.partial(product_kernel, turned_right), grid=(row...  28.2 us
    pallas_call x2, Pallas kernels, mlp(): pl.pallas_call(mlp_kernel, grid=(rows // block,), out_shape=tuple((jax.Sh...  25.8 us
    unnamed x92, local copies, waits for them, and re-layouts  19.5 us
    reduce_scatter x3, waiting for transfers between devices, sum_groups(): lax.psum_scatter(grad.reshape(-1, width), BOTH, scatter_dimension=0, tile...  18.1 us
    pallas_call x1, Pallas kernels, long_backward(): pl.pallas_call(long_backward_kernel, out_shape=(jax.ShapeDtypeStruct((2 *...  17.2 us
  transfers between devices with their start and end apart: 77, of which 27 were waited for; matrix products, arithmetic and copies ran while one was open for 14% of the time, Pallas kernels for 29%

profile of v4, /device:TPU:1, one launch (start us, length us, event | category | flops | bytes accessed | tf_op | source)
XLA Modules:
  0.0 594.2 jit_solution(15511383563669828728)
XLA Ops:
  25.2 9.0 %collective-permute-done.6.refs_6_.grad_ref = bf16[136,2048]{1,0:T(8,128)(2,1)S(1)} collective-permute-done((bf16[136,2048]{1,0:T(8,128)(2,1)}, bf16[136,2048]{1,0:T(8,128)(2,1)S(1)}, u32[]{:S(2)}, u32[]{:S(2)}) %collective-permute-start.6) | collective-permute-done | bytes 557088 | tf_op jit(solution)/shard_map/ppermute | solution.py:78
  36.9 10.4 %collective-permute-done.1.refs_1_ = bf16[136,2048]{1,0:T(8,128)(2,1)} collective-permute-done((bf16[136,2048]{1,0:T(8,128)(2,1)}, bf16[136,2048]{1,0:T(8,128)(2,1)}, u32[]{:S(2)}, u32[]{:S(2)}) %collective-permute-start.1) | collective-permute-done | bytes 557088 | tf_op jit(solution)/shard_map/ppermute | solution.py:78
  96.6 9.2 %collective-permute-done.12 = bf16[1024,128]{1,0:T(8,128)(2,1)S(1)} collective-permute-done((bf16[1024,128]{1,0:T(8,128)(2,1)S(1)}, bf16[1024,128]{1,0:T(8,128)(2,1)S(1)}, u32[]{:S(2)}, u32[]{:S(2)}) %collective-permute-start.12) | collective-permute-done | bytes 262176 | tf_op jit(solution)/shard_map/ppermute | solution.py:78
  113.0 13.8 %long_forward.1 = (bf16[256,256]{1,0:T(8,128)(2,1)}, f32[2,8,512]{2,1,0:T(8,128)}) custom-call(bf16[256,384]{1,0:T(8,128)(2,1)} %slice.264.q_ref, bf16[4096,128]{1,0:T(8,128)(2,1)} %copy-done.34, s32[4,8,1024]{2,1,0:T(8,128)} %broadcast_in_dim.129.far_pos_ref, s32[256,128]{1,0:T(8,128)} %broadcast_in_dim.132.pos_ref, ...), custom_call_target="tpu_custom_call" | custom-call | flops 10000000000 | bytes 2000000 | tf_op jit(solution)/shard_map/long_forward/pallas_call | solution.py:263
  134.0 7.0 %collective-permute-done.17.refs_2_ = bf16[544,2048]{1,0:T(8,128)(2,1)S(1)} collective-permute-done((bf16[544,2048]{1,0:T(8,128)(2,1)}, bf16[544,2048]{1,0:T(8,128)(2,1)S(1)}, u32[]{:S(2)}, u32[]{:S(2)}) %collective-permute-start.17) | collective-permute-done | bytes 2228256 | tf_op jit(solution)/shard_map/ppermute | solution.py:78
  174.4 7.0 %collective-permute-done.21.refs_6_.gate_ref.refs_1_ = bf16[2048,1024]{1,0:T(8,128)(2,1)} collective-permute-done((bf16[2048,1024]{1,0:T(8,128)(2,1)}, bf16[2048,1024]{1,0:T(8,128)(2,1)}, u32[]{:S(2)}, u32[]{:S(2)}) %collective-permute-start.21) | collective-permute-done | bytes 4194336 | tf_op jit(solution)/shard_map/ppermute | solution.py:78
  189.0 13.0 %collective-permute-done.23.refs_1_ = bf16[136,2048]{1,0:T(8,128)(2,1)S(1)} collective-permute-done((bf16[136,2048]{1,0:T(8,128)(2,1)}, bf16[136,2048]{1,0:T(8,128)(2,1)S(1)}, u32[]{:S(2)}, u32[]{:S(2)}) %collective-permute-start.23) | collective-permute-done | bytes 557088 | tf_op jit(solution)/shard_map/ppermute | solution.py:78
  204.2 11.8 %collective-permute-done.25.refs_3_ = bf16[136,2048]{1,0:T(8,128)(2,1)S(1)} collective-permute-done((bf16[136,2048]{1,0:T(8,128)(2,1)}, bf16[136,2048]{1,0:T(8,128)(2,1)S(1)}, u32[]{:S(2)}, u32[]{:S(2)}) %collective-permute-start.25) | collective-permute-done | bytes 557088 | tf_op jit(solution)/shard_map/ppermute | solution.py:78
  226.8 15.3 %mlp.3 = (bf16[544,1024]{1,0:T(8,128)(2,1)}, bf16[544,2048]{1,0:T(8,128)(2,1)}, bf16[544,2048]{1,0:T(8,128)(2,1)}) custom-call(bf16[544,2048]{1,0:T(8,128)(2,1)} %copy-done.36, bf16[544,1024]{1,0:T(8,128)(2,1)} %product.7.refs_5_.grad_act_ref, bf16[2048,1024]{1,0:T(8,128)(2,1)} %collective-permute-done.21.refs_6_.gate_ref.refs_1_, ...), custom_call_target="tpu_custom_call" | custom-call | flops 9126805504 | bytes 13369344 | tf_op jit(solution)/shard_map/mlp/pallas_call | solution.py:692
  242.5 10.5 %mlp.2 = (bf16[544,1024]{1,0:T(8,128)(2,1)}, bf16[544,2048]{1,0:T(8,128)(2,1)}) custom-call(bf16[544,2048]{1,0:T(8,128)(2,1)} %bitcast.72, bf16[544,1024]{1,0:T(8,128)(2,1)} %product.6.refs_4_.grad_act_ref, bf16[2048,1024]{1,0:T(8,128)(2,1)} %collective-permute-done.21.refs_6_.gate_ref.refs_1_, bf16[2048,1024]{1,0:T(8,128)(2,1)} %collective-permute-done.22.refs_7_.up_ref.refs_3_), custom_call_target="tpu_custom_call" | custom-call | flops 4563402752 | bytes 13369344 | tf_op jit(solution)/shard_map/mlp/pallas_call | solution.py:692
  257.5 9.4 %product_parts.3 = (bf16[136,2048]{1,0:T(8,128)(2,1)}, bf16[136,2048]{1,0:T(8,128)(2,1)}, bf16[136,2048]{1,0:T(8,128)(2,1)}, bf16[136,2048]{1,0:T(8,128)(2,1)}) custom-call(bf16[544,1024]{1,0:T(8,128)(2,1)} %get-tuple-element.134.refs_0_, bf16[2048,1024]{1,0:T(8,128)(2,1)} %collective-permute-done.21.refs_6_.gate_ref.refs_1_, ...), custom_call_target="tpu_custom_call" | custom-call | flops 4563402752 | bytes 6684672 | tf_op jit(solution)/shard_map/product_parts/pallas_call | solution.py:548
  269.6 11.5 %weight_grad.4.refs_0_ = bf16[2048,1024]{1,0:T(8,128)(2,1)} custom-call(bf16[544,2048]{1,0:T(8,128)(2,1)} %get-tuple-element.132.left_ref, bf16[544,2048]{1,0:T(8,128)(2,1)} %get-tuple-element.131.left_ref.other_left_ref, bf16[544,1024]{1,0:T(8,128)(2,1)} %get-tuple-element.58.right_ref.left_ref, ...), custom_call_target="tpu_custom_call" | custom-call | flops 7563402752 | bytes 12845056 | tf_op jit(solution)/shard_map/weight_grad/pallas_call | solution.py:433
  281.1 18.2 %weight_grad.5.refs_4_ = bf16[2048,2048]{1,0:T(8,128)(2,1)} custom-call(bf16[544,2048]{1,0:T(8,128)(2,1)} %bitcast.73, bf16[544,2048]{1,0:T(8,128)(2,1)} %copy-done.36, bf16[544,2048]{1,0:T(8,128)(2,1)} %get-tuple-element.59.right_ref, bf16[544,2048]{1,0:T(8,128)(2,1)} %get-tuple-element.65.other_right_ref, bf16[2048,1024]{1,0:T(8,128)(2,1)} %weight_grad.4.refs_0_), custom_call_target="tpu_custom_call" | custom-call | flops 12126806016 | bytes 21233664 | tf_op jit(solution)/shard_map/weight_grad/pallas_call | solution.py:433
  314.1 6.7 %product.8.refs_4_.left_ref = bf16[544,2048]{1,0:T(8,128)(2,1)} custom-call(bf16[544,1024]{1,0:T(8,128)(2,1)} %get-tuple-element.58.right_ref.left_ref, bf16[1024,2048]{1,0:T(8,128)(2,1)} %collective-permute-done.15.refs_0_.right_ref, bf16[136,2048]{1,0:T(8,128)(2,1)} %get-tuple-element.67.refs_0_), custom_call_target="tpu_custom_call" | custom-call | flops 2281701376 | bytes 6422528 | tf_op jit(solution)/shard_map/product/pallas_call | solution.py:512
  320.8 12.9 %collective-permute-done.34.refs_3_ = bf16[136,2048]{1,0:T(8,128)(2,1)S(1)} collective-permute-done((bf16[136,2048]{1,0:T(8,128)(2,1)}, bf16[136,2048]{1,0:T(8,128)(2,1)S(1)}, u32[]{:S(2)}, u32[]{:S(2)}) %collective-permute-start.34) | collective-permute-done | bytes 557088 | tf_op jit(solution)/shard_map/ppermute | solution.py:78
  359.6 17.2 %long_backward.1 = (bf16[256,256]{1,0:T(8,128)(2,1)}, bf16[4,1024,128]{2,1,0:T(8,128)(2,1)}) custom-call(bf16[256,384]{1,0:T(8,128)(2,1)} %slice.264.q_ref, bf16[4096,128]{1,0:T(8,128)(2,1)} %copy-done.34, s32[4096,128]{1,0:T(8,128)} %broadcast_in_dim.134.far_pos_ref, s32[8,256]{1,0:T(8,128)} %broadcast_in_dim.135.pos_ref, ...), custom_call_target="tpu_custom_call" | custom-call | flops 12999999488 | bytes 3000000 | tf_op jit(solution)/shard_map/long_backward/pallas_call | solution.py:399
  381.3 7.6 %weight_grad.6.refs_0_ = bf16[2048,256]{1,0:T(8,128)(2,1)} custom-call(bf16[544,2048]{1,0:T(8,128)(2,1)} %bitcast.69, bf16[544,2048]{1,0:T(8,128)(2,1)} %collective-permute-done.35.refs_0_.other_left_ref, bf16[544,256]{1,0:T(8,128)(2,1)} %get-tuple-element.153.refs_0_.right_ref, bf16[544,256]{1,0:T(8,128)(2,1)} %get-tuple-element.152.left_ref.other_right_ref, ...), custom_call_target="tpu_custom_call" | custom-call | flops 4140850688 | bytes 6553600 | tf_op jit(solution)/shard_map/weight_grad/pallas_call | solution.py:433
  397.1 10.5 %short_backward.1 = bf16[896,384]{1,0:T(8,128)(2,1)} custom-call(bf16[1152,384]{1,0:T(8,128)(2,1)} %pad.8.qkv_ref, s32[8,896]{1,0:T(8,128)} %broadcast_in_dim.136.start_ref, bf16[896,256]{1,0:T(8,128)(2,1)} %get-tuple-element.50.attn_ref, bf16[1152,256]{1,0:T(8,128)(2,1)} %pad.9.grad_ref, f32[7,8,512]{2,1,0:T(8,128)} %get-tuple-element.76.lse_ref, ...), custom_call_target="tpu_custom_call" | custom-call | flops 7000000000 | bytes 2000000 | tf_op jit(solution)/shard_map/short_backward/pallas_call | solution.py:332
  416.2 9.0 %weight_grad.7.refs_5_ = bf16[2048,640]{1,0:T(8,128)(2,1)} custom-call(bf16[544,2048]{1,0:T(8,128)(2,1)} %bitcast.66, bf16[544,2048]{1,0:T(8,128)(2,1)} %collective-permute-done.8.hidden_ref.refs_3_.other_left_ref, bf16[544,384]{1,0:T(8,128)(2,1)} %get-tuple-element.147.right_ref.refs_0_, bf16[544,384]{1,0:T(8,128)(2,1)} %get-tuple-element.146.refs_0_.other_right_ref, ...), custom_call_target="tpu_custom_call" | custom-call | flops 4711276032 | bytes 7602176 | tf_op jit(solution)/shard_map/weight_grad/pallas_call | solution.py:433
  443.9 10.8 %collective-permute-done.37 = bf16[136,2048]{1,0:T(8,128)(2,1)S(1)} collective-permute-done((bf16[136,2048]{1,0:T(8,128)(2,1)}, bf16[136,2048]{1,0:T(8,128)(2,1)S(1)}, u32[]{:S(2)}, u32[]{:S(2)}) %collective-permute-start.37) | collective-permute-done | bytes 557088 | tf_op jit(solution)/shard_map/ppermute | solution.py:78
  478.6 14.2 %collective-permute-done.48 = bf16[136,2048]{1,0:T(8,128)(2,1)S(1)} collective-permute-done((bf16[136,2048]{1,0:T(8,128)(2,1)}, bf16[136,2048]{1,0:T(8,128)(2,1)S(1)}, u32[]{:S(2)}, u32[]{:S(2)}) %collective-permute-start.48) | collective-permute-done | bytes 557088 | tf_op jit(solution)/shard_map/ppermute | solution.py:78
  502.8 7.2 %collective-permute-start.50 = (bf16[136,2048]{1,0:T(8,128)(2,1)}, bf16[136,2048]{1,0:T(8,128)(2,1)}, u32[]{:S(2)}, u32[]{:S(2)}) collective-permute-start(bf16[136,2048]{1,0:T(8,128)(2,1)} %fusion.11), channel_id=1, source_target_pairs={{0,0},{1,1},{2,2},{3,3},{4,8},{5,9},{6,10},{7,11},{8,4},{9,5},{10,... | collective-permute-start | bytes 1671176 | tf_op jit(solution)/shard_map/ppermute | solution.py:78
  523.4 18.1 %reduce-scatter.6.cloned.1.call-done = bf16[512,2048]{1,0:T(8,128)(2,1)} async-done(((bf16[2048,2048]{1,0:T(8,128)(2,1)}), bf16[512,2048]{1,0:T(8,128)(2,1)}) %reduce-scatter.6.cloned.1.call-update) | async-done | bytes 2097168 | tf_op jit(solution)/shard_map/reduce_scatter | solution.py:121
  558.6 15.8 %collective-permute-done.65 = bf16[256,2048]{1,0:T(8,128)(2,1)} collective-permute-done((bf16[256,2048]{1,0:T(8,128)(2,1)S(1)}, bf16[256,2048]{1,0:T(8,128)(2,1)}, u32[]{:S(2)}, u32[]{:S(2)}) %collective-permute-start.65) | collective-permute-done | bytes 1048608 | tf_op jit(solution)/shard_map/ppermute | solution.py:78
  (347 shorter events, 301.9 us)
Async XLA Ops:
  7.2 143.2 %all-gather.2.cloned.1.call-start = ((), (), s32[]{:S(2)}) async-start(), calls=%async_computation.3 | async-start | bytes 5013504 | tf_op jit(solution)/shard_map/all_gather | solution.py:852
  24.5 26.7 %collective-permute-start.3 = (bf16[136,2048]{1,0:T(8,128)(2,1)}, bf16[136,2048]{1,0:T(8,128)(2,1)}, u32[]{:S(2)}, u32[]{:S(2)}) collective-permute-start(bf16[136,2048]{1,0:T(8,128)(2,1)} %fusion.6.refs_0_), channel_id=1, source_target_pairs={{0,1},{1,2},{2,3},{3,0},{4,5},{5,6},{6,7},{7,4},{8,9},{9,10},{10,1... | collective-permute-start | bytes 1671176 | tf_op jit(solution)/shard_map/ppermute | solution.py:78
  36.9 74.6 %collective-permute-start.15 = (bf16[1024,2048]{1,0:T(8,128)(2,1)}, bf16[1024,2048]{1,0:T(8,128)(2,1)}, u32[]{:S(2)}, u32[]{:S(2)}) collective-permute-start(bf16[1024,2048]{1,0:T(8,128)(2,1)} %param.24), channel_id=1, source_target_pairs={{0,4},{1,5},{2,6},{3,7},{4,12},{5,13},{6,14},{7,15},{8,0},{9,1},{1... | collective-permute-start | bytes 12582920 | tf_op jit(solution)/shard_map/ppermute | solution.py:78
  47.3 63.2 %collective-permute-start.16 = (bf16[256,2048]{1,0:T(8,128)(2,1)}, bf16[256,2048]{1,0:T(8,128)(2,1)S(1)}, u32[]{:S(2)}, u32[]{:S(2)}) collective-permute-start(bf16[256,2048]{1,0:T(8,128)(2,1)} %param.20), channel_id=1, source_target_pairs={{0,68},{1,69},{2,70},{3,71},{4,12},{5,13},{6,14},{7,15},{8,0},{9,1... | collective-permute-start | bytes 3145736 | tf_op jit(solution)/shard_map/ppermute | solution.py:78
  56.8 436.6 %reduce-scatter.8.cloned.1.call-start = ((), (), s32[]{:S(2)}) async-start(), calls=%async_computation.6 | async-start | bytes 5242880 | tf_op jit(solution)/shard_map/reduce_scatter | solution.py:121
  133.7 47.7 %collective-permute-start.21 = (bf16[2048,1024]{1,0:T(8,128)(2,1)}, bf16[2048,1024]{1,0:T(8,128)(2,1)}, u32[]{:S(2)}, u32[]{:S(2)}) collective-permute-start(bf16[2048,1024]{1,0:T(8,128)(2,1)} %param.22), channel_id=1, source_target_pairs={{0,4},{1,5},{2,6},{3,7},{4,12},{5,13},{6,14},{7,15},{8,0},{9,1},{1... | collective-permute-start | bytes 12582920 | tf_op jit(solution)/shard_map/ppermute | solution.py:78
  133.7 48.9 %collective-permute-start.22 = (bf16[2048,1024]{1,0:T(8,128)(2,1)}, bf16[2048,1024]{1,0:T(8,128)(2,1)}, u32[]{:S(2)}, u32[]{:S(2)}) collective-permute-start(bf16[2048,1024]{1,0:T(8,128)(2,1)} %param.23), channel_id=1, source_target_pairs={{0,68},{1,69},{2,70},{3,71},{4,12},{5,13},{6,14},{7,15},{8,0},{9,1... | collective-permute-start | bytes 12582920 | tf_op jit(solution)/shard_map/ppermute | solution.py:78
  147.0 35.6 %collective-permute-start.18 = (bf16[136,2048]{1,0:T(8,128)(2,1)}, bf16[136,2048]{1,0:T(8,128)(2,1)S(1)}, u32[]{:S(2)}, u32[]{:S(2)}) collective-permute-start(bf16[136,2048]{1,0:T(8,128)(2,1)} %get-tuple-element.52), channel_id=1, source_target_pairs={{0,1},{1,2},{2,3},{3,0},{4,5},{5,6},{6,7},{7,4},{8,9},{9,10},{10,1... | collective-permute-start | bytes 1671176 | tf_op jit(solution)/shard_map/ppermute | solution.py:78
  147.3 35.3 %collective-permute-start.19 = (bf16[136,2048]{1,0:T(8,128)(2,1)}, bf16[136,2048]{1,0:T(8,128)(2,1)S(1)}, u32[]{:S(2)}, u32[]{:S(2)}) collective-permute-start(bf16[136,2048]{1,0:T(8,128)(2,1)} %get-tuple-element.53), channel_id=1, source_target_pairs={{0,2},{1,3},{2,0},{3,1},{4,6},{5,7},{6,4},{7,5},{8,10},{9,11},{10,... | collective-permute-start | bytes 1671176 | tf_op jit(solution)/shard_map/ppermute | solution.py:78
  149.2 33.4 %collective-permute-start.20 = (bf16[136,2048]{1,0:T(8,128)(2,1)}, bf16[136,2048]{1,0:T(8,128)(2,1)S(1)}, u32[]{:S(2)}, u32[]{:S(2)}) collective-permute-start(bf16[136,2048]{1,0:T(8,128)(2,1)} %get-tuple-element.54), channel_id=1, source_target_pairs={{0,3},{1,0},{2,1},{3,2},{4,7},{5,4},{6,5},{7,6},{8,11},{9,8},{10,9... | collective-permute-start | bytes 1671176 | tf_op jit(solution)/shard_map/ppermute | solution.py:78
  188.1 27.9 %collective-permute-start.25 = (bf16[136,2048]{1,0:T(8,128)(2,1)}, bf16[136,2048]{1,0:T(8,128)(2,1)S(1)}, u32[]{:S(2)}, u32[]{:S(2)}) collective-permute-start(bf16[136,2048]{1,0:T(8,128)(2,1)} %get-tuple-element.57.refs_0_), channel_id=1, source_target_pairs={{0,1},{1,2},{2,3},{3,0},{4,5},{5,6},{6,7},{7,4},{8,9},{9,10},{10,1... | collective-permute-start | bytes 1671176 | tf_op jit(solution)/shard_map/ppermute | solution.py:78
  266.9 32.4 %collective-permute-start.28 = (bf16[136,2048]{1,0:T(8,128)(2,1)}, bf16[136,2048]{1,0:T(8,128)(2,1)S(1)}, u32[]{:S(2)}, u32[]{:S(2)}) collective-permute-start(bf16[136,2048]{1,0:T(8,128)(2,1)} %get-tuple-element.62), channel_id=1, source_target_pairs={{0,1},{1,2},{2,3},{3,0},{4,5},{5,6},{6,7},{7,4},{8,9},{9,10},{10,1... | collective-permute-start | bytes 1671176 | tf_op jit(solution)/shard_map/ppermute | solution.py:78
  267.0 32.4 %collective-permute-start.29 = (bf16[136,2048]{1,0:T(8,128)(2,1)}, bf16[136,2048]{1,0:T(8,128)(2,1)S(1)}, u32[]{:S(2)}, u32[]{:S(2)}) collective-permute-start(bf16[136,2048]{1,0:T(8,128)(2,1)} %get-tuple-element.63), channel_id=1, source_target_pairs={{0,2},{1,3},{2,0},{3,1},{4,6},{5,7},{6,4},{7,5},{8,10},{9,11},{10,... | collective-permute-start | bytes 1671176 | tf_op jit(solution)/shard_map/ppermute | solution.py:78
  268.6 30.8 %collective-permute-start.30 = (bf16[136,2048]{1,0:T(8,128)(2,1)}, bf16[136,2048]{1,0:T(8,128)(2,1)S(1)}, u32[]{:S(2)}, u32[]{:S(2)}) collective-permute-start(bf16[136,2048]{1,0:T(8,128)(2,1)} %get-tuple-element.64), channel_id=1, source_target_pairs={{0,3},{1,0},{2,1},{3,2},{4,7},{5,4},{6,5},{7,6},{8,11},{9,8},{10,9... | collective-permute-start | bytes 1671176 | tf_op jit(solution)/shard_map/ppermute | solution.py:78
  308.0 202.0 %reduce-scatter.4.cloned.1.call-start = ((), (), s32[]{:S(2)}) async-start(), calls=%async_computation.4 | async-start | bytes 3276800 | tf_op jit(solution)/shard_map/reduce_scatter | solution.py:121
  425.2 116.3 %reduce-scatter.6.cloned.1.call-start = ((), (), s32[]{:S(2)}) async-start(), calls=%async_computation.5 | async-start | bytes 10485760 | tf_op jit(solution)/shard_map/reduce_scatter | solution.py:121
  428.1 26.7 %collective-permute-start.37 = (bf16[136,2048]{1,0:T(8,128)(2,1)}, bf16[136,2048]{1,0:T(8,128)(2,1)S(1)}, u32[]{:S(2)}, u32[]{:S(2)}) collective-permute-start(bf16[136,2048]{1,0:T(8,128)(2,1)} %get-tuple-element.70), channel_id=1, source_target_pairs={{0,2},{1,3},{2,0},{3,1},{4,6},{5,7},{6,4},{7,5},{8,10},{9,11},{10,... | collective-permute-start | bytes 1671176 | tf_op jit(solution)/shard_map/ppermute | solution.py:78
  465.4 27.4 %collective-permute-start.48 = (bf16[136,2048]{1,0:T(8,128)(2,1)}, bf16[136,2048]{1,0:T(8,128)(2,1)S(1)}, u32[]{:S(2)}, u32[]{:S(2)}) collective-permute-start(bf16[136,2048]{1,0:T(8,128)(2,1)} %get-tuple-element.80), channel_id=1, source_target_pairs={{0,2},{1,3},{2,0},{3,1},{4,6},{5,7},{6,4},{7,5},{8,10},{9,11},{10,... | collective-permute-start | bytes 1671176 | tf_op jit(solution)/shard_map/ppermute | solution.py:78
  502.8 41.4 %collective-permute-start.50 = (bf16[136,2048]{1,0:T(8,128)(2,1)}, bf16[136,2048]{1,0:T(8,128)(2,1)}, u32[]{:S(2)}, u32[]{:S(2)}) collective-permute-start(bf16[136,2048]{1,0:T(8,128)(2,1)} %fusion.11), channel_id=1, source_target_pairs={{0,0},{1,1},{2,2},{3,3},{4,8},{5,9},{6,10},{7,11},{8,4},{9,5},{10,... | collective-permute-start | bytes 1671176 | tf_op jit(solution)/shard_map/ppermute | solution.py:78
  511.9 44.2 %collective-permute-start.62 = (bf16[256,640]{1,0:T(8,128)(2,1)}, bf16[256,640]{1,0:T(8,128)(2,1)}, u32[]{:S(2)}, u32[]{:S(2)}) collective-permute-start(bf16[256,640]{1,0:T(8,128)(2,1)} %get-tuple-element.151), channel_id=1, source_target_pairs={{4,64},{5,65},{6,66},{7,67},{8,76},{9,77},{10,78},{11,79},{20,80},... | collective-permute-start | bytes 983048 | tf_op jit(solution)/shard_map/ppermute | solution.py:78
  513.9 42.2 %collective-permute-start.63 = (bf16[256,640]{1,0:T(8,128)(2,1)}, bf16[256,640]{1,0:T(8,128)(2,1)}, u32[]{:S(2)}, u32[]{:S(2)}) collective-permute-start(bf16[256,640]{1,0:T(8,128)(2,1)} %get-tuple-element.151), channel_id=1, source_target_pairs={{0,64},{1,65},{2,66},{3,67},{12,76},{13,77},{14,78},{15,79},{16,80... | collective-permute-start | bytes 983048 | tf_op jit(solution)/shard_map/ppermute | solution.py:78
  517.1 32.4 %collective-permute-start.72 = (bf16[128,1024]{1,0:T(8,128)(2,1)S(1)}, bf16[128,1024]{1,0:T(8,128)(2,1)S(1)}, u32[]{:S(2)}, u32[]{:S(2)}) collective-permute-start(bf16[128,1024]{1,0:T(8,128)(2,1)S(1)} %select_convert_fusion.1), channel_id=1, source_target_pairs={{0,8},{1,9},{2,10},{3,11},{12,4},{13,5},{14,6},{15,7},{16,24},{17,... | collective-permute-start | bytes 786440 | tf_op jit(solution)/shard_map/ppermute | solution.py:78
  518.4 32.7 %collective-permute-start.61 = (bf16[256,640]{1,0:T(8,128)(2,1)S(1)}, bf16[256,640]{1,0:T(8,128)(2,1)S(1)}, u32[]{:S(2)}, u32[]{:S(2)}) collective-permute-start(bf16[256,640]{1,0:T(8,128)(2,1)S(1)} %get-tuple-element.150), channel_id=1, source_target_pairs={{4,0},{5,1},{6,2},{7,3},{8,12},{9,13},{10,14},{11,15},{20,16},{21,... | collective-permute-start | bytes 983048 | tf_op jit(solution)/shard_map/ppermute | solution.py:78
  544.2 30.3 %collective-permute-start.66 = (bf16[256,2048]{1,0:T(8,128)(2,1)}, bf16[256,2048]{1,0:T(8,128)(2,1)}, u32[]{:S(2)}, u32[]{:S(2)}) collective-permute-start(bf16[256,2048]{1,0:T(8,128)(2,1)} %get-tuple-element.136), channel_id=1, source_target_pairs={{4,64},{5,65},{6,66},{7,67},{8,76},{9,77},{10,78},{11,79},{20,80},... | collective-permute-start | bytes 3145736 | tf_op jit(solution)/shard_map/ppermute | solution.py:78
  (93 other events, 1170.5 us)
Sparse Core Ops, SparseCore 0:
  56.9 31.6 all-gather.1
  308.1 44.7 reduce-scatter.7
  425.3 33.3 reduce-scatter.3
  461.2 80.2 reduce-scatter.5

commit v5 on v2

v5 whole, which is shorter than its diff:
```python
import functools

import jax
import jax.numpy as jnp
from jax import lax
from jax.experimental import pallas as pl
from jax.experimental.pallas import tpu as pltpu
from jax.sharding import PartitionSpec as P

HEAD_DIM = 64
HALF = 128
MASKED = -1e30


EPS = 1e-05
THETA = 500000.0

BOTH = ("dp", "mp")


def place_of(yh, z, c, yl, x):
    return ((yh * 4 + z) * 2 + c) * 8 + yl * 4 + x


def pairs_of(target, sender=lambda yh, z, c, yl, x: True):
    return [
        (place_of(yh, z, c, yl, x), place_of(*target(yh, z, c, yl, x)))
        for yh in range(2)
        for z in range(4)
        for c in range(2)
        for yl in range(2)
        for x in range(4)
        if sender(yh, z, c, yl, x)
    ]


X_UP = pairs_of(lambda yh, z, c, yl, x: (yh, z, c, yl, (x + 1) % 4))
X_DOWN = pairs_of(lambda yh, z, c, yl, x: (yh, z, c, yl, (x + 3) % 4))
X_FAR = pairs_of(lambda yh, z, c, yl, x: (yh, z, c, yl, (x + 2) % 4))
Z_UP = pairs_of(lambda yh, z, c, yl, x: (yh, (z + 1) % 4, c, yl, x))
Z_DOWN = pairs_of(lambda yh, z, c, yl, x: (yh, (z + 3) % 4, c, yl, x))
Z_FAR = pairs_of(lambda yh, z, c, yl, x: (yh, (z + 2) % 4, c, yl, x))
CORE = pairs_of(lambda yh, z, c, yl, x: (yh, z, 1 - c, yl, x))
Y_LOW = pairs_of(lambda yh, z, c, yl, x: (yh, z, c, 1 - yl, x))
Y_HIGH = pairs_of(lambda yh, z, c, yl, x: (1 - yh, z, c, 1 - yl, x))
Y_FAR = pairs_of(lambda yh, z, c, yl, x: (1 - yh, z, c, yl, x))
TURN = pairs_of(lambda yh, z, c, yl, x: (yh, z, yl, c, x))
NATIVE = lambda yh, z, c, yl, x: c == yl
FOREIGN = lambda yh, z, c, yl, x: c != yl
FOREIGN_LOW = pairs_of(lambda yh, z, c, yl, x: (yh, z, c, 1 - yl, x), FOREIGN)
FOREIGN_HIGH = pairs_of(lambda yh, z, c, yl, x: (1 - yh, z, c, 1 - yl, x), FOREIGN)
NATIVE_LOW = pairs_of(lambda yh, z, c, yl, x: (yh, z, c, 1 - yl, x), NATIVE)
NATIVE_HIGH = pairs_of(lambda yh, z, c, yl, x: (1 - yh, z, c, 1 - yl, x), NATIVE)
NATIVE_CORE = pairs_of(lambda yh, z, c, yl, x: (yh, z, 1 - c, yl, x), NATIVE)
WEIGHT_LOW = pairs_of(
    lambda yh, z, c, yl, x: (yh, z, c, 1 - yl, x) if c == yl else (yh, z, 1 - c, yl, x)
)
WEIGHT_HIGH = pairs_of(
    lambda yh, z, c, yl, x: (1 - yh, z, c, 1 - yl, x) if c == yl else (yh, z, 1 - c, yl, x)
)
Z_GROUPS = [
    [place_of(yh, z, c, yl, x) for z in range(4)]
    for yh in range(2)
    for c in range(2)
    for yl in range(2)
    for x in range(4)
]


Y_GROUPS = [
    [place_of(yh, z, c, yl, x) for yh in range(2) for yl in range(2)]
    for z in range(4)
    for c in range(2)
    for x in range(4)
]
CHIP_GROUPS = [
    [place_of(yh, z, c, yl, x) for c in range(2) for x in range(4)]
    for yh in range(2)
    for z in range(4)
    for yl in range(2)
]


def send(values, pairs):
    return lax.ppermute(values, BOTH, pairs)


CHUNKS = ((0, 136),)

VMEM = pl.BlockSpec(memory_space=pltpu.VMEM)
SMEM = pl.BlockSpec(memory_space=pltpu.SMEM)
ANY = pl.BlockSpec(memory_space=pl.ANY)
PARAMS = pltpu.CompilerParams(vmem_limit_bytes=64 * 1024 * 1024)
LASTS = {
    "tables": 6,
    "join": 4,
    "project_qkv": 4,
    "copied": 3,
    "short_forward": 6,
    "long_forward": 13,
    "product": 3,
    "product_parts": 5,
    "arrange": 5,
    "mix": 3,
    "mlp": 10,
    "weight_grad": 5,
    "mix_back": 4,
    "merged_product": 4,
    "merged_back": 3,
    "long_backward": 16,
    "short_backward": 10,
    "turn_far": 2,
    "hidden_grad": 5,
    "gains": 2,
    "gated": 1,
}


def cost(name):
    return pl.CostEstimate(
        flops=int(1.15e9 * LASTS[name]), bytes_accessed=1000, transcendentals=0
    )


def shaped(shape, dtype=jnp.bfloat16):
    return pltpu.HBM(tuple(shape), dtype)


def rows_of(block, width):
    return pl.BlockSpec((block, width), lambda i: (i, 0))


def columns_of(rows, block):
    return pl.BlockSpec((rows, block), lambda i: (0, i))


def once(shape):
    return pl.BlockSpec(tuple(shape), lambda i: (0,) * len(shape), pipeline_mode=pl.Buffered(1))


class Line:
    def __init__(self):
        self.last = ()

    def __call__(self, name, kernel, operands, in_specs, outs, out_specs, scratch=(), **grid):
        after = self.last
        count = len(operands)

        def ordered(*refs):
            kernel(*refs[:count], *refs[count + len(after) :])

        results = pl.pallas_call(
            ordered,
            out_shape=tuple(outs),
            in_specs=list(in_specs) + [ANY] * len(after),
            out_specs=tuple(out_specs),
            scratch_shapes=list(scratch),
            compiler_params=PARAMS,
            cost_estimate=cost(name),
            name=name,
            **grid,
        )(*operands, *after)
        self.last = (min(results, key=lambda array: array.size),)
        return results


def dot(left, right, left_dim=1, right_dim=0):
    return lax.dot_general(
        left, right, (((left_dim,), (right_dim,)), ((), ())), preferred_element_type=jnp.float32
    )


def total_of(parts):
    one, two, three, four = [part.astype(jnp.float32) for part in parts]
    return (one + two) + (three + four)


def scatter(parts):
    return (
        parts[0],
        send(parts[1], X_UP),
        send(parts[2], X_FAR),
        send(parts[3], X_DOWN),
    )


def collect(rows):
    return (rows, send(rows, X_DOWN), send(rows, X_FAR), send(rows, X_UP))


def in_order(pair, core, x):
    half = pair.shape[1]
    start = (4 - x) % 4 * (half // 4)
    pair = lax.dynamic_slice_in_dim(jnp.concatenate([pair, pair], axis=1), start, half, axis=1)
    return jnp.where(core == 0, pair, pair[::-1]).reshape(2 * half, -1)


def from_order(values, core, x):
    half = values.shape[0] // 2
    pair = values.reshape(2, half, -1)
    pair = jnp.where(core == 0, pair, pair[::-1])
    return lax.dynamic_slice_in_dim(
        jnp.concatenate([pair, pair], axis=1), x * (half // 4), half, axis=1
    )


def chunks_of(half):
    cut = half.reshape(4, half.shape[0] // 4, -1)
    return [cut[:, low:high].reshape(4 * (high - low), -1) for low, high in CHUNKS]


def plus(left, right):
    return (left.astype(jnp.float32) + right.astype(jnp.float32)).astype(jnp.bfloat16)


def reduce_near(grad):
    return lax.psum_scatter(
        grad, BOTH, scatter_dimension=0, tiled=True, axis_index_groups=Z_GROUPS
    )


def reduce_y(kept):
    kept = lax.psum_scatter(
        kept, BOTH, scatter_dimension=0, tiled=True, axis_index_groups=Y_GROUPS
    )
    return send(kept, TURN).astype(jnp.float32)


def reduce_ring(grad, z):
    grad = grad.reshape(4, -1, grad.shape[1])
    here, above, far, below = [
        lax.dynamic_index_in_dim(grad, (z + k) % 4, 0, False) for k in range(4)
    ]
    rows = far.shape[0] // 2
    from_below, from_above = send(far[:rows], Z_UP), send(far[rows:], Z_DOWN)
    above = send(jnp.concatenate([plus(above[:rows], from_below), above[rows:]]), Z_UP)
    below = send(jnp.concatenate([below[:rows], plus(below[rows:], from_above)]), Z_DOWN)
    return (
        here.astype(jnp.float32) + above.astype(jnp.float32) + below.astype(jnp.float32)
    ).astype(jnp.bfloat16)


def sum_groups(kept, yh, core, native):
    kept = kept.reshape(2, -1, kept.shape[1])
    near = jnp.where(yh == 0, kept[0], kept[1])
    far = jnp.where(yh == 0, kept[1], kept[0])
    rows = near.shape[0] // 2
    by_low = send(far[:rows], NATIVE_LOW)
    by_high = send(far[rows:], NATIVE_HIGH)
    low = send(jnp.concatenate([near[:rows], plus(near[rows:], by_high)]), FOREIGN_LOW)
    high = send(jnp.concatenate([plus(far[:rows], by_low), far[rows:]]), FOREIGN_HIGH)
    total = near.astype(jnp.float32) + low.astype(jnp.float32) + high.astype(jnp.float32)
    mine = jnp.where(core == 0, total[:rows], total[rows:])
    theirs = jnp.where(core == 0, total[rows:], total[:rows])
    passed = send(theirs.astype(jnp.bfloat16), NATIVE_CORE).astype(jnp.float32)
    return jnp.where(native, mine, passed), (low, high)


def all_sum(values):
    for group in ((CORE,), (X_UP, X_DOWN, X_FAR), (Z_UP, Z_DOWN, Z_FAR), (Y_LOW, Y_HIGH, Y_FAR)):
        values = sum([send(values, pairs) for pairs in group], values)
    return values


def inverse_freq(head_width):
    indices = jnp.arange(head_width // 2, dtype=jnp.float32)
    base_freq = jnp.exp(-jnp.log(THETA) * 2.0 * indices / head_width)
    wavelength = 2.0 * jnp.pi / base_freq
    smooth = (8192.0 / wavelength - 1.0) / 3.0
    blended = (1.0 - smooth) * base_freq / 32.0 + smooth * base_freq
    return jnp.where(
        wavelength < 2048.0, base_freq, jnp.where(wavelength > 8192.0, base_freq / 32.0, blended)
    )


FIRST_PLACE, SECOND_START, THIRD_START, CORE_AT, X_AT, FAR_PLACE = 0, 2, 3, 4, 5, 6


def tables_kernel(rows, facts_ref, freq_ref, *out_refs):
    sign = jnp.where(lax.broadcasted_iota(jnp.int32, (1, 128), 1) % 64 < 32, -1.0, 1.0)
    group_rows, half_rows = rows * 8, rows * 4
    for gathered, (cos_ref, sin_ref) in enumerate((out_refs[:2], out_refs[2:])):
        row = lax.broadcasted_iota(jnp.int32, cos_ref.shape, 0)
        if gathered == 0:
            other = (row >= half_rows).astype(jnp.int32)
            rest = row - other * half_rows
            step = sum([(rest >= k * rows).astype(jnp.int32) for k in (1, 2, 3)])
            core = jnp.where(other == 0, facts_ref[CORE_AT], 1 - facts_ref[CORE_AT])
            row = core * half_rows + ((facts_ref[X_AT] + step) & 3) * rows + rest - step * rows
        packed = row - 2 * HALF
        second, third = facts_ref[SECOND_START], facts_ref[THIRD_START]
        start = jnp.where(packed >= third, third, jnp.where(packed >= second, second, 0))
        own = jnp.where(row < HALF, facts_ref[FIRST_PLACE], facts_ref[FIRST_PLACE + 1])
        position = jnp.where(row < 2 * HALF, own * HALF + (row & (HALF - 1)), packed - start)
        angles = position.astype(jnp.float32) * freq_ref[...]
        cos_ref[...] = jnp.cos(angles)
        sin_ref[...] = jnp.sin(angles) * sign


def turned(values, cos_rows, sin_rows):
    first = lax.broadcasted_iota(jnp.int32, (1, 128), 1) % 64 < 32
    tiles = []
    for at in range(0, values.shape[1], 128):
        tile = values[:, at : at + 128]
        swapped = jnp.where(first, pltpu.roll(tile, 96, 1), pltpu.roll(tile, 32, 1))
        tiles.append(tile * cos_rows + swapped * sin_rows)
    return tiles[0] if len(tiles) == 1 else jnp.concatenate(tiles, axis=1)


def turned_key(values, cos_rows, sin_rows):
    key = lax.broadcasted_iota(jnp.int32, (1, 128), 1) < HEAD_DIM
    return jnp.where(key, turned(values, cos_rows, sin_rows), values)


def join_kernel(count, *refs):
    for k in range(count):
        refs[-1][k] = refs[k][...]


def join(line, pieces):
    count = len(pieces)
    rows, width = pieces[0].shape
    block = width // 4
    (joined,) = line(
        "join",
        functools.partial(join_kernel, count),
        pieces,
        [columns_of(rows, block)] * count,
        [shaped((count, rows, width))],
        [pl.BlockSpec((count, rows, block), lambda i: (0, 0, i))],
        grid=(4,),
    )
    return joined.reshape(count * rows, width)


def qkv_kernel(hidden_ref, query_ref, kv_ref, cos_ref, sin_ref, out_ref):
    hidden = hidden_ref[...]
    cos_rows, sin_rows = cos_ref[...], sin_ref[...]
    out_ref[:, :256] = turned(dot(hidden, query_ref[...]), cos_rows, sin_rows).astype(jnp.bfloat16)
    out_ref[:, 256:] = turned_key(dot(hidden, kv_ref[...]), cos_rows, sin_rows).astype(
        jnp.bfloat16
    )


def project_qkv(line, hidden, w_query, w_key_value, cos_rows, sin_rows, at):
    rows, d = hidden.shape
    block = rows // 2
    table = pl.BlockSpec((block, 128), lambda i: (i + 2 * at, 0))
    return line(
        "project_qkv",
        qkv_kernel,
        (hidden, w_query, w_key_value, cos_rows, sin_rows),
        [rows_of(block, d), once((d, 256)), once((d, 128)), table, table],
        [shaped((rows, 384))],
        [rows_of(block, 384)],
        grid=(2,),
    )[0]


def stacked(block):
    return jnp.concatenate(
        [block[:, h * HEAD_DIM : (h + 1) * HEAD_DIM] for h in range(4)], axis=0
    )


def unstacked(block):
    rows = block.shape[0] // 4
    return jnp.concatenate([block[h * rows : (h + 1) * rows] for h in range(4)], axis=1)


def as_row(column):
    return jnp.transpose(jnp.broadcast_to(column, (column.shape[0], 128)))[:8]


def start_of(row, facts_ref, pack_rows):
    second, third = facts_ref[SECOND_START], facts_ref[THIRD_START]
    start = jnp.where(row >= third, third, jnp.where(row >= second, second, 0))
    return jnp.where(row >= pack_rows, pack_rows, start)


def short_forward_kernel(pack_rows, qkv_ref, facts_ref, attn_ref, lse_ref):
    for i in range(attn_ref.shape[0] // HALF):
        rows = pl.ds((i + 2) * HALF, HALF)
        keys = (i + 1) * HALF
        q = stacked(qkv_ref[rows, :256]) * jnp.bfloat16(HEAD_DIM**-0.5)
        k = qkv_ref[pl.ds(2 * HALF, keys), 256:320]
        v = qkv_ref[pl.ds(2 * HALF, keys), 320:384]
        scores = dot(q, k, 1, 1)
        column = lax.broadcasted_iota(jnp.int32, (HALF, keys), 1)
        row = lax.broadcasted_iota(jnp.int32, (HALF, 1), 0) + i * HALF
        seen = (column <= row) & (column >= start_of(row, facts_ref, pack_rows))
        scores = jnp.where(jnp.concatenate([seen] * 4, axis=0), scores, MASKED)
        top = jnp.max(scores, axis=1, keepdims=True)
        weights = jnp.exp(scores - top)
        total = jnp.sum(weights, axis=1, keepdims=True)
        out = dot(weights.astype(jnp.bfloat16), v) / total
        attn_ref[pl.ds(i * HALF, HALF), :] = unstacked(out).astype(jnp.bfloat16)
        lse_ref[i] = as_row(top + jnp.log(total))


def short_forward(line, qkv, facts, pack_rows):
    rows = qkv.shape[0] - 2 * HALF
    return line(
        "short_forward",
        functools.partial(short_forward_kernel, pack_rows),
        (qkv, facts),
        [VMEM, SMEM],
        [shaped((rows, 256)), shaped((rows // HALF, 8, 4 * HALF), jnp.float32)],
        [VMEM] * 2,
    )


def long_forward_kernel(q_ref, *refs):
    far_refs, (facts_ref, short_ref, attn_ref, lse_ref) = refs[:4], refs[4:]
    within = lax.broadcasted_iota(jnp.int32, (1, HALF), 1)
    blocks = far_refs[0].shape[0] // HALF
    for half in range(2):
        rows = pl.ds(half * HALF, HALF)
        q = stacked(q_ref[rows, :256]) * jnp.bfloat16(HEAD_DIM**-0.5)
        row = lax.broadcasted_iota(jnp.int32, (HALF, 1), 0)
        position = jnp.concatenate([row + facts_ref[FIRST_PLACE + half] * HALF] * 4, axis=0)
        top = jnp.full((4 * HALF, 1), MASKED, jnp.float32)
        total = jnp.zeros((4 * HALF, 1), jnp.float32)
        out = jnp.zeros((4 * HALF, HEAD_DIM), jnp.float32)
        for i, far_ref in enumerate(far_refs):
            scores = dot(q, far_ref[:, :HEAD_DIM], 1, 1)
            key = jnp.concatenate(
                [within + facts_ref[FAR_PLACE + i * blocks + k] * HALF for k in range(blocks)],
                axis=1,
            )
            seen = key <= position
            scores = jnp.where(seen, scores, MASKED)
            now = jnp.maximum(top, jnp.max(scores, axis=1, keepdims=True))
            weights = jnp.where(seen, jnp.exp(scores - now), 0.0)
            scale = jnp.exp(top - now)
            total = total * scale + jnp.sum(weights, axis=1, keepdims=True)
            out = out * scale + dot(weights.astype(jnp.bfloat16), far_ref[:, HEAD_DIM:])
            top = now
        attn_ref[rows, :] = unstacked(out / total).astype(jnp.bfloat16)
        lse_ref[half] = as_row(top + jnp.log(total))
    packed = attn_ref.shape[0] - 2 * HALF
    attn_ref[pl.ds(2 * HALF, packed), :] = short_ref[pl.ds(0, packed), :]


def long_forward(line, q, far, facts, short, rows):
    return line(
        "long_forward",
        long_forward_kernel,
        (q, *far, facts, short),
        [VMEM] * 5 + [SMEM, VMEM],
        [shaped((rows, 256)), shaped((2, 8, 4 * HALF), jnp.float32)],
        [VMEM] * 2,
    )


def grad_terms(q, grad, k, v, seen, lse, delta):
    weights = jnp.where(seen, jnp.exp(dot(k, q, 1, 1) - lse), 0.0)
    grad_scores = (weights * (dot(v, grad, 1, 1) - delta)).astype(jnp.bfloat16)
    return (
        dot(grad_scores, k, 0, 0),
        dot(grad_scores, q),
        dot(weights.astype(jnp.bfloat16), grad),
    )


def row_product(left, right):
    return as_row(
        jnp.sum(left.astype(jnp.float32) * right.astype(jnp.float32), axis=1, keepdims=True)
    )[:1]


def short_backward_kernel(
    pack_rows, qkv_ref, facts_ref, attn_ref, grad_ref, lse_ref, cos_ref, sin_ref, out_ref,
    dk_ref, dv_ref,
):
    blocks = attn_ref.shape[0] // HALF
    scale = HEAD_DIM**-0.5
    dk_ref[...] = jnp.zeros_like(dk_ref)
    dv_ref[...] = jnp.zeros_like(dv_ref)
    for i in range(blocks):
        rows = pl.ds((i + 2) * HALF, HALF)
        keys = (i + 1) * HALF
        q = stacked(qkv_ref[rows, :256]) * jnp.bfloat16(scale)
        k = qkv_ref[pl.ds(2 * HALF, keys), 256:320]
        v = qkv_ref[pl.ds(2 * HALF, keys), 320:384]
        grad = stacked(grad_ref[rows, :])
        delta = row_product(grad, stacked(attn_ref[pl.ds(i * HALF, HALF), :]))
        key = lax.broadcasted_iota(jnp.int32, (keys, HALF), 0)
        query = lax.broadcasted_iota(jnp.int32, (1, HALF), 1) + i * HALF
        seen = (key <= query) & (key >= start_of(query, facts_ref, pack_rows))
        dq, dk, dv = grad_terms(
            q, grad, k, v, jnp.concatenate([seen] * 4, axis=1), lse_ref[i, :1], delta
        )
        out_ref[pl.ds(i * HALF, HALF), :256] = turned(
            unstacked(dq * scale), cos_ref[rows, :], -sin_ref[rows, :]
        ).astype(jnp.bfloat16)
        dk_ref[pl.ds(0, keys), :] += dk
        dv_ref[pl.ds(0, keys), :] += dv
    rows = pl.ds(2 * HALF, blocks * HALF)
    out_ref[:, 256:] = turned_key(
        jnp.concatenate([dk_ref[...], dv_ref[...]], axis=1), cos_ref[rows, :], -sin_ref[rows, :]
    ).astype(jnp.bfloat16)


def short_backward(line, qkv, facts, attn, grad, lse, cos_rows, sin_rows, pack_rows):
    rows = attn.shape[0]
    return line(
        "short_backward",
        functools.partial(short_backward_kernel, pack_rows),
        (qkv, facts, attn, grad, lse, cos_rows, sin_rows),
        [VMEM, SMEM] + [VMEM] * 5,
        [shaped((rows, 384))],
        [VMEM],
        [pltpu.VMEM((rows, HEAD_DIM), jnp.float32)] * 2,
    )[0]


def long_backward_kernel(q_ref, *refs):
    far_refs = refs[:4]
    facts_ref, attn_ref, grad_ref, lse_ref, cos_ref, sin_ref = refs[4:10]
    dq_ref, far_grad_ref, acc_ref = refs[10:]
    scale = HEAD_DIM**-0.5
    count = far_refs[0].shape[0]
    blocks = count // HALF
    queries = []
    for half in range(2):
        rows = pl.ds(half * HALF, HALF)
        grad = stacked(grad_ref[rows, :])
        column = lax.broadcasted_iota(jnp.int32, (1, HALF), 1)
        queries.append(
            (
                stacked(q_ref[rows, :256]) * jnp.bfloat16(scale),
                grad,
                lse_ref[half, :1],
                row_product(grad, stacked(attn_ref[rows, :])),
                jnp.concatenate([column + facts_ref[FIRST_PLACE + half] * HALF] * 4, axis=1),
            )
        )
    within = lax.broadcasted_iota(jnp.int32, (HALF, 1), 0)
    for i, far_ref in enumerate(far_refs):
        k, v = far_ref[:, :HEAD_DIM], far_ref[:, HEAD_DIM:]
        key = jnp.concatenate(
            [within + facts_ref[FAR_PLACE + i * blocks + n] * HALF for n in range(blocks)], axis=0
        )
        sums = []
        for half, (q, grad, lse, delta, position) in enumerate(queries):
            dq, dk, dv = grad_terms(q, grad, k, v, key <= position, lse, delta)
            acc_ref[half] = dq if i == 0 else acc_ref[half] + dq
            sums.append((dk, dv))
        total = jnp.concatenate(
            [sums[0][0] + sums[1][0], sums[0][1] + sums[1][1]], axis=1
        ).astype(jnp.bfloat16)
        rows = count // 4
        for n in range(4):
            far_grad_ref[n, pl.ds(i * rows, rows), :] = total[n * rows : (n + 1) * rows]
    for half in range(2):
        rows = pl.ds(half * HALF, HALF)
        dq_ref[rows, :] = turned(
            unstacked(acc_ref[half] * scale), cos_ref[rows, :], -sin_ref[rows, :]
        ).astype(jnp.bfloat16)


def long_backward(line, q, far, facts, attn, grad, lse, cos_rows, sin_rows):
    return line(
        "long_backward",
        long_backward_kernel,
        (q, *far, facts, attn, grad, lse, cos_rows, sin_rows),
        [VMEM] * 5 + [SMEM] + [VMEM] * 5,
        [shaped((2 * HALF, 256)), shaped((4, *far[0].shape))],
        [VMEM] * 2,
        [pltpu.VMEM((2, 4 * HALF, HEAD_DIM), jnp.float32)],
    )


def product_kernel(turned_right, left_ref, right_ref, out_ref):
    out_ref[...] = dot(left_ref[...], right_ref[...], 1, 1 if turned_right else 0).astype(
        out_ref.dtype
    )


def product(line, left, right, turned_right=False):
    rows, depth = left.shape
    width = right.shape[0] if turned_right else right.shape[1]
    block = rows // 2
    return line(
        "product",
        functools.partial(product_kernel, turned_right),
        (left, right),
        [rows_of(block, depth), once(right.shape)],
        [shaped((rows, width))],
        [rows_of(block, width)],
        grid=(2,),
    )[0]


def product_parts_kernel(terms, turned_right, *refs):
    outs = refs[2 * terms + 1 :]
    total = refs[2 * terms][...].astype(jnp.float32)
    for k in range(terms):
        total += dot(refs[2 * k][...], refs[2 * k + 1][...], 1, 1 if turned_right else 0)
    rows = outs[0].shape[0]
    for k, out_ref in enumerate(outs):
        out_ref[...] = total[k * rows : (k + 1) * rows].astype(jnp.bfloat16)


def product_parts(line, pairs, sent, turned_right=False):
    rows, width = sent.shape
    block = width // 4
    specs = []
    for left, right in pairs:
        specs.append(once(left.shape))
        if turned_right:
            specs.append(rows_of(block, right.shape[1]))
        else:
            specs.append(columns_of(right.shape[0], block))
    return line(
        "product_parts",
        functools.partial(product_parts_kernel, len(pairs), turned_right),
        [array for pair in pairs for array in pair] + [sent],
        specs + [columns_of(rows, block)],
        [shaped((rows // 4, width))] * 4,
        [columns_of(rows // 4, block)] * 4,
        grid=(4,),
    )


def merged(chunks):
    pieces = []
    for k in range(4):
        for (low, high), chunk in zip(CHUNKS, chunks):
            pieces.append(chunk[k * (high - low) : (k + 1) * (high - low)])
    return jnp.concatenate(pieces, axis=0)


def merged_product_kernel(count, with_sent, *refs):
    right = refs[count][...]
    total = dot(merged([ref[...] for ref in refs[:count]]), right)
    outs = refs[count + 1 :]
    if with_sent:
        total += outs[0][...].astype(jnp.float32)
        outs = outs[1:]
    rows = outs[0].shape[0]
    for k, out_ref in enumerate(outs):
        out_ref[...] = total[k * rows : (k + 1) * rows].astype(jnp.bfloat16)


def merged_product(line, chunks, right, sent=None):
    rows = sum([chunk.shape[0] for chunk in chunks])
    depth, width = right.shape
    block = width // 4
    count = 1 if sent is None else 4
    extra = () if sent is None else (sent,)
    return line(
        "merged_product",
        functools.partial(merged_product_kernel, len(chunks), sent is not None),
        (*chunks, right, *extra),
        [once(chunk.shape) for chunk in chunks]
        + [columns_of(depth, block)]
        + [columns_of(rows, block)] * len(extra),
        [shaped((rows // count, width))] * count,
        [columns_of(rows // count, block)] * count,
        grid=(4,),
    )


def merged_back_kernel(count, *refs):
    left = merged([ref[...] for ref in refs[:count]])
    refs[-1][...] = dot(left, refs[count][...], 1, 1).astype(jnp.bfloat16)


def merged_back(line, chunks, right):
    rows = sum([chunk.shape[0] for chunk in chunks])
    return line(
        "merged_back",
        functools.partial(merged_back_kernel, len(chunks)),
        (*chunks, right),
        [VMEM] * (len(chunks) + 1),
        [shaped((rows, right.shape[0]))],
        [VMEM],
    )[0]


def arrange_kernel(facts_ref, rows_ref, *out_refs):
    del facts_ref
    for (low, high), out_ref in zip(CHUNKS, out_refs):
        out_ref[0] = rows_ref[0, low:high, :]


def arrange(line, rows, facts):
    _, count, d = rows.shape
    after = line.last

    def kernel(facts_ref, rows_ref, *refs):
        arrange_kernel(facts_ref, rows_ref, *refs[len(after) :])

    def source(i, facts_ref):
        core = jnp.where(i < 4, facts_ref[CORE_AT], 1 - facts_ref[CORE_AT])
        return core * 4 + (facts_ref[X_AT] + i) % 4, 0, 0

    results = pl.pallas_call(
        kernel,
        grid_spec=pltpu.PrefetchScalarGridSpec(
            num_scalar_prefetch=1,
            grid=(8,),
            in_specs=[pl.BlockSpec((1, count, d), source)] + [ANY] * len(after),
            out_specs=tuple(
                pl.BlockSpec((1, high - low, d), lambda i, facts_ref: (i, 0, 0))
                for low, high in CHUNKS
            ),
        ),
        out_shape=tuple(shaped((8, high - low, d)) for low, high in CHUNKS),
        compiler_params=PARAMS,
        cost_estimate=cost("arrange"),
        name="arrange",
    )(facts, rows, *after)
    return [array.reshape(-1, d) for array in results]


def weight_grad_kernel(count, beside, *refs):
    out_ref, width = refs[-1], refs[count].shape[1]
    total = dot(refs[0][...], refs[count][...], 0, 0)
    for k in range(1, count):
        total += dot(refs[k][...], refs[count + k][...], 0, 0)
    out_ref[:, :width] = total.astype(jnp.bfloat16)
    if beside:
        out_ref[:, width:] = refs[2 * count][...]


def weight_grad(line, left, right, beside=()):
    left = [piece if isinstance(piece, tuple) else (piece, 0) for piece in left]
    columns, width = left[0][0].shape[1], right[0].shape[1]
    whole = width + sum([array.shape[1] for array in beside])

    def out_block(n):
        return pl.BlockSpec((columns // 8, n), lambda i: (i % 4 * 2 + i // 4, 0))

    return line(
        "weight_grad",
        functools.partial(weight_grad_kernel, len(left), len(beside)),
        (*[array for array, _ in left], *right, *beside),
        [
            pl.BlockSpec((part.shape[0], columns // 8), lambda i, at=at: (at, i))
            for (_, at), part in zip(left, right)
        ]
        + [once(array.shape) for array in right]
        + [out_block(array.shape[1]) for array in beside],
        [shaped((columns, whole))],
        [out_block(whole)],
        grid=(8,),
    )[0]


def mix_kernel(low, high, tokens_ref, gain_ref, *refs):
    parts, (mixed_ref, hidden_ref) = refs[:4], refs[4:]
    mixed = tokens_ref[low:high, :].astype(jnp.float32) + total_of([ref[...] for ref in parts])
    inv = lax.rsqrt(jnp.mean(mixed * mixed, axis=-1, keepdims=True) + EPS)
    mixed_ref[...] = mixed
    hidden_ref[...] = (mixed * inv * gain_ref[...]).astype(jnp.bfloat16)


def mix(line, chunk, tokens, gain, parts):
    low, high = chunk
    d = tokens.shape[1]
    return line(
        "mix",
        functools.partial(mix_kernel, low, high),
        (tokens, gain, *parts),
        [VMEM] * 6,
        [shaped((high - low, d), jnp.float32), shaped((high - low, d))],
        [VMEM] * 2,
    )


def norm_back(grad_in, values, gain):
    inv = lax.rsqrt(jnp.mean(values * values, axis=-1, keepdims=True) + EPS)
    unit = values * inv
    scaled = grad_in * gain
    return inv * (scaled - unit * jnp.mean(scaled * unit, axis=-1, keepdims=True)), unit


def mix_back_kernel(low, high, grad_ref, mixed_ref, gain_ref, *refs):
    parts, (total_ref, low_ref, part_ref) = refs[:4], refs[4:]
    grad_in = total_of([ref[...] for ref in parts])
    back, unit = norm_back(grad_in, mixed_ref[...], gain_ref[...])
    total = grad_ref[low:high, :].astype(jnp.float32) + back
    total_ref[...] = total
    low_ref[...] = total.astype(jnp.bfloat16)
    part_ref[...] = jnp.sum(grad_in * unit, axis=0, keepdims=True)


def mix_back(line, chunk, grad, mixed, gain, parts):
    low, high = chunk
    rows, d = mixed.shape
    return line(
        "mix_back",
        functools.partial(mix_back_kernel, low, high),
        (grad, mixed, gain, *parts),
        [VMEM] * 7,
        [shaped((rows, d), jnp.float32), shaped((rows, d)), shaped((1, d), jnp.float32)],
        [VMEM] * 3,
    )


def mlp_kernel(hidden_ref, grad_act_ref, gate_ref, up_ref, act_ref, gate_out_ref, up_out_ref, *refs):
    hidden = hidden_ref[...]
    gate = dot(hidden, gate_ref[...])
    up = dot(hidden, up_ref[...])
    grad_act = grad_act_ref[...].astype(jnp.float32)
    sig = jax.nn.sigmoid(gate)
    silu = gate * sig
    act_ref[...] = (silu * up).astype(jnp.bfloat16)
    grad_gate = (grad_act * up * sig * (1.0 + gate * (1.0 - sig))).astype(jnp.bfloat16)
    grad_up = (grad_act * silu).astype(jnp.bfloat16)
    gate_out_ref[...] = grad_gate
    up_out_ref[...] = grad_up
    if refs:
        i = pl.program_id(0)
        back_ref, acc_ref = refs
        part = dot(grad_gate, gate_ref[...], 1, 1) + dot(grad_up, up_ref[...], 1, 1)

        @pl.when(i == 0)
        def _():
            acc_ref[...] = part

        @pl.when((i > 0) & (i < pl.num_programs(0) - 1))
        def _():
            acc_ref[...] += part

        @pl.when(i == pl.num_programs(0) - 1)
        def _():
            back_ref[...] = (acc_ref[...] + part).astype(jnp.bfloat16)


def mlp(line, hidden, grad_act, at, w_gate, w_up, with_back):
    rows, d = hidden.shape
    width = w_gate.shape[1]
    block = width // 4
    outs = [shaped((rows, width))] * 3
    out_specs = [columns_of(rows, block)] * 3
    if with_back:
        outs.append(shaped((rows, d)))
        out_specs.append(pl.BlockSpec((rows, d), lambda i: (0, 0)))
    return line(
        "mlp",
        mlp_kernel,
        (hidden, grad_act, w_gate, w_up),
        [
            once((rows, d)),
            pl.BlockSpec((rows, block), lambda i: (at, i)),
            columns_of(d, block),
            columns_of(d, block),
        ],
        outs,
        out_specs,
        [pltpu.VMEM((rows, d), jnp.float32)] if with_back else [],
        grid=(4,),
    )


def hidden_grad_kernel(with_sent, low_ref, query_ref, kv_ref, hidden_ref, *refs):
    low = low_ref[...]
    grad = dot(low[:, :256], query_ref[...], 1, 1) + dot(low[:, 256:], kv_ref[...], 1, 1)
    refs[-1][...] = jnp.sum(grad * hidden_ref[...].astype(jnp.float32), axis=0, keepdims=True)
    if with_sent:
        grad += refs[0][...].astype(jnp.float32)
        rows = refs[1].shape[0]
        for k, out_ref in enumerate(refs[1:-1]):
            out_ref[...] = grad[k * rows : (k + 1) * rows].astype(jnp.bfloat16)
    else:
        refs[0][...] = grad.astype(jnp.bfloat16)


def hidden_grad(line, low, w_query, w_key_value, hidden, sent=None):
    rows, d = hidden.shape
    block = d // 4
    count = 1 if sent is None else 4
    extra = () if sent is None else (sent,)
    return line(
        "hidden_grad",
        functools.partial(hidden_grad_kernel, sent is not None),
        (low, w_query, w_key_value, hidden, *extra),
        [once((rows, 384)), rows_of(block, 256), rows_of(block, 128)]
        + [columns_of(rows, block)] * (1 + len(extra)),
        [shaped((rows // count, d))] * count + [shaped((1, d), jnp.float32)],
        [columns_of(rows // count, block)] * count + [columns_of(1, block)],
        grid=(4,),
    )


def copy_kernel(source_ref, out_ref):
    out_ref[...] = source_ref[...]


def copied(line, array):
    rows, width = array.shape
    block = columns_of(rows, width // 4)
    return line(
        "copied", copy_kernel, (array,), [block], [shaped((rows, width))], [block], grid=(4,)
    )[0]


def gate_kernel(*refs):
    del refs


def gated(line, arrays):
    return line(
        "gated",
        gate_kernel,
        arrays,
        [ANY] * len(arrays),
        [shaped(array.shape, array.dtype) for array in arrays],
        [ANY] * len(arrays),
        input_output_aliases={k: k for k in range(len(arrays))},
    )


def gains_kernel(own_ref, other_ref, gain_ref, mlp_ref, out_ref):
    out_ref[:1] = (own_ref[...] + other_ref[...]) / gain_ref[...]
    out_ref[1:] = mlp_ref[...]


def turn_far_kernel(grad_ref, cos_ref, sin_ref, long_ref, short_ref, out_ref):
    rows = pl.ds(0, 2 * HALF)
    packed = out_ref.shape[0] - 2 * HALF
    out_ref[rows, :256] = long_ref[...]
    out_ref[rows, 256:] = turned_key(grad_ref[...], cos_ref[rows, :], -sin_ref[rows, :]).astype(
        jnp.bfloat16
    )
    out_ref[pl.ds(2 * HALF, packed), :] = short_ref[pl.ds(0, packed), :]


def local(
    tokens,
    lengths,
    place,
    attn_gain,
    w_query,
    w_key,
    w_value,
    w_out,
    mlp_gain,
    w_gate,
    w_up,
    w_down,
    out_grad,
):
    rows, d = tokens.shape
    group_rows = rows * 8
    half_rows = rows * 4
    long_rows = 2 * HALF
    pack_rows = group_rows - long_rows
    padded_rows = -(-group_rows // HALF) * HALF
    dp_index, mp_index = lax.axis_index("dp"), lax.axis_index("mp")
    yh, z, core = dp_index // 8, dp_index // 2 % 4, dp_index % 2
    yl, x = mp_index // 4, mp_index % 4
    native = core == yl
    line = Line()
    mlp_gain_row = mlp_gain.reshape(1, d)

    tokens = send(tokens, TURN)
    lengths = send(lengths, TURN)[0]
    w_key_value = send(jnp.concatenate([w_key, w_value], axis=1), WEIGHT_HIGH)
    w_query = send(w_query, WEIGHT_LOW)
    w_out = send(w_out, WEIGHT_HIGH)
    w_gate = send(w_gate, WEIGHT_LOW)
    w_up = send(w_up, WEIGHT_HIGH)
    w_down = send(w_down, WEIGHT_LOW)
    out_grad = send(out_grad, TURN)

    step = jnp.arange(16, dtype=jnp.int32)
    far_yh = jnp.where(step % 4 >= 2, 1 - yh, yh)
    far_yl = jnp.where((step % 4 == 1) | (step % 4 == 2), 1 - yl, yl)
    far_group = (far_yh * 4 + (z + step // 4) % 4) * 2 + far_yl
    far_index = (2 * far_group[:, None] + jnp.arange(2, dtype=jnp.int32)[None, :]).reshape(-1)
    half_ids = jnp.arange(place.shape[0], dtype=jnp.int32)
    far_place = jnp.sum(jnp.where(far_index[:, None] == half_ids[None, :], place, 0), axis=1)
    facts = jnp.concatenate(
        [
            far_place[:2],
            jnp.stack([lengths[0], lengths[0] + lengths[1], core, x]),
            far_place,
        ]
    ).astype(jnp.int32)

    residual = tokens.astype(jnp.float32)
    inv_one = lax.rsqrt(jnp.mean(residual * residual, axis=-1, keepdims=True) + EPS)
    hidden_one = collect((residual * inv_one * attn_gain).astype(jnp.bfloat16))
    freq = jnp.tile(inverse_freq(HEAD_DIM), 4).reshape(1, 128)
    cos_gathered, sin_gathered, cos_ordered, sin_ordered = line(
        "tables",
        functools.partial(tables_kernel, rows),
        (facts, freq),
        [SMEM, VMEM],
        [shaped((n, 128), jnp.float32) for n in (group_rows, group_rows, padded_rows, padded_rows)],
        [VMEM] * 4,
    )
    line.last += (w_query, w_key_value, out_grad)
    hidden_own = join(line, hidden_one)
    hidden_one = (hidden_own, send(hidden_own, CORE))
    qkv = []
    for at, half in enumerate(hidden_one):
        qkv.append(
            project_qkv(line, half, w_query, w_key_value, cos_gathered, sin_gathered, at)
        )
    qkv = in_order(jnp.stack(qkv), core, x)
    qkv = jnp.pad(qkv, ((0, padded_rows - group_rows), (0, 0)))
    near_rows = qkv[:long_rows, 256:]
    ring_rows = jnp.concatenate(
        [near_rows, send(near_rows, Y_LOW), send(near_rows, Y_HIGH), send(near_rows, Y_FAR)]
    )
    far_rows = (
        ring_rows, send(ring_rows, Z_DOWN), send(ring_rows, Z_FAR), send(ring_rows, Z_UP)
    )
    line.last += (ring_rows, w_out, w_down)
    grad_rows = lax.all_gather(
        copied(line, out_grad), BOTH, axis=0, axis_index_groups=CHIP_GROUPS
    )
    short_attn, short_lse = short_forward(line, qkv, facts, pack_rows)
    attn_ordered, long_lse = long_forward(line, qkv, far_rows, facts, short_attn, group_rows)
    attn_rows = from_order(attn_ordered, core, x)
    attn_rows = [chunks_of(attn_rows[half]) for half in range(2)]

    sent = [send(product(line, part, w_out), CORE) for part in attn_rows[1]]
    mixed_parts = [
        scatter(product_parts(line, [(part, w_out)], other))
        for part, other in zip(attn_rows[0], sent)
    ]
    grad_rows = arrange(line, grad_rows, facts)
    grad_act = [product(line, part, w_down, True) for part in grad_rows]
    mixed, hidden_two = [], []
    for chunk, parts in zip(CHUNKS, mixed_parts):
        mixed_rows, hidden_rows = mix(line, chunk, tokens, mlp_gain_row, parts)
        mixed.append(mixed_rows)
        hidden_two.append(collect(hidden_rows))

    count = len(CHUNKS)
    own, other, act, gate, up, back = ([None] * count for _ in range(6))

    def first_half(n):
        own[n] = join(line, hidden_two[n])
        other[n] = send(own[n], CORE)
        act[n], gate[n], up[n] = mlp(line, own[n], grad_act[n], 0, w_gate, w_up, False)

    def second_half(n):
        *terms, sum_back = mlp(line, other[n], grad_act[n], 1, w_gate, w_up, True)
        act[n], gate[n], up[n] = zip((act[n], gate[n], up[n]), terms)
        back[n] = send(sum_back, CORE)

    hidden_parts = []
    first_half(0)
    second_half(0)
    for n in range(count):
        if n + 1 < count:
            first_half(n + 1)
        terms = [(gate[n][0], w_gate), (up[n][0], w_up)]
        hidden_parts.append(scatter(product_parts(line, terms, back[n], True)))
        if n + 1 < count:
            second_half(n + 1)
    act, gate, up = [[pair[k] for pair in part for k in range(2)] for part in (act, gate, up)]
    hidden_two = [piece for pair in zip(own, other) for piece in pair]
    grad_pieces = [(part, at) for part in grad_rows for at in range(2)]

    (down_rows,) = merged_product(line, act[1::2], w_down)
    down_rows = send(down_rows, CORE)
    down_part = weight_grad(line, grad_pieces, act)
    first_part = weight_grad(line, hidden_two, gate, (down_part,))
    grad_mixed, mixed_grad, gain_parts = [], [], []
    for n, (chunk, parts) in enumerate(zip(CHUNKS, hidden_parts)):
        total, low, gain_part = mix_back(line, chunk, out_grad, mixed[n], mlp_gain_row, parts)
        grad_mixed.append(total)
        mixed_grad.append(collect(low))
        gain_parts.append(gain_part)
    first_kept = reduce_near(gated(line, (first_part,))[0])
    second_part = weight_grad(line, hidden_two, up)
    out_parts = scatter(merged_product(line, act[0::2], w_down, down_rows))

    grad_own = [join(line, parts) for parts in mixed_grad]
    grad_other = [send(part, CORE) for part in grad_own]
    grad_attn = jnp.stack([merged_back(line, part, w_out) for part in (grad_own, grad_other)])
    grad_attn = in_order(grad_attn, core, x)
    grad_attn = jnp.pad(grad_attn, ((0, padded_rows - group_rows), (0, 0)))
    long_dq, far_terms = long_backward(
        line,
        qkv,
        far_rows,
        facts,
        attn_ordered,
        grad_attn,
        long_lse,
        cos_ordered,
        sin_ordered,
    )
    ring_terms = total_of(
        (
            far_terms[0],
            send(far_terms[1], Y_LOW),
            send(far_terms[2], Y_HIGH),
            send(far_terms[3], Y_FAR),
        )
    ).astype(jnp.bfloat16)
    near = ring_terms.reshape(4, long_rows, -1)
    far_grads = total_of(
        (near[0], send(near[1], Z_UP), send(near[2], Z_FAR), send(near[3], Z_DOWN))
    )
    out_part = weight_grad(
        line,
        [piece for pair in zip(grad_own, grad_other) for piece in pair],
        [piece for pair in zip(*attn_rows) for piece in pair],
    )
    line.last += (first_kept,)
    second_sum = reduce_y(reduce_near(gated(line, (second_part,))[0]))
    line.last += out_parts[1:]
    short_low = short_backward(
        line, qkv, facts, short_attn, grad_attn, short_lse, cos_ordered, sin_ordered, pack_rows
    )
    (low_ordered,) = line(
        "turn_far",
        turn_far_kernel,
        (far_grads, cos_ordered, sin_ordered, long_dq, short_low),
        [VMEM] * 5,
        [shaped((group_rows, 384))],
        [VMEM],
    )
    low_rows = from_order(low_ordered, core, x)
    first_sum, first_received = sum_groups(first_kept, yh, core, native)
    back, gain_other = hidden_grad(line, low_rows[1], w_query, w_key_value, hidden_one[1])
    back = send(back, CORE)
    last_part = weight_grad(line, hidden_one, (low_rows[0], low_rows[1]), (out_part,))
    line.last += first_received
    *parts, gain_own = hidden_grad(line, low_rows[0], w_query, w_key_value, hidden_one[0], back)
    grad_parts = scatter(parts)
    last_kept = reduce_ring(gated(line, (last_part,))[0], z)
    output = jnp.concatenate(mixed) + total_of(out_parts)
    output = send(output.astype(jnp.bfloat16), TURN)
    line.last += (grad_parts[1],)
    (gains,) = line(
        "gains",
        gains_kernel,
        (gain_own, gain_other, attn_gain.reshape(1, d), sum(gain_parts[1:], gain_parts[0])),
        [VMEM] * 4,
        [shaped((2, d), jnp.float32)],
        [VMEM],
    )
    gains = all_sum(gains)
    last_sum, _ = sum_groups(last_kept, yh, core, native)
    grad_tokens = (
        jnp.concatenate(grad_mixed) + norm_back(total_of(grad_parts), residual, attn_gain)[0]
    )
    grad_tokens = send(grad_tokens.astype(jnp.bfloat16), TURN)
    ff = w_gate.shape[1]
    return (
        output,
        grad_tokens,
        gains[0],
        last_sum[:, :256],
        last_sum[:, 256:320],
        last_sum[:, 320:384],
        last_sum[:, 384:].T,
        gains[1],
        first_sum[:, :ff],
        second_sum,
        first_sum[:, ff:].T,
    )


def solution(mesh):
    placed = (
        P(("dp", "mp"), None),
        P("dp", None),
        P(),
        P(),
        P(None, "mp"),
        P(None, "mp"),
        P(None, "mp"),
        P("mp", None),
        P(),
        P(None, "mp"),
        P(None, "mp"),
        P("mp", None),
        P(("dp", "mp"), None),
    )
    return jax.shard_map(
        local,
        mesh=mesh,
        in_specs=placed,
        out_specs=(
            P(("dp", "mp"), None),
            P(("dp", "mp"), None),
            P(),
            P("dp", "mp"),
            P("dp", "mp"),
            P("dp", "mp"),
            P("mp", "dp"),
            P(),
            P("dp", "mp"),
            P("dp", "mp"),
            P("mp", "dp"),
        ),
        check_vma=False,
    )
```

time: 628 us -> 567 us (0.903)
  Pallas kernels: 98.5 us -> 230 us
  waiting for transfers between devices: 251 us -> 132 us
  matrix products: 28.5 us -> 0 us
  local copies, waits for them, and re-layouts: 51.3 us -> 31.5 us
  starting transfers between devices: 123 us -> 108 us
  other arithmetic: 48.9 us -> 38.6 us
    pallas_call x10 -> x36, Pallas kernels: 98.5 us -> 230 us  [the longest x35 223 us: __call__(): pl.pallas_call(ordered, out_shape=tuple(outs), in_specs=list(in_specs) +...]
    ppermute x81 -> x76, waiting for transfers between devices: 251 us -> 132 us  [send(): return lax.ppermute(values, BOTH, pairs)]
    dot_general x7 -> x0, matrix products: 28.5 us -> none  [the longest x4 16.8 us: dot(): lax.dot_general(left, right, (((left_dim,), (right_dim,)), ((), ())), pre...]
    unnamed x148 -> x61, local copies, waits for them, and re-layouts: 29.7 us -> 14.4 us
    ppermute x81 -> x76, starting transfers between devices: 123 us -> 108 us  [send(): return lax.ppermute(values, BOTH, pairs)]
    reshape x3 -> x0, local copies, waits for them, and re-layouts: 10.5 us -> none  [sum_groups(): grad.reshape(-1, width)]
  transfers between devices with their start and end apart: 85 -> 80, of which waited for: 36 -> 25; matrix products, arithmetic and copies ran while one was open for 14% -> 11% of each run, Pallas kernels for 11% -> 35%
where the time goes in v5:
time: 567 us; the launch traced here: 556 us
  Pallas kernels  230 us (41%)
  waiting for transfers between devices  132 us (23%)
  starting transfers between devices  108 us (19%)
  other arithmetic  38.6 us (7%)
  local copies, waits for them, and re-layouts  31.5 us (6%)
  between operations  16.4 us (3%)
    pallas_call x35, Pallas kernels, __call__(): pl.pallas_call(ordered, out_shape=tuple(outs), in_specs=list(in_specs) +...  223 us
    ppermute x76, waiting for transfers between devices, send(): return lax.ppermute(values, BOTH, pairs)  132 us
    ppermute x76, starting transfers between devices, send(): return lax.ppermute(values, BOTH, pairs)  108 us
    unnamed x61, local copies, waits for them, and re-layouts  14.4 us
  transfers between devices with their start and end apart: 80, of which 25 were waited for; matrix products, arithmetic and copies ran while one was open for 11% of the time, Pallas kernels for 35%

profile of v5, /device:TPU:1, one launch (start us, length us, event | category | flops | bytes accessed | tf_op | source)
XLA Modules:
  0.0 556.3 jit_solution(2019825861617364548)
XLA Ops:
  38.2 6.1 %tables.1 = (f32[1088,128]{1,0:T(8,128)}, f32[1088,128]{1,0:T(8,128)}, f32[1152,128]{1,0:T(8,128)}, f32[1152,128]{1,0:T(8,128)}) custom-call(s32[38]{0:T(128)} %concatenate.39.refs_0_.refs_1_.refs_5_.facts_ref, f32[1,128]{1,0:T(1,128)} %reshape_tile.3.refs_1_), custom_call_target="tpu_custom_call" | custom-call | flops 6899999744 | bytes 1000 | tf_op jit(solution)/shard_map/tables/pallas_call | solution.py:152
  44.3 13.7 %collective-permute-done.3.refs_3_ = bf16[136,2048]{1,0:T(8,128)(2,1)} collective-permute-done((bf16[136,2048]{1,0:T(8,128)(2,1)}, bf16[136,2048]{1,0:T(8,128)(2,1)}, u32[]{:S(2)}, u32[]{:S(2)}) %collective-permute-start.3) | collective-permute-done | bytes 557088 | tf_op jit(solution)/shard_map/ppermute | solution.py:85
  94.9 6.2 %short_forward.1 = (bf16[896,256]{1,0:T(8,128)(2,1)}, f32[7,8,512]{2,1,0:T(8,128)}) custom-call(bf16[1152,384]{1,0:T(8,128)(2,1)} %pad.8.refs_0_, s32[38]{0:T(128)} %concatenate.39.refs_0_.refs_1_.refs_5_.facts_ref, bf16[136,2048]{1,0:T(8,128)(2,1)} %copied.1.refs_2_), custom_call_target="tpu_custom_call" | custom-call | flops 6899999744 | bytes 1000 | tf_op jit(solution)/shard_map/short_forward/pallas_call | solution.py:152
  109.2 11.8 %long_forward.1 = (bf16[1088,256]{1,0:T(8,128)(2,1)}, f32[2,8,512]{2,1,0:T(8,128)}) custom-call(bf16[1152,384]{1,0:T(8,128)(2,1)} %pad.8.refs_0_, bf16[1024,128]{1,0:T(8,128)(2,1)} %pad_maximum_fusion.7.refs_2_.refs_1_, bf16[1024,128]{1,0:T(8,128)(2,1)} %collective-permute-done.12.refs_2_, bf16[1024,128]{1,0:T(8,128)(2,1)} %collective-permute-done.13.refs_3_, ...), custom_call_target="tpu_custom_call" | custom-call | flops 14949999616 | bytes 1000 | tf_op jit(solution)/shard_map/long_forward/pallas_call | solution.py:152
  141.7 7.4 %arrange.1 = bf16[8,136,2048]{2,1,0:T(8,128)(2,1)} custom-call(s32[38]{0:T(128)} %concatenate.39.refs_0_.refs_1_.refs_5_.facts_ref, bf16[8,136,2048]{2,1,0:T(8,128)(2,1)} %bitcast.79, bf16[136,2048]{1,0:T(8,128)(2,1)} %get-tuple-element.58.refs_0_.refs_2_), custom_call_target="tpu_custom_call" | custom-call | flops 5750000128 | bytes 1000 | tf_op jit(solution)/shard_map/arrange/pallas_call | solution.py:700
  149.1 8.9 %product.3.refs_6_.refs_1_ = bf16[1088,1024]{1,0:T(8,128)(2,1)} custom-call(bf16[1088,2048]{1,0:T(8,128)(2,1)} %bitcast.89, bf16[1024,2048]{1,0:T(8,128)(2,1)} %collective-permute-done.16.refs_4_.refs_1_, bf16[136,2048]{1,0:T(8,128)(2,1)} %get-tuple-element.58.refs_0_.refs_2_), custom_call_target="tpu_custom_call" | custom-call | flops 3449999872 | bytes 1000 | tf_op jit(solution)/shard_map/product/pallas_call | solution.py:152
  158.1 7.0 %collective-permute-done.19.refs_4_ = bf16[136,2048]{1,0:T(8,128)(2,1)} collective-permute-done((bf16[136,2048]{1,0:T(8,128)(2,1)}, bf16[136,2048]{1,0:T(8,128)(2,1)}, u32[]{:S(2)}, u32[]{:S(2)}) %collective-permute-start.19) | collective-permute-done | bytes 557088 | tf_op jit(solution)/shard_map/ppermute | solution.py:85
  171.8 23.0 %collective-permute-done.21.refs_1_ = bf16[136,2048]{1,0:T(8,128)(2,1)} collective-permute-done((bf16[136,2048]{1,0:T(8,128)(2,1)}, bf16[136,2048]{1,0:T(8,128)(2,1)}, u32[]{:S(2)}, u32[]{:S(2)}) %collective-permute-start.21) | collective-permute-done | bytes 557088 | tf_op jit(solution)/shard_map/ppermute | solution.py:85
  203.9 10.1 %mlp.2 = (bf16[544,1024]{1,0:T(8,128)(2,1)}, bf16[544,1024]{1,0:T(8,128)(2,1)}, bf16[544,1024]{1,0:T(8,128)(2,1)}) custom-call(bf16[544,2048]{1,0:T(8,128)(2,1)} %bitcast.62, bf16[1088,1024]{1,0:T(8,128)(2,1)} %product.3.refs_6_.refs_1_, bf16[2048,1024]{1,0:T(8,128)(2,1)} %collective-permute-done.24.refs_2_.refs_1_, ...), custom_call_target="tpu_custom_call" | custom-call | flops 11500000256 | bytes 1000 | tf_op jit(solution)/shard_map/mlp/pallas_call | solution.py:152
  214.1 16.6 %mlp.3 = (bf16[544,1024]{1,0:T(8,128)(2,1)}, bf16[544,1024]{1,0:T(8,128)(2,1)}, bf16[544,1024]{1,0:T(8,128)(2,1)}, bf16[544,2048]{1,0:T(8,128)(2,1)}) custom-call(bf16[544,2048]{1,0:T(8,128)(2,1)} %collective-permute-done.26.refs_0_.refs_1_, bf16[1088,1024]{1,0:T(8,128)(2,1)} %product.3.refs_6_.refs_1_, ...), custom_call_target="tpu_custom_call" | custom-call | flops 11500000256 | bytes 1000 | tf_op jit(solution)/shard_map/mlp/pallas_call | solution.py:152
  235.5 9.4 %product_parts.3 = (bf16[136,2048]{1,0:T(8,128)(2,1)}, bf16[136,2048]{1,0:T(8,128)(2,1)}, bf16[136,2048]{1,0:T(8,128)(2,1)}, bf16[136,2048]{1,0:T(8,128)(2,1)}) custom-call(bf16[544,1024]{1,0:T(8,128)(2,1)} %get-tuple-element.66.refs_0_.refs_2_, bf16[2048,1024]{1,0:T(8,128)(2,1)} %collective-permute-done.24.refs_2_.refs_1_, ...), custom_call_target="tpu_custom_call" | custom-call | flops 5750000128 | bytes 1000 | tf_op jit(solution)/shard_map/product_parts/pallas_call | solution.py:152
  247.5 6.2 %merged_product.2.refs_4_ = bf16[544,2048]{1,0:T(8,128)(2,1)} custom-call(bf16[544,1024]{1,0:T(8,128)(2,1)} %get-tuple-element.65.refs_5_.refs_0_.refs_3_, bf16[1024,2048]{1,0:T(8,128)(2,1)} %collective-permute-done.16.refs_4_.refs_1_, bf16[136,2048]{1,0:T(8,128)(2,1)} %get-tuple-element.69.refs_2_.refs_3_), custom_call_target="tpu_custom_call" | custom-call | flops 4600000000 | bytes 1000 | tf_op jit(solution)/shard_map/merged_product/pallas_call | solution.py:152
  253.7 11.5 %weight_grad.5.refs_4_.refs_5_ = bf16[2048,1024]{1,0:T(8,128)(2,1)} custom-call(bf16[1088,2048]{1,0:T(8,128)(2,1)} %bitcast.90, bf16[1088,2048]{1,0:T(8,128)(2,1)} %bitcast.91, bf16[544,1024]{1,0:T(8,128)(2,1)} %get-tuple-element.64.refs_4_.refs_2_.refs_0_, bf16[544,1024]{1,0:T(8,128)(2,1)} %get-tuple-element.65.refs_5_.refs_0_.refs_3_, ...), custom_call_target="tpu_custom_call" | custom-call | flops 5750000128 | bytes 1000 | tf_op jit(solution)/shard_map/weight_grad/pallas_call | solution.py:152
  265.2 13.1 %weight_grad.6.refs_7_.refs_0_ = bf16[2048,2048]{1,0:T(8,128)(2,1)} custom-call(bf16[544,2048]{1,0:T(8,128)(2,1)} %bitcast.63, bf16[544,2048]{1,0:T(8,128)(2,1)} %collective-permute-done.26.refs_0_.refs_1_, bf16[544,1024]{1,0:T(8,128)(2,1)} %get-tuple-element.66.refs_0_.refs_2_, bf16[544,1024]{1,0:T(8,128)(2,1)} %get-tuple-element.71.refs_3_, ...), custom_call_target="tpu_custom_call" | custom-call | flops 5750000128 | bytes 1000 | tf_op jit(solution)/shard_map/weight_grad/pallas_call | solution.py:152
  286.9 11.6 %weight_grad.7.refs_3_.refs_0_ = bf16[2048,1024]{1,0:T(8,128)(2,1)} custom-call(bf16[544,2048]{1,0:T(8,128)(2,1)} %bitcast.64, bf16[544,2048]{1,0:T(8,128)(2,1)} %collective-permute-done.26.refs_0_.refs_1_, bf16[544,1024]{1,0:T(8,128)(2,1)} %get-tuple-element.67.refs_2_, bf16[544,1024]{1,0:T(8,128)(2,1)} %get-tuple-element.70.refs_3_, ...), custom_call_target="tpu_custom_call" | custom-call | flops 5750000128 | bytes 1000 | tf_op jit(solution)/shard_map/weight_grad/pallas_call | solution.py:152
  298.5 6.3 %merged_product.3 = (bf16[136,2048]{1,0:T(8,128)(2,1)}, bf16[136,2048]{1,0:T(8,128)(2,1)}, bf16[136,2048]{1,0:T(8,128)(2,1)}, bf16[136,2048]{1,0:T(8,128)(2,1)}) custom-call(bf16[544,1024]{1,0:T(8,128)(2,1)} %get-tuple-element.64.refs_4_.refs_2_.refs_0_, bf16[1024,2048]{1,0:T(8,128)(2,1)} %collective-permute-done.16.refs_4_.refs_1_, ...), custom_call_target="tpu_custom_call" | custom-call | flops 4600000000 | bytes 1000 | tf_op jit(solution)/shard_map/merged_product/pallas_call | solution.py:152
  304.8 7.6 %collective-permute-done.38.refs_3_ = bf16[136,2048]{1,0:T(8,128)(2,1)} collective-permute-done((bf16[136,2048]{1,0:T(8,128)(2,1)}, bf16[136,2048]{1,0:T(8,128)(2,1)}, u32[]{:S(2)}, u32[]{:S(2)}) %collective-permute-start.38) | collective-permute-done | bytes 557088 | tf_op jit(solution)/shard_map/ppermute | solution.py:85
  329.1 16.5 %long_backward.1 = (bf16[256,256]{1,0:T(8,128)(2,1)}, bf16[4,1024,128]{2,1,0:T(8,128)(2,1)}) custom-call(bf16[1152,384]{1,0:T(8,128)(2,1)} %pad.8.refs_0_, bf16[1024,128]{1,0:T(8,128)(2,1)} %pad_maximum_fusion.7.refs_2_.refs_1_, bf16[1024,128]{1,0:T(8,128)(2,1)} %collective-permute-done.12.refs_2_, bf16[1024,128]{1,0:T(8,128)(2,1)} %collective-permute-done.13.refs_3_, ...), custom_call_target="tpu_custom_call" | custom-call | flops 18400000000 | bytes 1000 | tf_op jit(solution)/shard_map/long_backward/pallas_call | solution.py:152
  366.3 7.6 %weight_grad.8.refs_1_.refs_4_ = bf16[2048,256]{1,0:T(8,128)(2,1)} custom-call(bf16[544,2048]{1,0:T(8,128)(2,1)} %bitcast.86, bf16[544,2048]{1,0:T(8,128)(2,1)} %collective-permute-done.39.refs_0_.refs_1_, bf16[544,256]{1,0:T(8,128)(2,1)} %get-tuple-element.146.refs_0_.refs_2_, bf16[544,256]{1,0:T(8,128)(2,1)} %get-tuple-element.145.refs_0_.refs_3_, ...), custom_call_target="tpu_custom_call" | custom-call | flops 5750000128 | bytes 1000 | tf_op jit(solution)/shard_map/weight_grad/pallas_call | solution.py:152
  381.9 10.4 %short_backward.1.refs_4_.refs_5_ = bf16[896,384]{1,0:T(8,128)(2,1)} custom-call(bf16[1152,384]{1,0:T(8,128)(2,1)} %pad.8.refs_0_, s32[38]{0:T(128)} %concatenate.39.refs_0_.refs_1_.refs_5_.facts_ref, bf16[896,256]{1,0:T(8,128)(2,1)} %get-tuple-element.54.refs_6_.refs_2_, bf16[1152,256]{1,0:T(8,128)(2,1)} %pad.9.refs_7_.refs_3_, ...), custom_call_target="tpu_custom_call" | custom-call | flops 11500000256 | bytes 1000 | tf_op jit(solution)/shard_map/short_backward/pallas_call | solution.py:152
  427.6 9.0 %weight_grad.9.refs_5_.refs_0_ = bf16[2048,640]{1,0:T(8,128)(2,1)} custom-call(bf16[544,2048]{1,0:T(8,128)(2,1)} %bitcast.82, bf16[544,2048]{1,0:T(8,128)(2,1)} %collective-permute-done.8.refs_0_.refs_3_.refs_1_, bf16[544,384]{1,0:T(8,128)(2,1)} %get-tuple-element.142.refs_2_.refs_0_, bf16[544,384]{1,0:T(8,128)(2,1)} %get-tuple-element.141.refs_0_.refs_3_, ...), custom_call_target="tpu_custom_call" | custom-call | flops 5750000128 | bytes 1000 | tf_op jit(solution)/shard_map/weight_grad/pallas_call | solution.py:152
  464.4 16.3 %collective-permute-done.51.refs_5_ = bf16[136,2048]{1,0:T(8,128)(2,1)} collective-permute-done((bf16[136,2048]{1,0:T(8,128)(2,1)}, bf16[136,2048]{1,0:T(8,128)(2,1)}, u32[]{:S(2)}, u32[]{:S(2)}) %collective-permute-start.51) | collective-permute-done | bytes 557088 | tf_op jit(solution)/shard_map/ppermute | solution.py:85
  491.2 8.1 %collective-permute-start.54 = (bf16[136,2048]{1,0:T(8,128)(2,1)S(1)}, bf16[136,2048]{1,0:T(8,128)(2,1)S(1)}, u32[]{:S(2)}, u32[]{:S(2)}) collective-permute-start(bf16[136,2048]{1,0:T(8,128)(2,1)S(1)} %fusion.10), channel_id=1, source_target_pairs={{0,0},{1,1},{2,2},{3,3},{4,8},{5,9},{6,10},{7,11},{8,4},{9,5},{10,... | collective-permute-start | bytes 1671176 | tf_op jit(solution)/shard_map/ppermute | solution.py:85
  529.0 8.9 %collective-permute-done.73 = bf16[128,640]{0,1:T(8,128)(2,1)S(1)} collective-permute-done((bf16[128,640]{0,1:T(8,128)(2,1)S(1)}, bf16[128,640]{0,1:T(8,128)(2,1)S(1)}, u32[]{:S(2)}, u32[]{:S(2)}) %collective-permute-start.73) | collective-permute-done | bytes 163872 | tf_op jit(solution)/shard_map/ppermute | solution.py:85
  (308 shorter events, 286.6 us)
Async XLA Ops:
  7.2 134.6 %all-gather.3.cloned.1.call-start = ((), (), s32[]{:S(2)}) async-start(), calls=%async_computation.6 | async-start | bytes 5013504 | tf_op jit(solution)/shard_map/all_gather | solution.py:1016
  13.8 30.5 %collective-permute-start.5 = (bf16[2048,256]{1,0:T(8,128)(2,1)}, bf16[2048,256]{1,0:T(8,128)(2,1)}, u32[]{:S(2)}, u32[]{:S(2)}) collective-permute-start(bf16[2048,256]{1,0:T(8,128)(2,1)} %param.17), channel_id=1, source_target_pairs={{0,4},{1,5},{2,6},{3,7},{4,12},{5,13},{6,14},{7,15},{8,0},{9,1},{1... | collective-permute-start | bytes 3145736 | tf_op jit(solution)/shard_map/ppermute | solution.py:85
  22.0 62.9 %collective-permute-start.16 = (bf16[1024,2048]{1,0:T(8,128)(2,1)}, bf16[1024,2048]{1,0:T(8,128)(2,1)}, u32[]{:S(2)}, u32[]{:S(2)}) collective-permute-start(bf16[1024,2048]{1,0:T(8,128)(2,1)} %param.24), channel_id=1, source_target_pairs={{0,4},{1,5},{2,6},{3,7},{4,12},{5,13},{6,14},{7,15},{8,0},{9,1},{1... | collective-permute-start | bytes 12582920 | tf_op jit(solution)/shard_map/ppermute | solution.py:85
  88.1 287.4 %reduce-scatter.4.cloned.1.call-start = ((), (), s32[]{:S(2)}) async-start(), calls=%async_computation.3 | async-start | bytes 10485760 | tf_op jit(solution)/shard_map/reduce_scatter | solution.py:217
  128.1 75.9 %collective-permute-start.24 = (bf16[2048,1024]{1,0:T(8,128)(2,1)}, bf16[2048,1024]{1,0:T(8,128)(2,1)}, u32[]{:S(2)}, u32[]{:S(2)}) collective-permute-start(bf16[2048,1024]{1,0:T(8,128)(2,1)} %param.22), channel_id=1, source_target_pairs={{0,4},{1,5},{2,6},{3,7},{4,12},{5,13},{6,14},{7,15},{8,0},{9,1},{1... | collective-permute-start | bytes 12582920 | tf_op jit(solution)/shard_map/ppermute | solution.py:85
  128.1 75.9 %collective-permute-start.25 = (bf16[2048,1024]{1,0:T(8,128)(2,1)}, bf16[2048,1024]{1,0:T(8,128)(2,1)}, u32[]{:S(2)}, u32[]{:S(2)}) collective-permute-start(bf16[2048,1024]{1,0:T(8,128)(2,1)} %param.23), channel_id=1, source_target_pairs={{0,68},{1,69},{2,70},{3,71},{4,12},{5,13},{6,14},{7,15},{8,0},{9,1... | collective-permute-start | bytes 12582920 | tf_op jit(solution)/shard_map/ppermute | solution.py:85
  138.1 27.0 %collective-permute-start.19 = (bf16[136,2048]{1,0:T(8,128)(2,1)}, bf16[136,2048]{1,0:T(8,128)(2,1)}, u32[]{:S(2)}, u32[]{:S(2)}) collective-permute-start(bf16[136,2048]{1,0:T(8,128)(2,1)} %get-tuple-element.60), channel_id=1, source_target_pairs={{0,2},{1,3},{2,0},{3,1},{4,6},{5,7},{6,4},{7,5},{8,10},{9,11},{10,... | collective-permute-start | bytes 1671176 | tf_op jit(solution)/shard_map/ppermute | solution.py:85
  168.5 26.3 %collective-permute-start.21 = (bf16[136,2048]{1,0:T(8,128)(2,1)}, bf16[136,2048]{1,0:T(8,128)(2,1)}, u32[]{:S(2)}, u32[]{:S(2)}) collective-permute-start(bf16[136,2048]{1,0:T(8,128)(2,1)} %get-tuple-element.63.refs_0_), channel_id=1, source_target_pairs={{0,3},{1,0},{2,1},{3,2},{4,7},{5,4},{6,5},{7,6},{8,11},{9,8},{10,9... | collective-permute-start | bytes 1671176 | tf_op jit(solution)/shard_map/ppermute | solution.py:85
  171.3 27.8 %collective-permute-start.23 = (bf16[136,2048]{1,0:T(8,128)(2,1)}, bf16[136,2048]{1,0:T(8,128)(2,1)}, u32[]{:S(2)}, u32[]{:S(2)}) collective-permute-start(bf16[136,2048]{1,0:T(8,128)(2,1)} %get-tuple-element.63.refs_0_), channel_id=1, source_target_pairs={{0,1},{1,2},{2,3},{3,0},{4,5},{5,6},{6,7},{7,4},{8,9},{9,10},{10,1... | collective-permute-start | bytes 1671176 | tf_op jit(solution)/shard_map/ppermute | solution.py:85
  244.8 33.4 %collective-permute-start.29 = (bf16[136,2048]{1,0:T(8,128)(2,1)}, bf16[136,2048]{1,0:T(8,128)(2,1)}, u32[]{:S(2)}, u32[]{:S(2)}) collective-permute-start(bf16[136,2048]{1,0:T(8,128)(2,1)} %get-tuple-element.72), channel_id=1, source_target_pairs={{0,1},{1,2},{2,3},{3,0},{4,5},{5,6},{6,7},{7,4},{8,9},{9,10},{10,1... | collective-permute-start | bytes 1671176 | tf_op jit(solution)/shard_map/ppermute | solution.py:85
  244.9 33.4 %collective-permute-start.30 = (bf16[136,2048]{1,0:T(8,128)(2,1)}, bf16[136,2048]{1,0:T(8,128)(2,1)}, u32[]{:S(2)}, u32[]{:S(2)}) collective-permute-start(bf16[136,2048]{1,0:T(8,128)(2,1)} %get-tuple-element.73), channel_id=1, source_target_pairs={{0,2},{1,3},{2,0},{3,1},{4,6},{5,7},{6,4},{7,5},{8,10},{9,11},{10,... | collective-permute-start | bytes 1671176 | tf_op jit(solution)/shard_map/ppermute | solution.py:85
  246.6 31.7 %collective-permute-start.31 = (bf16[136,2048]{1,0:T(8,128)(2,1)}, bf16[136,2048]{1,0:T(8,128)(2,1)}, u32[]{:S(2)}, u32[]{:S(2)}) collective-permute-start(bf16[136,2048]{1,0:T(8,128)(2,1)} %get-tuple-element.74), channel_id=1, source_target_pairs={{0,3},{1,0},{2,1},{3,2},{4,7},{5,4},{6,5},{7,6},{8,11},{9,8},{10,9... | collective-permute-start | bytes 1671176 | tf_op jit(solution)/shard_map/ppermute | solution.py:85
  282.5 228.5 %reduce-scatter.6.cloned.1.call-start = ((), (), s32[]{:S(2)}) async-start(), calls=%async_computation.4 | async-start | bytes 5242880 | tf_op jit(solution)/shard_map/reduce_scatter | solution.py:217
  286.0 26.3 %collective-permute-start.38 = (bf16[136,2048]{1,0:T(8,128)(2,1)}, bf16[136,2048]{1,0:T(8,128)(2,1)}, u32[]{:S(2)}, u32[]{:S(2)}) collective-permute-start(bf16[136,2048]{1,0:T(8,128)(2,1)} %get-tuple-element.81.refs_0_), channel_id=1, source_target_pairs={{0,1},{1,2},{2,3},{3,0},{4,5},{5,6},{6,7},{7,4},{8,9},{9,10},{10,1... | collective-permute-start | bytes 1671176 | tf_op jit(solution)/shard_map/ppermute | solution.py:85
  316.8 34.0 %collective-permute-start.34 = (bf16[136,2048]{1,0:T(8,128)(2,1)}, bf16[136,2048]{1,0:T(8,128)(2,1)}, u32[]{:S(2)}, u32[]{:S(2)}) collective-permute-start(bf16[136,2048]{1,0:T(8,128)(2,1)} %get-tuple-element.79), channel_id=1, source_target_pairs={{0,3},{1,0},{2,1},{3,2},{4,7},{5,4},{6,5},{7,6},{8,11},{9,8},{10,9... | collective-permute-start | bytes 1671176 | tf_op jit(solution)/shard_map/ppermute | solution.py:85
  317.1 33.6 %collective-permute-start.33 = (bf16[136,2048]{1,0:T(8,128)(2,1)}, bf16[136,2048]{1,0:T(8,128)(2,1)}, u32[]{:S(2)}, u32[]{:S(2)}) collective-permute-start(bf16[136,2048]{1,0:T(8,128)(2,1)} %get-tuple-element.78), channel_id=1, source_target_pairs={{0,2},{1,3},{2,0},{3,1},{4,6},{5,7},{6,4},{7,5},{8,10},{9,11},{10,... | collective-permute-start | bytes 1671176 | tf_op jit(solution)/shard_map/ppermute | solution.py:85
  319.1 31.7 %collective-permute-start.32 = (bf16[136,2048]{1,0:T(8,128)(2,1)}, bf16[136,2048]{1,0:T(8,128)(2,1)}, u32[]{:S(2)}, u32[]{:S(2)}) collective-permute-start(bf16[136,2048]{1,0:T(8,128)(2,1)} %get-tuple-element.77), channel_id=1, source_target_pairs={{0,1},{1,2},{2,3},{3,0},{4,5},{5,6},{6,7},{7,4},{8,9},{9,10},{10,1... | collective-permute-start | bytes 1671176 | tf_op jit(solution)/shard_map/ppermute | solution.py:85
  353.6 64.2 %collective-permute-start.35 = (bf16[136,2048]{1,0:T(8,128)(2,1)}, bf16[136,2048]{1,0:T(8,128)(2,1)}, u32[]{:S(2)}, u32[]{:S(2)}) collective-permute-start(bf16[136,2048]{1,0:T(8,128)(2,1)} %add_convert_fusion), channel_id=1, source_target_pairs={{0,0},{1,1},{2,2},{3,3},{4,8},{5,9},{6,10},{7,11},{8,4},{9,5},{10,... | collective-permute-start | bytes 1671176 | tf_op jit(solution)/shard_map/ppermute | solution.py:85
  381.8 156.1 %reduce-scatter.8.cloned.1.call-start = ((), (), s32[]{:S(2)}) async-start(), calls=%async_computation.5 | async-start | bytes 1310720 | tf_op jit(solution)/shard_map/reduce_scatter | solution.py:223
  452.0 32.5 %collective-permute-start.53 = (bf16[136,2048]{1,0:T(8,128)(2,1)}, bf16[136,2048]{1,0:T(8,128)(2,1)}, u32[]{:S(2)}, u32[]{:S(2)}) collective-permute-start(bf16[136,2048]{1,0:T(8,128)(2,1)} %get-tuple-element.91), channel_id=1, source_target_pairs={{0,3},{1,0},{2,1},{3,2},{4,7},{5,4},{6,5},{7,6},{8,11},{9,8},{10,9... | collective-permute-start | bytes 1671176 | tf_op jit(solution)/shard_map/ppermute | solution.py:85
  454.5 30.0 %collective-permute-start.52 = (bf16[136,2048]{1,0:T(8,128)(2,1)}, bf16[136,2048]{1,0:T(8,128)(2,1)}, u32[]{:S(2)}, u32[]{:S(2)}) collective-permute-start(bf16[136,2048]{1,0:T(8,128)(2,1)} %get-tuple-element.90), channel_id=1, source_target_pairs={{0,2},{1,3},{2,0},{3,1},{4,6},{5,7},{6,4},{7,5},{8,10},{9,11},{10,... | collective-permute-start | bytes 1671176 | tf_op jit(solution)/shard_map/ppermute | solution.py:85
  460.7 40.3 %collective-permute-start.68 = (bf16[512,640]{0,1:T(8,128)(2,1)}, bf16[512,640]{0,1:T(8,128)(2,1)}, u32[]{:S(2)}, u32[]{:S(2)}) collective-permute-start(bf16[512,640]{0,1:T(8,128)(2,1)} %pad_maximum_fusion.3), channel_id=1, source_target_pairs={{0,48},{1,49},{2,50},{3,51},{4,52},{5,53},{6,54},{7,55},{8,56},{9,... | collective-permute-start | bytes 1966088 | tf_op jit(solution)/shard_map/ppermute | solution.py:85
  464.4 37.6 %collective-permute-start.66 = (bf16[512,640]{0,1:T(8,128)(2,1)}, bf16[512,640]{0,1:T(8,128)(2,1)}, u32[]{:S(2)}, u32[]{:S(2)}) collective-permute-start(bf16[512,640]{0,1:T(8,128)(2,1)} %pad_maximum_fusion.2), channel_id=1, source_target_pairs={{0,16},{1,17},{2,18},{3,19},{4,20},{5,21},{6,22},{7,23},{8,24},{9,... | collective-permute-start | bytes 1966088 | tf_op jit(solution)/shard_map/ppermute | solution.py:85
  491.2 37.8 %collective-permute-start.54 = (bf16[136,2048]{1,0:T(8,128)(2,1)S(1)}, bf16[136,2048]{1,0:T(8,128)(2,1)S(1)}, u32[]{:S(2)}, u32[]{:S(2)}) collective-permute-start(bf16[136,2048]{1,0:T(8,128)(2,1)S(1)} %fusion.10), channel_id=1, source_target_pairs={{0,0},{1,1},{2,2},{3,3},{4,8},{5,9},{6,10},{7,11},{8,4},{9,5},{10,... | collective-permute-start | bytes 1671176 | tf_op jit(solution)/shard_map/ppermute | solution.py:85
  (80 other events, 794.0 us)
Sparse Core Ops, SparseCore 0:
  88.3 35.6 all-gather.2
  282.7 80.0 reduce-scatter.3
  381.9 53.7 reduce-scatter.5
  511.2 25.8 reduce-scatter.7
